TPU v7x, 128 devices: a whole 4x4x4 slice. The times are simulated.
128 devices in a mesh: replica: 16 (over z_lo, x, core), fsdp: 8 (over y, z_hi).
Axes of the slice: x: 4, y: 4, z: 4 (z_hi: 2, z_lo: 2; z = z_hi * 2 + z_lo), core: 2. Of those that a mesh axis runs over, the one named last changes fastest.
Arguments:
- context: bfloat16 [65536, 2048], P(('replica', 'fsdp')), may hold values from -6 to 6
- cotangent: bfloat16 [65536, 3584], P(('replica', 'fsdp')), may hold values from -60 to 60
- weight: bfloat16 [16, 2048, 3584], P('replica', 'fsdp'), may hold values from -0.125 to 0.125
- gain: float32 [16, 3584], P('replica'), may hold values from 0.1 to 1.9
- delta: float32 [16, 2048, 3584], P('replica', 'fsdp'), may hold values from -6 to 6
- anchor: float32 [2048, 3584], P('fsdp', 'replica'), may hold values from -6 to 6
- momentum: float32 [2048, 3584], P('fsdp', 'replica'), may hold values from -6 to 6
Outputs:
- grad_context: bfloat16 [65536, 2048], P(('replica', 'fsdp'))
- grad_weight: float32 [16, 2048, 3584], P('replica', 'fsdp')
- grad_gain: float32 [16, 3584], P('replica')
- new_anchor: float32 [2048, 3584], P('fsdp', 'replica')
- new_momentum: float32 [2048, 3584], P('fsdp', 'replica')
All inputs are finite; a program needn't handle non-finite values.
Results may differ from a plain program's by a relative error of at most 0.014.
Values may be sent and summed in bfloat16 or wider, within the bound.
No kernel may reach another device: no remote copies, remote signals or barrier semaphores. Data moves between devices by JAX's collectives and lax.ppermute only.
A program may use at most 128 MiB of HBM per device.

v0:
```python
import jax
import jax.numpy as jnp
from jax import lax
from jax.sharding import PartitionSpec as P


def outer_update(delta, anchor, momentum):
    replicas = lax.axis_size("replica")
    summed = lax.psum(delta[0].astype(jnp.bfloat16), "replica").astype(jnp.float32)
    columns = anchor.shape[1]
    own_part = lax.dynamic_slice_in_dim(summed, lax.axis_index("replica") * columns, columns, 1)
    outer_grad = own_part / replicas
    new_momentum = 0.9 * momentum + outer_grad
    new_anchor = anchor - 0.7 * (outer_grad + 0.9 * new_momentum)
    return (new_anchor, new_momentum)


def inner_step(context, cotangent, weight, gain):
    whole_weight = lax.all_gather(weight[0], "fsdp", axis=0, tiled=True)
    projected = jnp.dot(context, whole_weight, preferred_element_type=jnp.float32)
    inverse = lax.rsqrt(jnp.mean(projected * projected, axis=-1, keepdims=True) + 1e-06)
    normed = projected * inverse
    cot_float = cotangent.astype(jnp.float32)
    scaled = cot_float * gain[0]
    grad_out = (
        (scaled - normed * jnp.mean(scaled * normed, axis=-1, keepdims=True)) * inverse
    ).astype(jnp.bfloat16)
    grad_context = lax.dot_general(
        grad_out, whole_weight, (((1,), (1,)), ((), ())), preferred_element_type=jnp.float32
    ).astype(jnp.bfloat16)
    grad_weight = lax.psum_scatter(
        lax.dot_general(
            context, grad_out, (((0,), (0,)), ((), ())), preferred_element_type=jnp.float32
        ).astype(jnp.bfloat16),
        "fsdp",
        scatter_dimension=0,
        tiled=True,
    ).astype(jnp.float32)
    grad_gain = lax.psum(jnp.sum(cot_float * normed, axis=0), "fsdp")
    return (grad_context, grad_weight[None], grad_gain[None])


def per_device(context, cotangent, weight, gain, delta, anchor, momentum):
    grad_context, grad_weight, grad_gain = inner_step(context, cotangent, weight, gain)
    new_anchor, new_momentum = outer_update(delta, anchor, momentum)
    return (grad_context, grad_weight, grad_gain, new_anchor, new_momentum)


def solution(mesh):
    placed = (
        P(("replica", "fsdp"), None),
        P(("replica", "fsdp"), None),
        P("replica", "fsdp", None),
        P("replica", None),
        P("replica", "fsdp", None),
        P("fsdp", "replica"),
        P("fsdp", "replica"),
    )
    return jax.shard_map(
        per_device,
        mesh=mesh,
        in_specs=placed,
        out_specs=(
            P(("replica", "fsdp"), None),
            P("replica", "fsdp", None),
            P("replica", None),
            P("fsdp", "replica"),
            P("fsdp", "replica"),
        ),
        check_vma=False,
    )
```

profile of v0, /device:TPU:1, one launch (start us, length us, event | category | flops | bytes accessed | tf_op | source)
XLA Modules:
  0.0 408.7 jit_solution(8683289248157210364)
XLA Ops:
  8.0 0.0 copy-start
  8.0 0.0 copy-start.6
  8.0 0.0 all-gather.3.cloned.1.call-start
  8.1 0.7 all-gather.3.cloned.1.call-update
  8.8 0.0 all-reduce.2.cloned.1.call-start
  8.8 4.3 %copy.12 = bf16[1,256,3584]{1,2,0:T(8,128)(2,1)} copy(f32[1,256,3584]{2,1,0:T(8,128)} %param.11) | data formatting | bytes 5505024 | tf_op args[4]
  13.2 0.0 all-reduce.2.cloned.1.call-update
  13.2 0.0 reduce-scatter.2.cloned.1.call-start
  13.2 0.0 copy-done.6
  13.3 180.7 %all-gather.3.cloned.1.call-done = bf16[1,2048,3584]{2,1,0:T(8,128)(2,1)} async-done(((bf16[1,256,3584]{2,1,0:T(8,128)(2,1)}), bf16[1,2048,3584]{2,1,0:T(8,128)(2,1)}) %all-gather.3.cloned.1.call-update) | async-done | bytes 14680080 | tf_op jit(solution)/shard_map/all_gather | solution.py:19
  194.0 0.0 copy-done
  194.0 0.0 copy-start.2
  194.0 11.4 %multiply_reduce_fusion = (f32[512]{0:T(512)S(1)}, f32[512,3584]{1,0:T(8,128)S(1)}) fusion(bf16[512,2048]{1,0:T(8,128)(2,1)S(1)} %copy-done, bf16[1,2048,3584]{2,1,0:T(8,128)(2,1)} %all-gather.3.cloned.1.call-done), kind=kOutput, calls=%fused_computation.14 | convolution fusion | flops 7519862272 | bytes 24119296 | tf_op jit(solution)/shard_map/dot_general | solution.py:20
  205.5 0.0 copy-done.2
  205.5 3.1 fusion.10
  208.6 2.4 fusion.9
  211.1 0.0 copy-start.3
  211.1 1.8 copy-done.3
  212.9 11.0 %fusion.4 = bf16[2048,3584]{0,1:T(8,128)(2,1)} fusion(bf16[512,3584]{1,0:T(8,128)(2,1)S(1)} %fusion.9, bf16[512,2048]{1,0:T(8,128)(2,1)S(1)} %copy-done), kind=kOutput, calls=%fused_computation.5 | convolution fusion | flops 7523532800 | bytes 20447232 | tf_op jit(solution)/shard_map/dot_general | solution.py:32
  223.9 0.0 copy-start.4
  223.9 0.0 copy-start.5
  223.9 0.0 reduce-scatter.2.cloned.1.call-update
  224.0 0.0 all-reduce.2.cloned.1.call-done
  224.0 0.9 copy-done.4
  224.9 0.1 copy-done.5
  225.0 1.7 multiply_subtract_fusion
  226.7 31.5 %psum.14 = f32[1,3584]{1,0:T(1,128)} all-reduce(f32[1,3584]{1,0:T(1,128)S(1)} %broadcast_in_dim.13), channel_id=1, replica_groups=mesh['replica'=16,'fsdp'=8] {'fsdp'}, use_global_device_ids=true, to_apply=%region_4.0 | all-reduce | flops 3584 | bytes 28672 | tf_op jit(solution)/shard_map/psum | solution.py:39
  258.2 13.4 %fusion.11 = bf16[512,2048]{1,0:T(8,128)(2,1)} fusion(bf16[512,3584]{1,0:T(8,128)(2,1)} %copy-done.3, bf16[1,2048,3584]{2,1,0:T(8,128)(2,1)} %all-gather.3.cloned.1.call-done), kind=kOutput, calls=%fused_computation.15 | convolution fusion | flops 7517241344 | bytes 20447232 | tf_op jit(solution)/shard_map/dot_general | solution.py:28
  271.6 121.0 %reduce-scatter.2.cloned.1.call-done = bf16[256,3584]{0,1:T(8,128)(2,1)} async-done(((bf16[2048,3584]{0,1:T(8,128)(2,1)}), bf16[256,3584]{0,1:T(8,128)(2,1)}) %reduce-scatter.2.cloned.1.call-update) | async-done | bytes 1835024 | tf_op jit(solution)/shard_map/reduce_scatter | solution.py:31
  392.6 3.6 bitcast_convert_fusion
  396.2 5.1 %copy.13 = f32[1,256,3584]{2,1,0:T(8,128)} copy(f32[1,256,3584]{1,2,0:T(8,128)} %bitcast_convert_fusion) | data formatting | bytes 7340032
  401.3 0.0 copy-done.1
  (5 shorter events, 0.1 us)
Async XLA Ops:
  8.0 186.0 %copy-start = (bf16[512,2048]{1,0:T(8,128)(2,1)S(1)}, bf16[512,2048]{1,0:T(8,128)(2,1)}, u32[]{:S(2)}) copy-start(bf16[512,2048]{1,0:T(8,128)(2,1)} %param.7) | copy-start | bytes 6291460
  8.0 5.2 %copy-start.6 = (f32[1,3584]{1,0:T(1,128)S(1)}, f32[1,3584]{1,0:T(1,128)}, u32[]{:S(2)}) copy-start(f32[1,3584]{1,0:T(1,128)} %param.10) | copy-start | bytes 43012
  8.0 186.0 %all-gather.3.cloned.1.call-start = ((), (), s32[]{:S(2)}) async-start(), calls=%async_computation.3 | async-start | bytes 16515072 | tf_op jit(solution)/shard_map/all_gather | solution.py:19
  8.8 215.2 %all-reduce.2.cloned.1.call-start = ((), (), s32[]{:S(2)}) async-start(), calls=%async_computation.2 | async-start | bytes 3670016 | tf_op jit(solution)/shard_map/psum | solution.py:9
  13.2 379.4 %reduce-scatter.2.cloned.1.call-start = ((), (), s32[]{:S(2)}) async-start(), calls=%async_computation.1 | async-start | bytes 16515072 | tf_op jit(solution)/shard_map/reduce_scatter | solution.py:31
  194.0 11.5 %copy-start.2 = (bf16[512,3584]{1,0:T(8,128)(2,1)S(1)}, bf16[512,3584]{1,0:T(8,128)(2,1)}, u32[]{:S(2)}) copy-start(bf16[512,3584]{1,0:T(8,128)(2,1)} %param.8) | copy-start | bytes 11010052
  211.1 1.8 copy-start.3
  223.9 0.9 copy-start.4
  223.9 1.0 copy-start.5
  258.2 143.1 %copy-start.1 = (bf16[512,2048]{1,0:T(8,128)(2,1)S(1)}, bf16[512,2048]{1,0:T(8,128)(2,1)}, u32[]{:S(2)}) copy-start(bf16[512,2048]{1,0:T(8,128)(2,1)} %param.7) | copy-start | bytes 6291460
Sparse Core Ops, SparseCore 0:
  11.2 182.8 all-gather.2
  224.1 168.4 reduce-scatter.1
Sparse Core Ops, SparseCore 1:
  13.3 127.2 all-reduce.1
where the time goes:
time: 409 us
  waiting for transfers between devices  302 us (74%)
  matrix products  35.9 us (9%)
  blocking collectives  31.5 us (8%)
  between operations  15.6 us (4%)
  local copies, waits for them, and re-layouts  12.3 us (3%)
  other arithmetic  10.9 us (3%)
    all_gather x1, waiting for transfers between devices, inner_step(): whole_weight = lax.all_gather(weight[0], 'fsdp', axis=0, tiled=True)  181 us
    reduce_scatter x1, waiting for transfers between devices, inner_step(): lax.psum_scatter(lax.dot_general(context, grad_out, (((0,), (0,)), ((), (...  121 us
    psum x1, blocking collectives, inner_step(): grad_gain = lax.psum(jnp.sum(cot_float * normed, axis=0), 'fsdp')  31.5 us
    dot_general x1, matrix products, inner_step(): lax.dot_general(grad_out, whole_weight, (((1,), (1,)), ((), ())), preferr...  13.4 us
    unnamed x16, local copies, waits for them, and re-layouts  12.3 us
    dot_general x1, matrix products, inner_step(): jnp.dot(context, whole_weight, preferred_element_type=jnp.float32)  11.4 us
    dot_general x1, matrix products, inner_step(): lax.dot_general(context, grad_out, (((0,), (0,)), ((), ())), preferred_el...  11 us
  transfers between devices with their start and end apart: 3, of which 2 were waited for; matrix products, arithmetic and copies ran while one was open for 12% of the time, Pallas kernels for 0%

commit v1 on v0

v1 whole, which is shorter than its diff:
```python
import jax
import jax.numpy as jnp
from jax import lax
from jax.sharding import PartitionSpec as P

BF16 = jnp.bfloat16
F32 = jnp.float32
BOTH = ("replica", "fsdp")


def partner_y(y, core):
    if core == 0:
        return y ^ 1
    return (y - 1) % 4 if y % 2 == 0 else (y + 1) % 4


def table(move):
    pairs = []
    for r in range(16):
        for f in range(8):
            z_lo, x, core, y, z_hi = r // 8, (r // 2) % 4, r % 2, f // 2, f % 2
            z_lo, x, core, y, z_hi = move(z_lo, x, core, y, z_hi)
            pairs.append((r * 8 + f, ((z_lo * 4 + x) * 2 + core) * 8 + y * 2 + z_hi))
    return pairs


TO_PARTNER = table(lambda a, x, c, y, z: (a, x, c, partner_y(y, c), z))
TO_MATE = table(lambda a, x, c, y, z: (a, x, c, partner_y(y, 1 - c), z))
TO_Z = table(lambda a, x, c, y, z: (a, x, c, y, 1 - z))
TO_CORE = table(lambda a, x, c, y, z: (a, x, 1 - c, y, z))
TO_X1 = table(lambda a, x, c, y, z: (a, x ^ 1, c, y, z))
TO_X3 = table(lambda a, x, c, y, z: (a, 3 - x, c, y, z))
TO_ZLO = table(lambda a, x, c, y, z: (1 - a, x, c, y, z))


def send(value, pairs):
    return lax.ppermute(value, BOTH, pairs)


def pick(stack, index):
    return lax.dynamic_index_in_dim(stack, index, 0, keepdims=False)


def outer_update(delta, anchor, momentum):
    r = lax.axis_index("replica")
    z_lo, x, core = r // 8, (r // 2) % 4, r % 2
    parts = jnp.transpose(delta[0].reshape(256, 8, 2, 224), (2, 1, 0, 3))
    got = send(pick(parts, 1 - core).astype(BF16), TO_CORE)
    sums = (pick(parts, core) + got.astype(F32)).reshape(2, 4, 256, 224)
    by_x = jnp.transpose(sums, (1, 0, 2, 3))
    away = jnp.stack([pick(by_x, x ^ 1), pick(by_x, 3 - (x ^ 1))])
    got = send(away.astype(BF16), TO_X1)
    kept = jnp.stack([pick(by_x, x), pick(by_x, 3 - x)]) + got.astype(F32)
    got = send(kept[1].astype(BF16), TO_X3)
    kept = kept[0] + got.astype(F32)
    got = send(pick(kept, 1 - z_lo).astype(BF16), TO_ZLO)
    total = pick(kept, z_lo) + got.astype(F32)
    outer_grad = total / 16
    new_momentum = 0.9 * momentum + outer_grad
    new_anchor = anchor - 0.7 * (outer_grad + 0.9 * new_momentum)
    return (new_anchor, new_momentum)


def inner_step(context, cotangent, weight, gain):
    core = lax.axis_index("replica") % 2
    f = lax.axis_index("fsdp")
    y, z = f // 2, f % 2
    even = y % 2 == 0
    low, high = y ^ 1, jnp.where(even, (y + 3) % 4, (y + 1) % 4)
    partner = jnp.where(core == 0, low, high)
    mate = jnp.where(core == 0, high, low)
    opposite = (y + 2) % 4
    half = jnp.where(core == 0, ((y + 1) // 2) % 2, y // 2)

    def columns(array, which):
        return lax.dynamic_slice_in_dim(array, which * 1792, 1792, array.ndim - 1)

    own = columns(weight[0], half)
    other = columns(weight[0], 1 - half)

    from_partner = send(other, TO_PARTNER)
    from_mate = send(own, TO_MATE)
    own_z = send(own, TO_Z)
    context_p = send(context, TO_PARTNER)
    from_opposite = send(from_partner, TO_MATE)
    mate_z = send(from_mate, TO_Z)
    partner_z = send(from_partner, TO_Z)
    opposite_z = send(from_opposite, TO_Z)
    cot_p = send(columns(cotangent, 1 - half), TO_PARTNER)

    tokens = jnp.concatenate([context, context_p], axis=0)
    cot = jnp.concatenate([columns(cotangent, half), cot_p], axis=0).astype(F32)

    def slab(owner, zz):
        return lax.dynamic_slice_in_dim(tokens, (owner * 2 + zz) * 256, 256, 1)

    blocks = [
        (own, y, z),
        (from_mate, mate, z),
        (from_partner, partner, z),
        (from_opposite, opposite, z),
        (own_z, y, 1 - z),
        (mate_z, mate, 1 - z),
        (partner_z, partner, 1 - z),
        (opposite_z, opposite, 1 - z),
    ]
    projected = None
    for block, owner, zz in blocks:
        term = jnp.dot(slab(owner, zz), block, preferred_element_type=F32)
        projected = term if projected is None else projected + term

    scaled = cot * columns(gain[0], half)
    stats = jnp.stack(
        [jnp.sum(projected * projected, axis=-1), jnp.sum(scaled * projected, axis=-1)]
    )
    stats_p = send(stats, TO_PARTNER)
    stats = stats + jnp.concatenate([stats_p[:, 512:], stats_p[:, :512]], axis=1)
    inverse = lax.rsqrt(stats[0] / 3584 + 1e-06)
    coupling = stats[1] / 3584 * inverse
    normed = projected * inverse[:, None]
    grad_out = ((scaled - normed * coupling[:, None]) * inverse[:, None]).astype(BF16)

    def weight_term(owner, zz):
        return lax.dot_general(
            slab(owner, zz), grad_out, (((0,), (0,)), ((), ())), preferred_element_type=F32
        )

    o_mate = send(weight_term(mate, z).astype(BF16), TO_MATE)
    x_mate_z = send(weight_term(opposite, 1 - z).astype(BF16), TO_Z)
    o_mate_z = send(weight_term(mate, 1 - z).astype(BF16), TO_MATE)
    x_self_z = send(weight_term(partner, 1 - z).astype(BF16), TO_Z)

    def context_term(rows):
        parts = []
        for block, owner, zz in blocks:
            parts.append(
                lax.dot_general(
                    rows, block, (((1,), (1,)), ((), ())), preferred_element_type=F32
                )
            )
        return parts

    part_p = context_term(grad_out[512:])
    place = [owner * 2 + zz for _, owner, zz in blocks]

    def arrange(parts, dtype):
        whole = jnp.zeros((512, 2048), dtype)
        for part, at in zip(parts, place):
            whole = lax.dynamic_update_slice_in_dim(whole, part.astype(dtype), at * 256, 1)
        return whole

    got_context = send(arrange(part_p, BF16), TO_PARTNER)

    x_mate = (weight_term(opposite, z) + x_mate_z.astype(F32)).astype(BF16)
    x_from_mate = send(x_mate, TO_MATE)
    o_self_z = (weight_term(y, 1 - z) + o_mate_z.astype(F32)).astype(BF16)
    o_from_z = send(o_self_z, TO_Z)
    x_self = weight_term(partner, z) + x_self_z.astype(F32) + x_from_mate.astype(F32)
    x_got = send(x_self.astype(BF16), TO_PARTNER)
    o_self = weight_term(y, z) + o_mate.astype(F32) + o_from_z.astype(F32)
    x_got = x_got.astype(F32)

    grad_weight = jnp.concatenate(
        [jnp.where(half == 0, o_self, x_got), jnp.where(half == 0, x_got, o_self)], axis=1
    )

    grad_context = (
        arrange(context_term(grad_out[:512]), F32) + got_context.astype(F32)
    ).astype(BF16)

    gain_part = jnp.sum(cot * normed, axis=0)
    gain_part = gain_part + send(gain_part, TO_Z)
    gain_part = gain_part + send(gain_part, TO_MATE)
    gain_other = send(gain_part, TO_PARTNER)
    grad_gain = jnp.concatenate(
        [jnp.where(half == 0, gain_part, gain_other), jnp.where(half == 0, gain_other, gain_part)]
    )
    return (grad_context, grad_weight[None], grad_gain[None])


def per_device(context, cotangent, weight, gain, delta, anchor, momentum):
    new_anchor, new_momentum = outer_update(delta, anchor, momentum)
    grad_context, grad_weight, grad_gain = inner_step(context, cotangent, weight, gain)
    return (grad_context, grad_weight, grad_gain, new_anchor, new_momentum)


def solution(mesh):
    placed = (
        P(("replica", "fsdp"), None),
        P(("replica", "fsdp"), None),
        P("replica", "fsdp", None),
        P("replica", None),
        P("replica", "fsdp", None),
        P("fsdp", "replica"),
        P("fsdp", "replica"),
    )
    return jax.shard_map(
        per_device,
        mesh=mesh,
        in_specs=placed,
        out_specs=(
            P(("replica", "fsdp"), None),
            P("replica", "fsdp", None),
            P("replica", None),
            P("fsdp", "replica"),
            P("fsdp", "replica"),
        ),
        check_vma=False,
    )
```

time: 409 us -> 241 us (0.59)
  waiting for transfers between devices: 302 us -> 87.3 us
  matrix products: 35.9 us -> 79.9 us
  starting transfers between devices: 0.12 us -> 39 us
  blocking collectives: 31.5 us -> 0 us
  between operations: 15.6 us -> 1.11 us
  other arithmetic: 10.9 us -> 16.1 us
  local copies, waits for them, and re-layouts: 12.3 us -> 16.7 us
    all_gather x1 -> x0, waiting for transfers between devices: 181 us -> none  [inner_step(): whole_weight = lax.all_gather(weight[0], 'fsdp', axis=0, tiled=True)]
    reduce_scatter x1 -> x0, waiting for transfers between devices: 121 us -> none  [inner_step(): lax.psum_scatter(lax.dot_general(context, grad_out, (((0,), (0,)), ((), (...]
    ppermute x0 -> x25, waiting for transfers between devices: none -> 87.3 us  [send(): return lax.ppermute(value, BOTH, pairs)]
    dot_general x3 -> x32, matrix products: 35.9 us -> 79.9 us  [the longest x8 49.8 us: inner_step(): term = jnp.dot(slab(owner, zz), block, preferred_element_type=F32)]
    ppermute x0 -> x25, starting transfers between devices: none -> 39 us  [send(): return lax.ppermute(value, BOTH, pairs)]
    psum x1 -> x0, blocking collectives: 31.5 us -> none  [inner_step(): grad_gain = lax.psum(jnp.sum(cot_float * normed, axis=0), 'fsdp')]
    unnamed x16 -> x30, local copies, waits for them, and re-layouts: 12.3 us -> 7.1 us
  transfers between devices with their start and end apart: 3 -> 25, of which waited for: 2 -> 9; matrix products, arithmetic and copies ran while one was open for 12% -> 38% of each run, Pallas kernels for 0% -> 0%
where the time goes in v1:
time: 241 us; the launch traced here: 240 us
  waiting for transfers between devices  87.3 us (36%)
  matrix products  79.9 us (33%)
  starting transfers between devices  39 us (16%)
  local copies, waits for them, and re-layouts  16.7 us (7%)
  other arithmetic  16.1 us (7%)
    ppermute x25, waiting for transfers between devices, send(): return lax.ppermute(value, BOTH, pairs)  87.3 us
    dot_general x8, matrix products, inner_step(): term = jnp.dot(slab(owner, zz), block, preferred_element_type=F32)  49.8 us
    ppermute x25, starting transfers between devices, send(): return lax.ppermute(value, BOTH, pairs)  39 us
    dot_general x16, matrix products, context_term(): lax.dot_general(rows, block, (((1,), (1,)), ((), ())), preferred_element_...  20.4 us
    dot_general x8, matrix products, weight_term(): lax.dot_general(slab(owner, zz), grad_out, (((0,), (0,)), ((), ())), pref...  9.72 us
    unnamed x30, local copies, waits for them, and re-layouts  7.1 us
    reduce_sum x1, other arithmetic, inner_step(): gain_part = jnp.sum(cot * normed, axis=0)  5.46 us
  transfers between devices with their start and end apart: 25, of which 9 were waited for; matrix products, arithmetic and copies ran while one was open for 38% of the time, Pallas kernels for 0%

profile of v1, /device:TPU:1, one launch (start us, length us, event | category | flops | bytes accessed | tf_op | source)
XLA Modules:
  0.0 240.2 jit_solution(4038396732059043344)
XLA Ops:
  0.7 5.3 %copy.13 = f32[1,256,3584]{1,2,0:T(8,128)} copy(f32[1,256,3584]{2,1,0:T(8,128)} %param.11) | data formatting | bytes 7340032 | tf_op args[4]
  5.9 2.5 %fusion.19 = bf16[8,256,224]{1,2,0:T(8,128)(2,1)} fusion(f32[256,8,2,224]{0,3,2,1:T(8,128)} %bitcast.81, s32[]{:T(128)S(6)} %select_n.204), kind=kLoop, calls=%fused_computation.54 | loop fusion | bytes 1835012 | tf_op jit(solution)/shard_map/convert_element_type | solution.py:48
  12.3 3.6 %collective-permute-start.5 = (bf16[256,1792]{1,0:T(8,128)(2,1)S(1)}, bf16[256,1792]{1,0:T(8,128)(2,1)}, u32[]{:S(2)}, u32[]{:S(2)}) collective-permute-start(bf16[256,1792]{1,0:T(8,128)(2,1)S(1)} %get-tuple-element.20), channel_id=1, source_target_pairs={{0,1},{1,0},{2,3},{3,2},{4,5},{5,4},{6,7},{7,6},{8,9},{9,8},{10,11... | collective-permute-start | bytes 2752520 | tf_op jit(solution)/shard_map/ppermute | solution.py:37
  18.6 2.1 bitcast_add_fusion
  22.8 2.1 constant_dynamic-slice_fusion.2
  25.0 7.6 %collective-permute-done.22 = bf16[2,2,256,224]{2,3,1,0:T(8,128)(2,1)} collective-permute-done((bf16[2,2,256,224]{2,3,1,0:T(8,128)(2,1)}, bf16[2,2,256,224]{2,3,1,0:T(8,128)(2,1)}, u32[]{:S(2)}, u32[]{:S(2)}) %collective-permute-start.22) | collective-permute-done | bytes 458784 | tf_op jit(solution)/shard_map/ppermute | solution.py:37
  33.7 2.6 %collective-permute-start.23 = (bf16[2,256,224]{1,2,0:T(8,128)(2,1)S(1)}, bf16[2,256,224]{1,2,0:T(8,128)(2,1)S(1)}, u32[]{:S(2)}, u32[]{:S(2)}) collective-permute-start(bf16[2,256,224]{1,2,0:T(8,128)(2,1)S(1)} %fusion.62), channel_id=1, source_target_pairs={{0,48},{1,49},{2,50},{3,51},{4,52},{5,53},{6,54},{7,55},{8,56},{9,... | collective-permute-start | bytes 688136 | tf_op jit(solution)/shard_map/ppermute | solution.py:37
  38.0 19.2 %collective-permute-done.3 = bf16[256,1792]{1,0:T(8,128)(2,1)} collective-permute-done((bf16[256,1792]{1,0:T(8,128)(2,1)}, bf16[256,1792]{1,0:T(8,128)(2,1)}, u32[]{:S(2)}, u32[]{:S(2)}) %collective-permute-start.3) | collective-permute-done | bytes 917536 | tf_op jit(solution)/shard_map/ppermute | solution.py:37
  57.3 2.8 %collective-permute-start = (bf16[512,1792]{1,0:T(8,128)(2,1)S(1)}, bf16[512,1792]{1,0:T(8,128)(2,1)}, u32[]{:S(2)}, u32[]{:S(2)}) collective-permute-start(bf16[512,1792]{1,0:T(8,128)(2,1)S(1)} %copy-done.6), channel_id=1, source_target_pairs={{0,2},{1,3},{2,0},{3,1},{4,6},{5,7},{6,4},{7,5},{8,14},{9,15},{10,... | collective-permute-start | bytes 5505032 | tf_op jit(solution)/shard_map/ppermute | solution.py:37
  60.1 3.6 %collective-permute-start.7 = (bf16[256,1792]{1,0:T(8,128)(2,1)}, bf16[256,1792]{1,0:T(8,128)(2,1)S(1)}, u32[]{:S(2)}, u32[]{:S(2)}) collective-permute-start(bf16[256,1792]{1,0:T(8,128)(2,1)} %collective-permute-done.3), channel_id=1, source_target_pairs={{0,1},{1,0},{2,3},{3,2},{4,5},{5,4},{6,7},{7,6},{8,9},{9,8},{10,11... | collective-permute-start | bytes 2752520 | tf_op jit(solution)/shard_map/ppermute | solution.py:37
  67.4 5.5 %fusion.35 = f32[1024,1792]{1,0:T(8,128)} fusion(bf16[256,1792]{1,0:T(8,128)(2,1)} %collective-permute-done.3, bf16[1024,2048]{1,0:T(8,128)(2,1)S(1)} %constant_dynamic-update-slice_fusion, s32[]{:T(128)S(6)} %select_n.190), kind=kOutput, calls=%fused_computation.73 | convolution fusion | flops 939524096 | bytes 8781828 | tf_op jit(solution)/shard_map/dot_general | solution.py:109
  72.9 5.3 %fusion.38 = f32[1024,1792]{1,0:T(8,128)} fusion(bf16[256,1792]{1,0:T(8,128)(2,1)} %collective-permute-done.2, bf16[1024,2048]{1,0:T(8,128)(2,1)S(1)} %constant_dynamic-update-slice_fusion, s32[]{:T(128)S(6)} %select_n.188), kind=kOutput, calls=%fused_computation.76 | convolution fusion | flops 939524096 | bytes 8781828 | tf_op jit(solution)/shard_map/dot_general | solution.py:109
  78.2 9.0 %collective-permute-done.4 = bf16[256,1792]{1,0:T(8,128)(2,1)S(1)} collective-permute-done((bf16[256,1792]{1,0:T(8,128)(2,1)}, bf16[256,1792]{1,0:T(8,128)(2,1)S(1)}, u32[]{:S(2)}, u32[]{:S(2)}) %collective-permute-start.4) | collective-permute-done | bytes 917536 | tf_op jit(solution)/shard_map/ppermute | solution.py:37
  88.0 4.1 %fusion.32 = f32[1024,1792]{1,0:T(8,128)} fusion(bf16[256,1792]{1,0:T(8,128)(2,1)S(1)} %collective-permute-done.4, bf16[1024,2048]{1,0:T(8,128)(2,1)S(1)} %constant_dynamic-update-slice_fusion, s32[]{:T(128)S(6)} %select_n.192), kind=kOutput, calls=%fused_computation.70 | convolution fusion | flops 939524096 | bytes 8781828 | tf_op jit(solution)/shard_map/dot_general | solution.py:109
  92.0 11.4 %collective-permute-done.6 = bf16[256,1792]{1,0:T(8,128)(2,1)S(1)} collective-permute-done((bf16[256,1792]{1,0:T(8,128)(2,1)}, bf16[256,1792]{1,0:T(8,128)(2,1)S(1)}, u32[]{:S(2)}, u32[]{:S(2)}) %collective-permute-start.6) | collective-permute-done | bytes 917536 | tf_op jit(solution)/shard_map/ppermute | solution.py:37
  103.4 3.2 %collective-permute-start.8 = (bf16[256,1792]{1,0:T(8,128)(2,1)S(1)}, bf16[256,1792]{1,0:T(8,128)(2,1)}, u32[]{:S(2)}, u32[]{:S(2)}) collective-permute-start(bf16[256,1792]{1,0:T(8,128)(2,1)S(1)} %collective-permute-done.4), channel_id=1, source_target_pairs={{0,1},{1,0},{2,3},{3,2},{4,5},{5,4},{6,7},{7,6},{8,9},{9,8},{10,11... | collective-permute-start | bytes 2752520 | tf_op jit(solution)/shard_map/ppermute | solution.py:37
  106.7 4.1 %fusion.26 = f32[1024,1792]{1,0:T(8,128)} fusion(bf16[256,1792]{1,0:T(8,128)(2,1)S(1)} %collective-permute-done.6, bf16[1024,2048]{1,0:T(8,128)(2,1)S(1)} %constant_dynamic-update-slice_fusion, s32[]{:T(128)S(6)} %select_n.194), kind=kOutput, calls=%fused_computation.64 | convolution fusion | flops 939524096 | bytes 8781828 | tf_op jit(solution)/shard_map/dot_general | solution.py:109
  110.7 4.1 %fusion.23 = f32[1024,1792]{1,0:T(8,128)} fusion(bf16[256,1792]{1,0:T(8,128)(2,1)S(1)} %collective-permute-done.7, bf16[1024,2048]{1,0:T(8,128)(2,1)S(1)} %constant_dynamic-update-slice_fusion, s32[]{:T(128)S(6)} %select_n.195), kind=kOutput, calls=%fused_computation.61 | convolution fusion | flops 939524096 | bytes 8781828 | tf_op jit(solution)/shard_map/dot_general | solution.py:109
  114.8 5.3 %fusion.29 = f32[1024,1792]{1,0:T(8,128)} fusion(bf16[256,1792]{1,0:T(8,128)(2,1)} %collective-permute-done.5, bf16[1024,2048]{1,0:T(8,128)(2,1)S(1)} %constant_dynamic-update-slice_fusion, s32[]{:T(128)S(6)} %select_n.193), kind=kOutput, calls=%fused_computation.67 | convolution fusion | flops 939524096 | bytes 8781828 | tf_op jit(solution)/shard_map/dot_general | solution.py:109
  120.1 5.2 %collective-permute-done.8 = bf16[256,1792]{1,0:T(8,128)(2,1)} collective-permute-done((bf16[256,1792]{1,0:T(8,128)(2,1)S(1)}, bf16[256,1792]{1,0:T(8,128)(2,1)}, u32[]{:S(2)}, u32[]{:S(2)}) %collective-permute-start.8) | collective-permute-done | bytes 917536 | tf_op jit(solution)/shard_map/ppermute | solution.py:37
  125.3 20.4 %multiply_reduce_fusion = (f32[1024]{0:T(1024)S(1)}, f32[1024]{0:T(1024)S(1)}, f32[1024,1792]{1,0:T(8,128)}) fusion(f32[1792]{0:T(1024)S(1)} %fusion.81, bf16[512,1792]{1,0:T(8,128)(2,1)} %collective-permute-done, bf16[512,1792]{1,0:T(8,128)(2,1)} %get-tuple-element.11, bf16[256,1792]{1,0:T(8,128)(2,1)} %collective-permute-done.8, ...), kind=kOutput, calls=%fused_computation.8 | convolution fusion | flops 968882176 | bytes 63847428 | tf_op jit(solution)/shard_map/dot_general | solution.py:109
  145.7 2.4 collective-permute-start.9
  148.1 2.1 multiply_subtract_fusion
  150.2 5.5 %fusion.5 = (f32[1792]{0:T(1024)S(1)}, bf16[1024,1792]{1,0:T(8,128)(2,1)S(1)}) fusion(f32[1024,1792]{1,0:T(8,128)} %get-tuple-element.27, f32[1024]{0:T(1024)S(1)} %bitcast.90, bf16[512,1792]{1,0:T(8,128)(2,1)} %collective-permute-done, bf16[512,1792]{1,0:T(8,128)(2,1)} %get-tuple-element.11, f32[1024]{0:T(1024)S(1)} %mul.170, f32[1792]{0:T(1024)S(1)} %fusion.81), kind=kLoop, calls=%fused_computation.7 | loop fusion | flops 22018304 | bytes 14702592 | tf_op jit(solution)/shard_map/reduce_sum | solution.py:171
  159.2 2.7 %collective-permute-start.18 = (f32[1792]{0:T(1024)S(1)}, f32[1792]{0:T(1024)S(1)}, u32[]{:S(2)}, u32[]{:S(2)}) collective-permute-start(f32[1792]{0:T(1024)S(1)} %get-tuple-element.9), channel_id=1, source_target_pairs={{0,1},{1,0},{2,3},{3,2},{4,5},{5,4},{6,7},{7,6},{8,9},{9,8},{10,11... | collective-permute-start | bytes 21512 | tf_op jit(solution)/shard_map/ppermute | solution.py:37
  162.2 2.7 %collective-permute-start.14 = (bf16[256,1792]{1,0:T(8,128)(2,1)S(1)}, bf16[256,1792]{1,0:T(8,128)(2,1)S(1)}, u32[]{:S(2)}, u32[]{:S(2)}) collective-permute-start(bf16[256,1792]{1,0:T(8,128)(2,1)S(1)} %convolution_convert_fusion.1), channel_id=1, source_target_pairs={{0,1},{1,0},{2,3},{3,2},{4,5},{5,4},{6,7},{7,6},{8,9},{9,8},{10,11... | collective-permute-start | bytes 2752520 | tf_op jit(solution)/shard_map/ppermute | solution.py:37
  170.4 1.9 fusion.14
  192.0 18.5 %collective-permute-done.19 = f32[1792]{0:T(1024)S(1)} collective-permute-done((f32[1792]{0:T(1024)S(1)}, f32[1792]{0:T(1024)S(1)}, u32[]{:S(2)}, u32[]{:S(2)}) %collective-permute-start.19) | collective-permute-done | bytes 7200 | tf_op jit(solution)/shard_map/ppermute | solution.py:37
  217.9 2.1 add_convert_fusion
  219.9 9.7 %collective-permute-done.11 = bf16[256,1792]{1,0:T(8,128)(2,1)S(1)} collective-permute-done((bf16[256,1792]{1,0:T(8,128)(2,1)S(1)}, bf16[256,1792]{1,0:T(8,128)(2,1)S(1)}, u32[]{:S(2)}, u32[]{:S(2)}) %collective-permute-start.11) | collective-permute-done | bytes 917536 | tf_op jit(solution)/shard_map/ppermute | solution.py:37
  229.7 5.7 %collective-permute-done.13 = bf16[256,1792]{1,0:T(8,128)(2,1)S(1)} collective-permute-done((bf16[256,1792]{1,0:T(8,128)(2,1)S(1)}, bf16[256,1792]{1,0:T(8,128)(2,1)S(1)}, u32[]{:S(2)}, u32[]{:S(2)}) %collective-permute-start.13) | collective-permute-done | bytes 917536 | tf_op jit(solution)/shard_map/ppermute | solution.py:37
  237.8 2.3 maximum_bitcast_fusion
  (109 shorter events, 54.7 us)
Async XLA Ops:
  0.6 24.3 %copy-start = (f32[1,3584]{1,0:T(1,128)S(1)}, f32[1,3584]{1,0:T(1,128)}, u32[]{:S(2)}) copy-start(f32[1,3584]{1,0:T(1,128)} %param.10) | copy-start | bytes 43012
  0.7 9.2 %copy-start.5 = (bf16[1,256,3584]{2,1,0:T(8,128)(2,1)S(1)}, bf16[1,256,3584]{2,1,0:T(8,128)(2,1)}, u32[]{:S(2)}) copy-start(bf16[1,256,3584]{2,1,0:T(8,128)(2,1)} %param.9) | copy-start | bytes 5505028
  8.5 10.1 %collective-permute-start.21 = (bf16[8,256,224]{1,2,0:T(8,128)(2,1)}, bf16[8,256,224]{1,2,0:T(8,128)(2,1)}, u32[]{:S(2)}, u32[]{:S(2)}) collective-permute-start(bf16[8,256,224]{1,2,0:T(8,128)(2,1)} %fusion.19), channel_id=1, source_target_pairs={{0,8},{1,9},{2,10},{3,11},{4,12},{5,13},{6,14},{7,15},{8,0},{9,1},... | collective-permute-start | bytes 2752520 | tf_op jit(solution)/shard_map/ppermute | solution.py:37
  10.9 53.5 %collective-permute-start.2 = (bf16[256,1792]{1,0:T(8,128)(2,1)S(1)}, bf16[256,1792]{1,0:T(8,128)(2,1)}, u32[]{:S(2)}, u32[]{:S(2)}) collective-permute-start(bf16[256,1792]{1,0:T(8,128)(2,1)S(1)} %get-tuple-element.20), channel_id=1, source_target_pairs={{0,6},{1,7},{2,4},{3,5},{4,2},{5,3},{6,0},{7,1},{8,10},{9,11},{10,... | collective-permute-start | bytes 2752520 | tf_op jit(solution)/shard_map/ppermute | solution.py:37
  12.3 102.5 %collective-permute-start.5 = (bf16[256,1792]{1,0:T(8,128)(2,1)S(1)}, bf16[256,1792]{1,0:T(8,128)(2,1)}, u32[]{:S(2)}, u32[]{:S(2)}) collective-permute-start(bf16[256,1792]{1,0:T(8,128)(2,1)S(1)} %get-tuple-element.20), channel_id=1, source_target_pairs={{0,1},{1,0},{2,3},{3,2},{4,5},{5,4},{6,7},{7,6},{8,9},{9,8},{10,11... | collective-permute-start | bytes 2752520 | tf_op jit(solution)/shard_map/ppermute | solution.py:37
  15.9 48.6 %collective-permute-start.1 = (bf16[512,2048]{1,0:T(8,128)(2,1)}, bf16[512,2048]{1,0:T(8,128)(2,1)}, u32[]{:S(2)}, u32[]{:S(2)}) collective-permute-start(bf16[512,2048]{1,0:T(8,128)(2,1)} %param.7), channel_id=1, source_target_pairs={{0,2},{1,3},{2,0},{3,1},{4,6},{5,7},{6,4},{7,5},{8,14},{9,15},{10,... | collective-permute-start | bytes 6291464 | tf_op jit(solution)/shard_map/ppermute | solution.py:37
  17.8 39.4 %collective-permute-start.3 = (bf16[256,1792]{1,0:T(8,128)(2,1)}, bf16[256,1792]{1,0:T(8,128)(2,1)}, u32[]{:S(2)}, u32[]{:S(2)}) collective-permute-start(bf16[256,1792]{1,0:T(8,128)(2,1)} %get-tuple-element.19), channel_id=1, source_target_pairs={{0,2},{1,3},{2,0},{3,1},{4,6},{5,7},{6,4},{7,5},{8,14},{9,15},{10,... | collective-permute-start | bytes 2752520 | tf_op jit(solution)/shard_map/ppermute | solution.py:37
  21.6 11.0 %collective-permute-start.22 = (bf16[2,2,256,224]{2,3,1,0:T(8,128)(2,1)}, bf16[2,2,256,224]{2,3,1,0:T(8,128)(2,1)}, u32[]{:S(2)}, u32[]{:S(2)}) collective-permute-start(bf16[2,2,256,224]{2,3,1,0:T(8,128)(2,1)} %pad_maximum_fusion.1), channel_id=1, source_target_pairs={{0,16},{1,17},{2,18},{3,19},{4,20},{5,21},{6,22},{7,23},{8,24},{9,... | collective-permute-start | bytes 1376264 | tf_op jit(solution)/shard_map/ppermute | solution.py:37
  25.0 32.2 %copy-start.6 = (bf16[512,1792]{1,0:T(8,128)(2,1)S(1)}, bf16[512,1792]{1,0:T(8,128)(2,1)}, u32[]{:S(2)}) copy-start(bf16[512,1792]{1,0:T(8,128)(2,1)} %get-tuple-element.12) | copy-start | bytes 5505028
  33.7 26.3 %collective-permute-start.23 = (bf16[2,256,224]{1,2,0:T(8,128)(2,1)S(1)}, bf16[2,256,224]{1,2,0:T(8,128)(2,1)S(1)}, u32[]{:S(2)}, u32[]{:S(2)}) collective-permute-start(bf16[2,256,224]{1,2,0:T(8,128)(2,1)S(1)} %fusion.62), channel_id=1, source_target_pairs={{0,48},{1,49},{2,50},{3,51},{4,52},{5,53},{6,54},{7,55},{8,56},{9,... | collective-permute-start | bytes 688136 | tf_op jit(solution)/shard_map/ppermute | solution.py:37
  57.3 62.8 %collective-permute-start = (bf16[512,1792]{1,0:T(8,128)(2,1)S(1)}, bf16[512,1792]{1,0:T(8,128)(2,1)}, u32[]{:S(2)}, u32[]{:S(2)}) collective-permute-start(bf16[512,1792]{1,0:T(8,128)(2,1)S(1)} %copy-done.6), channel_id=1, source_target_pairs={{0,2},{1,3},{2,0},{3,1},{4,6},{5,7},{6,4},{7,5},{8,14},{9,15},{10,... | collective-permute-start | bytes 5505032 | tf_op jit(solution)/shard_map/ppermute | solution.py:37
  60.1 50.7 %collective-permute-start.7 = (bf16[256,1792]{1,0:T(8,128)(2,1)}, bf16[256,1792]{1,0:T(8,128)(2,1)S(1)}, u32[]{:S(2)}, u32[]{:S(2)}) collective-permute-start(bf16[256,1792]{1,0:T(8,128)(2,1)} %collective-permute-done.3), channel_id=1, source_target_pairs={{0,1},{1,0},{2,3},{3,2},{4,5},{5,4},{6,7},{7,6},{8,9},{9,8},{10,11... | collective-permute-start | bytes 2752520 | tf_op jit(solution)/shard_map/ppermute | solution.py:37
  64.5 22.7 %collective-permute-start.4 = (bf16[256,1792]{1,0:T(8,128)(2,1)}, bf16[256,1792]{1,0:T(8,128)(2,1)S(1)}, u32[]{:S(2)}, u32[]{:S(2)}) collective-permute-start(bf16[256,1792]{1,0:T(8,128)(2,1)} %collective-permute-done.3), channel_id=1, source_target_pairs={{0,6},{1,7},{2,4},{3,5},{4,2},{5,3},{6,0},{7,1},{8,10},{9,11},{10,... | collective-permute-start | bytes 2752520 | tf_op jit(solution)/shard_map/ppermute | solution.py:37
  64.5 38.9 %collective-permute-start.6 = (bf16[256,1792]{1,0:T(8,128)(2,1)}, bf16[256,1792]{1,0:T(8,128)(2,1)S(1)}, u32[]{:S(2)}, u32[]{:S(2)}) collective-permute-start(bf16[256,1792]{1,0:T(8,128)(2,1)} %collective-permute-done.2), channel_id=1, source_target_pairs={{0,1},{1,0},{2,3},{3,2},{4,5},{5,4},{6,7},{7,6},{8,9},{9,8},{10,11... | collective-permute-start | bytes 2752520 | tf_op jit(solution)/shard_map/ppermute | solution.py:37
  66.3 48.5 %copy-start.2 = (bf16[1024,2048]{1,0:T(8,128)(2,1)}, bf16[1024,2048]{1,0:T(8,128)(2,1)S(1)}, u32[]{:S(2)}) copy-start(bf16[1024,2048]{1,0:T(8,128)(2,1)S(1)} %constant_dynamic-update-slice_fusion) | copy-start | bytes 12582916
  87.2 16.2 %copy-start.10 = (bf16[256,1792]{1,0:T(8,128)(2,1)}, bf16[256,1792]{1,0:T(8,128)(2,1)S(1)}, u32[]{:S(2)}) copy-start(bf16[256,1792]{1,0:T(8,128)(2,1)S(1)} %collective-permute-done.4) | copy-start | bytes 2752516
  87.2 60.9 %collective-permute-start.24 = (bf16[256,224]{0,1:T(8,128)(2,1)}, bf16[256,224]{0,1:T(8,128)(2,1)}, u32[]{:S(2)}, u32[]{:S(2)}) collective-permute-start(bf16[256,224]{0,1:T(8,128)(2,1)} %fusion.64), channel_id=1, source_target_pairs={{0,64},{1,65},{2,66},{3,67},{4,68},{5,69},{6,70},{7,71},{8,72},{9,... | collective-permute-start | bytes 344072 | tf_op jit(solution)/shard_map/ppermute | solution.py:37
  103.4 7.3 %copy-start.12 = (bf16[256,1792]{1,0:T(8,128)(2,1)}, bf16[256,1792]{1,0:T(8,128)(2,1)S(1)}, u32[]{:S(2)}) copy-start(bf16[256,1792]{1,0:T(8,128)(2,1)S(1)} %collective-permute-done.6) | copy-start | bytes 2752516
  103.4 21.9 %collective-permute-start.8 = (bf16[256,1792]{1,0:T(8,128)(2,1)S(1)}, bf16[256,1792]{1,0:T(8,128)(2,1)}, u32[]{:S(2)}, u32[]{:S(2)}) collective-permute-start(bf16[256,1792]{1,0:T(8,128)(2,1)S(1)} %collective-permute-done.4), channel_id=1, source_target_pairs={{0,1},{1,0},{2,3},{3,2},{4,5},{5,4},{6,7},{7,6},{8,9},{9,8},{10,11... | collective-permute-start | bytes 2752520 | tf_op jit(solution)/shard_map/ppermute | solution.py:37
  145.7 4.4 %collective-permute-start.9 = (f32[2,1024]{1,0:T(2,128)S(1)}, f32[2,1024]{1,0:T(2,128)S(1)}, u32[]{:S(2)}, u32[]{:S(2)}) collective-permute-start(f32[2,1024]{1,0:T(2,128)S(1)} %pad_maximum_fusion.3), channel_id=1, source_target_pairs={{0,2},{1,3},{2,0},{3,1},{4,6},{5,7},{6,4},{7,5},{8,14},{9,15},{10,... | collective-permute-start | bytes 24584 | tf_op jit(solution)/shard_map/ppermute | solution.py:37
  150.2 5.5 %copy-start.3 = (bf16[1024,2048]{1,0:T(8,128)(2,1)S(1)}, bf16[1024,2048]{1,0:T(8,128)(2,1)}, u32[]{:S(2)}) copy-start(bf16[1024,2048]{1,0:T(8,128)(2,1)} %copy-done.2) | copy-start | bytes 12582916
  159.2 30.2 %collective-permute-start.18 = (f32[1792]{0:T(1024)S(1)}, f32[1792]{0:T(1024)S(1)}, u32[]{:S(2)}, u32[]{:S(2)}) collective-permute-start(f32[1792]{0:T(1024)S(1)} %get-tuple-element.9), channel_id=1, source_target_pairs={{0,1},{1,0},{2,3},{3,2},{4,5},{5,4},{6,7},{7,6},{8,9},{9,8},{10,11... | collective-permute-start | bytes 21512 | tf_op jit(solution)/shard_map/ppermute | solution.py:37
  161.9 49.4 %collective-permute-start.12 = (bf16[256,1792]{1,0:T(8,128)(2,1)S(1)}, bf16[256,1792]{1,0:T(8,128)(2,1)S(1)}, u32[]{:S(2)}, u32[]{:S(2)}) collective-permute-start(bf16[256,1792]{1,0:T(8,128)(2,1)S(1)} %convolution_convert_fusion.2), channel_id=1, source_target_pairs={{0,6},{1,7},{2,4},{3,5},{4,2},{5,3},{6,0},{7,1},{8,10},{9,11},{10,... | collective-permute-start | bytes 2752520 | tf_op jit(solution)/shard_map/ppermute | solution.py:37
  161.9 24.7 %collective-permute-start.15 = (bf16[256,1792]{1,0:T(8,128)(2,1)S(1)}, bf16[256,1792]{1,0:T(8,128)(2,1)S(1)}, u32[]{:S(2)}, u32[]{:S(2)}) collective-permute-start(bf16[256,1792]{1,0:T(8,128)(2,1)S(1)} %convolution_convert_fusion), channel_id=1, source_target_pairs={{0,1},{1,0},{2,3},{3,2},{4,5},{5,4},{6,7},{7,6},{8,9},{9,8},{10,11... | collective-permute-start | bytes 2752520 | tf_op jit(solution)/shard_map/ppermute | solution.py:37
  162.2 51.3 %collective-permute-start.14 = (bf16[256,1792]{1,0:T(8,128)(2,1)S(1)}, bf16[256,1792]{1,0:T(8,128)(2,1)S(1)}, u32[]{:S(2)}, u32[]{:S(2)}) collective-permute-start(bf16[256,1792]{1,0:T(8,128)(2,1)S(1)} %convolution_convert_fusion.1), channel_id=1, source_target_pairs={{0,1},{1,0},{2,3},{3,2},{4,5},{5,4},{6,7},{7,6},{8,9},{9,8},{10,11... | collective-permute-start | bytes 2752520 | tf_op jit(solution)/shard_map/ppermute | solution.py:37
  175.6 42.3 %collective-permute-start.10 = (bf16[512,2048]{1,0:T(8,128)(2,1)S(1)}, bf16[512,2048]{1,0:T(8,128)(2,1)S(1)}, u32[]{:S(2)}, u32[]{:S(2)}) collective-permute-start(bf16[512,2048]{1,0:T(8,128)(2,1)S(1)} %fusion.11), channel_id=1, source_target_pairs={{0,2},{1,3},{2,0},{3,1},{4,6},{5,7},{6,4},{7,5},{8,14},{9,15},{10,... | collective-permute-start | bytes 6291464 | tf_op jit(solution)/shard_map/ppermute | solution.py:37
  187.8 26.4 %collective-permute-start.16 = (bf16[256,1792]{1,0:T(8,128)(2,1)S(1)}, bf16[256,1792]{1,0:T(8,128)(2,1)S(1)}, u32[]{:S(2)}, u32[]{:S(2)}) collective-permute-start(bf16[256,1792]{1,0:T(8,128)(2,1)S(1)} %fusion.10), channel_id=1, source_target_pairs={{0,6},{1,7},{2,4},{3,5},{4,2},{5,3},{6,0},{7,1},{8,10},{9,11},{10,... | collective-permute-start | bytes 2752520 | tf_op jit(solution)/shard_map/ppermute | solution.py:37
  189.4 21.1 %collective-permute-start.19 = (f32[1792]{0:T(1024)S(1)}, f32[1792]{0:T(1024)S(1)}, u32[]{:S(2)}, u32[]{:S(2)}) collective-permute-start(f32[1792]{0:T(1024)S(1)} %add.297), channel_id=1, source_target_pairs={{0,6},{1,7},{2,4},{3,5},{4,2},{5,3},{6,0},{7,1},{8,10},{9,11},{10,... | collective-permute-start | bytes 21512 | tf_op jit(solution)/shard_map/ppermute | solution.py:37
  210.5 19.2 %collective-permute-start.11 = (bf16[256,1792]{1,0:T(8,128)(2,1)S(1)}, bf16[256,1792]{1,0:T(8,128)(2,1)S(1)}, u32[]{:S(2)}, u32[]{:S(2)}) collective-permute-start(bf16[256,1792]{1,0:T(8,128)(2,1)S(1)} %convolution_convert_fusion.3), channel_id=1, source_target_pairs={{0,6},{1,7},{2,4},{3,5},{4,2},{5,3},{6,0},{7,1},{8,10},{9,11},{10,... | collective-permute-start | bytes 2752520 | tf_op jit(solution)/shard_map/ppermute | solution.py:37
  211.3 5.9 %collective-permute-start.20 = (f32[1792]{0:T(1024)S(1)}, f32[1792]{0:T(1024)S(1)}, u32[]{:S(2)}, u32[]{:S(2)}) collective-permute-start(f32[1792]{0:T(1024)S(1)} %add.298), channel_id=1, source_target_pairs={{0,2},{1,3},{2,0},{3,1},{4,6},{5,7},{6,4},{7,5},{8,14},{9,15},{10,... | collective-permute-start | bytes 21512 | tf_op jit(solution)/shard_map/ppermute | solution.py:37
  213.6 21.8 %collective-permute-start.13 = (bf16[256,1792]{1,0:T(8,128)(2,1)S(1)}, bf16[256,1792]{1,0:T(8,128)(2,1)S(1)}, u32[]{:S(2)}, u32[]{:S(2)}) collective-permute-start(bf16[256,1792]{1,0:T(8,128)(2,1)S(1)} %fusion.9), channel_id=1, source_target_pairs={{0,1},{1,0},{2,3},{3,2},{4,5},{5,4},{6,7},{7,6},{8,9},{9,8},{10,11... | collective-permute-start | bytes 2752520 | tf_op jit(solution)/shard_map/ppermute | solution.py:37
  215.5 20.9 %collective-permute-start.17 = (bf16[256,1792]{1,0:T(8,128)(2,1)S(1)}, bf16[256,1792]{1,0:T(8,128)(2,1)S(1)}, u32[]{:S(2)}, u32[]{:S(2)}) collective-permute-start(bf16[256,1792]{1,0:T(8,128)(2,1)S(1)} %fusion.8), channel_id=1, source_target_pairs={{0,2},{1,3},{2,0},{3,1},{4,6},{5,7},{6,4},{7,5},{8,14},{9,15},{10,... | collective-permute-start | bytes 2752520 | tf_op jit(solution)/shard_map/ppermute | solution.py:37
  (7 other events, 20.6 us)

commit v2 on v0

v2 whole, which is shorter than its diff:
```python
import jax
import jax.numpy as jnp
from jax import lax
from jax.experimental import pallas as pl
from jax.experimental.pallas import tpu as pltpu
from jax.sharding import PartitionSpec as P

BF16 = jnp.bfloat16
F32 = jnp.float32
BOTH = ("replica", "fsdp")
HALF = 1792
COLS = 224
WIDE = 256
TILE = 256
TILES = HALF // TILE
LIMIT = 10 * 2**20


def partner_y(y, core):
    if core == 0:
        return y ^ 1
    return (y - 1) % 4 if y % 2 == 0 else (y + 1) % 4


def table(move):
    pairs = []
    for r in range(16):
        for f in range(8):
            z_lo, x, core, y, z_hi = r // 8, (r // 2) % 4, r % 2, f // 2, f % 2
            z_lo, x, core, y, z_hi = move(z_lo, x, core, y, z_hi)
            pairs.append((r * 8 + f, ((z_lo * 4 + x) * 2 + core) * 8 + y * 2 + z_hi))
    return pairs


TO_PARTNER = table(lambda a, x, c, y, z: (a, x, c, partner_y(y, c), z))
TO_MATE = table(lambda a, x, c, y, z: (a, x, c, partner_y(y, 1 - c), z))
TO_Z = table(lambda a, x, c, y, z: (a, x, c, y, 1 - z))
TO_CORE = table(lambda a, x, c, y, z: (a, x, 1 - c, y, z))
TO_X1 = table(lambda a, x, c, y, z: (a, x ^ 1, c, y, z))
TO_X3 = table(lambda a, x, c, y, z: (a, 3 - x, c, y, z))
TO_ZLO = table(lambda a, x, c, y, z: (1 - a, x, c, y, z))


def send(value, pairs):
    return lax.ppermute(value, BOTH, pairs)


def after(value, *others):
    return lax.optimization_barrier((value, *others))[0]


HELD = pl.BlockSpec(memory_space=pltpu.VMEM)


def near(x):
    return pltpu.with_memory_space_constraint(x, pltpu.VMEM)


def far(x):
    return pltpu.with_memory_space_constraint(x, pltpu.HBM)


def call(kernel, name, cost, out_shape, grid, in_specs, out_specs, scratch=(), aliases=None):
    built = pl.pallas_call(
        kernel,
        out_shape=out_shape,
        grid_spec=pltpu.PrefetchScalarGridSpec(
            num_scalar_prefetch=1,
            grid=grid,
            in_specs=in_specs,
            out_specs=out_specs,
            scratch_shapes=list(scratch),
        ),
        compiler_params=pltpu.CompilerParams(vmem_limit_bytes=LIMIT),
        cost_estimate=pl.CostEstimate(flops=0, bytes_accessed=int(cost * 3e6), transcendentals=0),
        input_output_aliases=aliases or {},
        name=name,
    )

    def run(at, *operands):
        placed = [near(x) if spec is HELD else far(x) for x, spec in zip(operands, in_specs)]
        return built(at, *placed)

    return run


def split_kernel(at_ref, in_ref, own_ref, other_ref, sems):
    copies = []
    rows = own_ref.shape[0] // 4
    for i in range(4):
        for s, (out_ref, half) in enumerate(((own_ref, at_ref[0]), (other_ref, 1 - at_ref[0]))):
            part = pl.ds(i * rows, rows)
            lanes = pl.ds(pl.multiple_of(half * HALF, 256), HALF)
            copies.append(
                pltpu.make_async_copy(in_ref.at[part, lanes], out_ref.at[part], sems.at[s, i])
            )
    for copy in copies:
        copy.start()
    for copy in copies:
        copy.wait()


def split(which, array):
    return call(
        split_kernel,
        "split", 2,
        [pltpu.VMEM((array.shape[0], HALF), BF16)] * 2,
        (1,),
        [pl.BlockSpec(memory_space=pl.ANY)],
        [HELD] * 2,
        [pltpu.SemaphoreType.DMA((2, 4))],
    )(which, array)


def turn_kernel(at_ref, own_ref, partner_ref, out_ref, slab_ref):
    for k in range(8):
        at = pl.ds(pl.multiple_of(at_ref[k] * 256, 256), 256)
        out_ref[k * 256 : (k + 1) * 256, :512] = jnp.transpose(own_ref[:, at])
        out_ref[k * 256 : (k + 1) * 256, 512:] = jnp.transpose(partner_ref[:, at])
    at = pl.ds(pl.multiple_of(at_ref[0] * 256, 256), 256)
    slab_ref[:512] = own_ref[:, at]
    slab_ref[512:] = partner_ref[:, at]


def turn(at, context, context_p):
    return call(
        turn_kernel,
        "turn", 4,
        [pltpu.VMEM((2048, 1024), BF16), pltpu.VMEM((1024, 256), BF16)],
        (1,),
        [HELD, HELD],
        [HELD, HELD],
    )(at, context, context_p)


def outer_parts_kernel(at_ref, delta_ref, low_ref, high_ref, kept_ref):
    rows = pl.ds(pl.multiple_of(pl.program_id(0) * 64, 64), 64)
    for core in range(2):

        @pl.when(at_ref[0] == core)
        def _(core=core):
            for k in range(8):
                away, kept = (2 * k + 1 - core) * COLS, (2 * k + core) * COLS
                away_ref = low_ref if k < 4 else high_ref
                away_ref[k % 4, rows, :COLS] = delta_ref[:, away : away + COLS].astype(BF16)
                kept_ref[k, rows, :COLS] = delta_ref[:, kept : kept + COLS]


def outer_parts(at, delta):
    return call(
        outer_parts_kernel,
        "outer_parts", 3,
        [pltpu.VMEM((4, 256, WIDE), BF16)] * 2 + [pltpu.VMEM((8, 256, WIDE), F32)],
        (4,),
        [pl.BlockSpec((64, 16 * COLS), lambda i, at: (i, 0))],
        [HELD, HELD, HELD],
    )(at, delta)


def outer_sum_kernel(at_ref, kept_in_ref, *refs, turned):
    *got_refs, away_ref, kept_ref = refs
    n = away_ref.shape[0]
    view = jnp.transpose if turned else lambda block: block

    def total(i, at):
        piece = i * len(got_refs) // n
        got = got_refs[piece][at - piece * got_refs[0].shape[0]]
        return view(kept_in_ref[at] + got.astype(F32))

    for i in range(n):
        away_ref[i] = total(i, at_ref[i]).astype(BF16)
        kept_ref[i] = total(i, at_ref[n + i])


def outer_sum(at, kept, *got, turned=False):
    n = at.shape[0] // 2

    def kernel(*refs):
        outer_sum_kernel(*refs, turned=turned)

    return call(
        kernel,
        "outer_sum", 1,
        [pltpu.VMEM((n, 256, WIDE), BF16), pltpu.VMEM((n, 256, WIDE), F32)],
        (1,),
        [HELD] * (1 + len(got)),
        [HELD, HELD],
    )(at, kept, *got)


def slabs(at_ref, block_refs):
    k = 0
    for ref in block_refs:
        for row in range(0, ref.shape[0], 256):
            yield ref, row, pl.ds(pl.multiple_of(at_ref[k] * 256, 256), 256)
            k += 1


def project_kernel(at_ref, own_ref, partner_ref, *refs):
    *block_refs, out_ref = refs
    for j in range(TILES):
        lanes = slice(j * TILE, (j + 1) * TILE)
        for s, rows_ref in enumerate((own_ref, partner_ref)):
            total = None
            for ref, row, at in slabs(at_ref, block_refs):
                term = jnp.dot(
                    rows_ref[:, at], ref[row : row + 256, lanes], preferred_element_type=F32
                )
                total = term if total is None else total + term
            out_ref[s * 512 : (s + 1) * 512, lanes] = total


def project(at, context, context_p, blocks):
    return call(
        project_kernel,
        "project", 14,
        pltpu.VMEM((1024, HALF), F32),
        (1,),
        [HELD] * (2 + len(blocks)),
        HELD,
    )(at, context, context_p, *blocks)


def gain_lanes(at_ref, j):
    return pl.ds(pl.multiple_of(at_ref[8] * HALF + j * TILE, TILE), TILE)


def stats_kernel(at_ref, acc_ref, slab_ref, block_ref, cot_ref, cot_p_ref, gain_ref, out_ref):
    for s in range(4):
        rows = slice(s * 256, (s + 1) * 256)
        part = slice((s % 2) * 256, (s % 2 + 1) * 256)
        c_ref = cot_ref if s < 2 else cot_p_ref
        squares = jnp.zeros((256, 128), F32)
        products = jnp.zeros((256, 128), F32)
        for j in range(TILES):
            lanes = slice(j * TILE, (j + 1) * TILE)
            p = acc_ref[rows, lanes] + jnp.dot(
                slab_ref[rows], block_ref[:, lanes], preferred_element_type=F32
            )
            scaled = c_ref[part, lanes].astype(F32) * gain_ref[:, gain_lanes(at_ref, j)] * p
            p = p * p
            squares += p[:, :128] + p[:, 128:]
            products += scaled[:, :128] + scaled[:, 128:]
        for i in range(2):
            chunk = slice(i * 128, (i + 1) * 128)
            top = jnp.sum(jnp.transpose(squares[chunk]), axis=0, keepdims=True)
            low = jnp.sum(jnp.transpose(products[chunk]), axis=0, keepdims=True)
            out_ref[2 * s + i] = jnp.concatenate([top] * 4 + [low] * 4, axis=0)


def row_stats(at, acc, slab, block, cot, cot_p, gain):
    return call(
        stats_kernel,
        "row_stats", 3,
        pltpu.VMEM((8, 8, 128), F32),
        (1,),
        [HELD] * 6,
        HELD,
    )(at, acc, slab, block, cot, cot_p, gain)


def two_parts(value):
    high = value.astype(BF16).astype(F32)
    row = lax.broadcasted_iota(jnp.int32, (16, value.shape[1]), 0)
    return jnp.where(row == 0, high, jnp.where(row == 1, value - high, 0.0)).astype(BF16)


def one_value(rows):
    return jnp.sum(rows.astype(F32), axis=0, keepdims=True)


def grad_kernel(
    at_ref, acc_ref, slab_ref, block_ref, cot_ref, cot_p_ref, gain_ref, mine_ref, theirs_ref,
    turned_ref,
    g_ref, x_mate_ref, o_z_ref, a_ref, b_ref,
):
    for i in range(8):
        total = mine_ref[i] + theirs_ref[(i + 4) % 8]
        inverse = lax.rsqrt(total[0:1] / 3584 + 1e-06)
        coupling = total[4:5] / 3584 * inverse * inverse * inverse
        rows = pl.ds(i * 128, 128)
        a_ref[rows, :] = jnp.transpose(jnp.broadcast_to(inverse, (128, 128)))
        b_ref[rows, :] = jnp.transpose(jnp.broadcast_to(coupling, (128, 128)))

    for j in range(TILES):
        lanes = slice(j * TILE, (j + 1) * TILE)
        block = block_ref[:, lanes]
        gain = gain_ref[:, gain_lanes(at_ref, j)]
        gain_total = jnp.zeros((8, TILE), F32)
        for i in range(4):
            rows = slice(i * 256, (i + 1) * 256)
            part = slice((i % 2) * 256, (i % 2 + 1) * 256)
            c_ref = cot_ref if i < 2 else cot_p_ref
            p = acc_ref[rows, lanes] + jnp.dot(slab_ref[rows], block, preferred_element_type=F32)
            inverse = jnp.concatenate([a_ref[rows]] * 2, axis=1)
            coupling = jnp.concatenate([b_ref[rows]] * 2, axis=1)
            cot = c_ref[part, lanes].astype(F32) * inverse
            g_ref[rows, lanes] = (cot * gain - p * coupling).astype(BF16)
            gain_total += jnp.sum((cot * p).reshape(32, 8, TILE), axis=0)
        terms = jnp.dot(turned_ref[:512], g_ref[:, lanes], preferred_element_type=F32)
        terms = terms.astype(BF16)
        x_mate_ref[:256, lanes] = terms[:256]
        x_mate_ref[256:, lanes] = two_parts(jnp.sum(gain_total, axis=0, keepdims=True))
        o_z_ref[:, lanes] = terms[256:]


def grad_step(at, acc, slab, block, cot, cot_p, gain, mine, theirs, turned):
    return call(
        grad_kernel,
        "grad_step", 6,
        (
            pltpu.VMEM((1024, HALF), BF16),
            pltpu.VMEM((272, HALF), BF16),
            pltpu.VMEM((256, HALF), BF16),
        ),
        (1,),
        [HELD] * 9,
        [HELD] * 3,
        [pltpu.VMEM((1024, 128), F32), pltpu.VMEM((1024, 128), F32)],
    )(at, acc, slab, block, cot, cot_p, gain, mine, theirs, turned)


def weight_kernel(at_ref, turned_ref, g_ref, *out_refs, first):
    n = len(out_refs)
    for j in range(TILES):
        lanes = slice(j * TILE, (j + 1) * TILE)
        terms = jnp.dot(
            turned_ref[first * 256 : (first + n) * 256],
            g_ref[:, lanes],
            preferred_element_type=F32,
        )
        for k, out_ref in enumerate(out_refs):
            out_ref[:, lanes] = terms[k * 256 : (k + 1) * 256].astype(out_ref.dtype)


def weight_terms(at, turned, g, first, n, dtype):
    def kernel(*refs):
        weight_kernel(*refs, first=first)

    return call(
        kernel,
        "weight_terms", n,
        [pltpu.VMEM((256, HALF), dtype)] * n,
        (1,),
        [HELD, HELD],
        [HELD] * n,
    )(at, turned, g)


def context_kernel(at_ref, g_ref, *refs, first):
    *block_refs, out_ref = refs
    rows = slice(first, first + out_ref.shape[0])
    for ref, row, at in slabs(at_ref, block_refs):
        part = lax.dot_general(
            g_ref[rows, :],
            ref[row : row + 256],
            (((1,), (1,)), ((), ())),
            preferred_element_type=F32,
        )
        out_ref[:, at] = part.astype(out_ref.dtype)


def context_term(at, g, first, blocks, dtype, tiles):
    def kernel(*refs):
        context_kernel(*refs, first=first)

    return call(
        kernel,
        "context_term", 2.5 * tiles,
        pltpu.VMEM((256 * tiles, 2048), dtype),
        (1,),
        [HELD] * (1 + len(blocks)),
        HELD,
    )(at, g, *blocks)


def add_kernel(at_ref, a_ref, b_ref, out_ref):
    out_ref[...] = (a_ref[...] + b_ref[...].astype(F32)).astype(BF16)


def add(at, a, b):
    return call(
        add_kernel, "add", 1, pltpu.VMEM((256, HALF), BF16), (1,), [HELD, HELD], HELD
    )(at, a, b)


def add_x_kernel(at_ref, a_ref, *refs):
    *in_refs, high_ref, low_ref = refs
    sent_ref, *got_refs = in_refs
    total = a_ref[...]
    if got_refs[0].shape[0] == 128:
        got = jnp.concatenate([got_refs[0][...], got_refs[1][:128]], axis=0)
        sums_ref, more = got_refs[1], got_refs[2:]
    else:
        got = got_refs[0][:256]
        sums_ref, more = got_refs[0], got_refs[1:]
    total = total + got.astype(F32)
    for ref in more:
        total = total + ref[...].astype(F32)
    high_ref[...] = total[:128].astype(BF16)
    low_ref[:128] = total[128:].astype(BF16)
    sums = one_value(sent_ref[sent_ref.shape[0] - 16 :])
    low_ref[128:] = two_parts(sums + one_value(sums_ref[sums_ref.shape[0] - 16 :]))


def add_x(at, own, sent, *got):
    return call(
        add_x_kernel,
        "add_x", 1,
        [pltpu.VMEM((128, HALF), BF16), pltpu.VMEM((144, HALF), BF16)],
        (1,),
        [HELD] * (2 + len(got)),
        [HELD, HELD],
    )(at, own, sent, *got)


def end_context_kernel(at_ref, a_ref, b_ref, c_ref, out_ref):
    step = pl.program_id(0)
    rows = pl.ds(pl.multiple_of(step * 128, 128), 128)
    place = pl.ds(pl.multiple_of((step % 2) * 128, 128), 128)

    @pl.when(step < 2)
    def _():
        out_ref[...] = (a_ref[rows, :] + b_ref[place, :].astype(F32)).astype(BF16)

    @pl.when(step >= 2)
    def _():
        out_ref[...] = (a_ref[rows, :] + c_ref[place, :].astype(F32)).astype(BF16)


def end_context(at, own, *got):
    return call(
        end_context_kernel,
        "end_context", 2,
        jax.ShapeDtypeStruct((512, 2048), BF16),
        (4,),
        [HELD, HELD, HELD],
        pl.BlockSpec((128, 2048), lambda i, at: (i, 0)),
    )(at, own, *got)


def place_x_kernel(at_ref, high_ref, low_ref, sent_ref, out_ref, gain_ref):
    step = pl.program_id(0)
    rows = pl.ds(pl.multiple_of((step % 2) * 64, 64), 64)

    @pl.when(step < 2)
    def _():
        out_ref[...] = high_ref[rows, :].astype(F32)

    @pl.when(step >= 2)
    def _():
        out_ref[...] = low_ref[rows, :].astype(F32)

    @pl.when(step == 0)
    def _():
        own = pl.ds(pl.multiple_of(at_ref[8] * HALF, 256), HALF)
        other = pl.ds(pl.multiple_of((1 - at_ref[8]) * HALF, 256), HALF)
        gain_ref[:, own] = one_value(sent_ref[128:])
        gain_ref[:, other] = one_value(low_ref[128:])


def place_x(at, high, low, sent):
    return call(
        place_x_kernel,
        "place_x", 2,
        [jax.ShapeDtypeStruct((256, 2 * HALF), F32), jax.ShapeDtypeStruct((1, 2 * HALF), F32)],
        (4,),
        [HELD, HELD, HELD],
        [
            pl.BlockSpec((64, HALF), lambda i, at: (i, 1 - at[8])),
            pl.BlockSpec((1, 2 * HALF), lambda i, at: (0, 0)),
        ],
    )(at, high, low, sent)


def place_o_kernel(at_ref, out_in_ref, a_ref, b_ref, c_ref, out_ref):
    rows = pl.ds(pl.multiple_of(pl.program_id(0) * 64, 64), 64)
    out_ref[...] = a_ref[rows, :] + b_ref[rows, :].astype(F32) + c_ref[rows, :].astype(F32)


def place_o(at, out, a, b, c):
    return call(
        place_o_kernel,
        "place_o", 2,
        jax.ShapeDtypeStruct((256, 2 * HALF), F32),
        (4,),
        [pl.BlockSpec(memory_space=pl.ANY), HELD, HELD, HELD],
        pl.BlockSpec((64, HALF), lambda i, at: (i, at[8])),
        aliases={1: 0},
    )(at, out, a, b, c)


def per_device(context, cotangent, weight, gain, delta, anchor, momentum):
    r = lax.axis_index("replica")
    z_lo, x, core = r // 8, (r // 2) % 4, r % 2
    f = lax.axis_index("fsdp")
    y, z = f // 2, f % 2
    low, high = y ^ 1, jnp.where(y % 2 == 0, (y + 3) % 4, (y + 1) % 4)
    partner = jnp.where(core == 0, low, high)
    mate = jnp.where(core == 0, high, low)
    opposite = (y + 2) % 4
    half = jnp.where(core == 0, ((y + 1) // 2) % 2, y // 2)

    def numbers(*values):
        return jnp.stack([jnp.asarray(value, jnp.int32) for value in values])

    def place(owner, zz):
        return owner * 2 + zz

    turn_order = numbers(
        place(opposite, 1 - z),
        place(mate, 1 - z),
        place(partner, 1 - z),
        place(mate, z),
        place(opposite, z),
        place(y, 1 - z),
        place(partner, z),
        place(y, z),
    )
    at = numbers(
        place(y, z),
        place(mate, z),
        place(partner, z),
        place(y, 1 - z),
        place(opposite, z),
        place(mate, 1 - z),
        place(partner, 1 - z),
        place(opposite, 1 - z),
        half,
    )
    which, which_core = numbers(half), numbers(core)
    x_away, x_pair = x ^ 1, 3 - x
    x1_at = numbers(
        x_away, 3 - x_away, 4 + x_away, 7 - x_away,
        x, x_pair, 4 + x, 4 + x_pair,
    )
    x3_at = numbers(1, 3, 0, 2)
    zlo_at = numbers(1 - z_lo, z_lo)

    own, other = split(which, weight[0])
    own_z = send(own, TO_Z)
    from_mate = send(own, TO_MATE)

    cot, cot_away = split(which, after(cotangent, own))
    core_low, core_high, core_kept = outer_parts(which_core, after(delta[0], own))
    core_got = [send(core_low, TO_CORE), send(core_high, TO_CORE)]
    from_partner = send(after(other, cot_away, core_high), TO_PARTNER)
    from_mate = after(from_mate, own_z, *core_got)

    mate_z = send(from_mate, TO_Z)
    from_partner = after(from_partner, from_mate)
    from_opposite = send(from_partner, TO_MATE)
    partner_z = send(from_partner, TO_Z)
    context_p = send(after(context, from_partner), TO_PARTNER)
    cot_p = send(after(cot_away, from_partner), TO_PARTNER)
    x1_away, x1_kept = outer_sum(x1_at, after(core_kept, from_partner), *core_got)
    from_opposite = after(from_opposite, mate_z, x1_away)

    x1_got = send(after(x1_away, from_opposite), TO_X1)
    opposite_z = send(from_opposite, TO_Z)

    turned, slab = turn(turn_order, context, context_p)
    x3_away, x3_kept = outer_sum(x3_at, after(x1_kept, turned), x1_got)
    x3_got = send(x3_away, TO_X3)
    blocks = [own, from_mate, from_partner, own_z, from_opposite, mate_z, partner_z, opposite_z]
    acc = project(at, context, after(context_p, turned, x3_away), blocks[:-1])
    zlo_away, zlo_kept = outer_sum(zlo_at, after(x3_kept, acc), x3_got, turned=True)
    zlo_got = send(zlo_away, TO_ZLO)

    last = (at, after(acc, zlo_away), slab, opposite_z, cot, cot_p, gain)
    mine = row_stats(*last)
    theirs = send(mine, TO_PARTNER)

    outer_grad = (after(zlo_kept, mine)[0, :COLS] + zlo_got[0, :COLS].astype(F32)) / 16
    new_momentum = 0.9 * momentum.T + outer_grad
    new_anchor = anchor.T - 0.7 * (outer_grad + 0.9 * new_momentum)
    new_momentum, new_anchor = new_momentum.T, new_anchor.T

    theirs = after(theirs, new_anchor, new_momentum)
    g, x_mate_away, o_mate_z = grad_step(*last, mine, theirs, turned)

    x_mate_z = send(x_mate_away, TO_Z)
    o_mate_z = send(o_mate_z, TO_MATE)
    part_p = context_term(at, g, 512, blocks, BF16, 1)
    got_high = send(part_p, TO_PARTNER)
    x_self_z, o_mate = weight_terms(which, turned, after(g, part_p), 2, 2, BF16)
    x_self_z = send(x_self_z, TO_Z)
    x_mate_own, o_self_z_own, x_self_own, o_self_own = weight_terms(
        which, turned, after(g, o_mate), 4, 4, F32
    )

    part_p = context_term(at, after(g, x_self_own), 768, blocks, BF16, 1)
    got_low = send(part_p, TO_PARTNER)

    x_mate = add_x(which, x_mate_own, x_mate_away, after(x_mate_z, part_p, o_mate_z))
    x_from_mate = [send(piece, TO_MATE) for piece in x_mate]
    o_self_z = add(which, after(o_self_z_own, x_mate[0]), o_mate_z)
    o_from_z = send(o_self_z, TO_Z)
    own_context = context_term(at, after(g, o_self_z), 0, blocks, F32, 2)
    o_mate = send(after(o_mate, x_mate[0], got_high), TO_MATE)

    x_self = add_x(
        which, x_self_own, x_mate[1], after(x_from_mate[0], own_context), x_from_mate[1], x_self_z
    )
    x_got = [send(piece, TO_PARTNER) for piece in x_self]
    grad_context = end_context(which, after(own_context, x_self[0]), got_high, got_low)
    grad_weight, grad_gain = place_x(at, after(x_got[0], grad_context), x_got[1], x_self[1])
    grad_weight = place_o(at, grad_weight, o_self_own, o_mate, o_from_z)
    return (grad_context, grad_weight[None], grad_gain, new_anchor, new_momentum)


def solution(mesh):
    placed = (
        P(("replica", "fsdp"), None),
        P(("replica", "fsdp"), None),
        P("replica", "fsdp", None),
        P("replica", None),
        P("replica", "fsdp", None),
        P("fsdp", "replica"),
        P("fsdp", "replica"),
    )
    return jax.shard_map(
        per_device,
        mesh=mesh,
        in_specs=placed,
        out_specs=(
            P(("replica", "fsdp"), None),
            P("replica", "fsdp", None),
            P("replica", None),
            P("fsdp", "replica"),
            P("fsdp", "replica"),
        ),
        check_vma=False,
    )
```

time: 409 us -> 188 us (0.46)
  waiting for transfers between devices: 302 us -> 74.7 us
  Pallas kernels: 0 us -> 68.9 us
  matrix products: 35.9 us -> 0 us
  blocking collectives: 31.5 us -> 0 us
  starting transfers between devices: 0.12 us -> 31.1 us
  between operations: 15.6 us -> 1.02 us
  other arithmetic: 10.9 us -> 0.91 us
    all_gather x1 -> x0, waiting for transfers between devices: 181 us -> none  [inner_step(): whole_weight = lax.all_gather(weight[0], 'fsdp', axis=0, tiled=True)]
    reduce_scatter x1 -> x0, waiting for transfers between devices: 121 us -> none  [inner_step(): lax.psum_scatter(lax.dot_general(context, grad_out, (((0,), (0,)), ((), (...]
    ppermute x0 -> x26, waiting for transfers between devices: none -> 74.7 us  [send(): return lax.ppermute(value, BOTH, pairs)]
    pallas_call x0 -> x21, Pallas kernels: none -> 68.9 us  [run(): return built(at, *placed)]
    dot_general x3 -> x0, matrix products: 35.9 us -> none  [the longest x1 13.4 us: inner_step(): lax.dot_general(grad_out, whole_weight, (((1,), (1,)), ((), ())), preferr...]
    psum x1 -> x0, blocking collectives: 31.5 us -> none  [inner_step(): grad_gain = lax.psum(jnp.sum(cot_float * normed, axis=0), 'fsdp')]
    ppermute x0 -> x26, starting transfers between devices: none -> 31.1 us  [send(): return lax.ppermute(value, BOTH, pairs)]
    unnamed x16 -> x38, local copies, waits for them, and re-layouts: 12.3 us -> 11 us
  transfers between devices with their start and end apart: 3 -> 26, of which waited for: 2 -> 14; matrix products, arithmetic and copies ran while one was open for 12% -> 1% of each run, Pallas kernels for 0% -> 31%
where the time goes in v2:
time: 188 us
  waiting for transfers between devices  74.7 us (40%)
  Pallas kernels  68.9 us (37%)
  starting transfers between devices  31.1 us (17%)
  local copies, waits for them, and re-layouts  11.3 us (6%)
    ppermute x26, waiting for transfers between devices, send(): return lax.ppermute(value, BOTH, pairs)  74.7 us
    pallas_call x21, Pallas kernels, run(): return built(at, *placed)  68.9 us
    ppermute x26, starting transfers between devices, send(): return lax.ppermute(value, BOTH, pairs)  31.1 us
    unnamed x38, local copies, waits for them, and re-layouts  11 us
  transfers between devices with their start and end apart: 26, of which 14 were waited for; matrix products, arithmetic and copies ran while one was open for 1% of the time, Pallas kernels for 31%

profile of v2, /device:TPU:1, one launch (start us, length us, event | category | flops | bytes accessed | tf_op | source)
XLA Modules:
  0.0 188.0 jit_solution(6058371963063853122)
XLA Ops:
  2.4 4.5 %collective-permute-start.2 = (bf16[256,1792]{1,0:T(8,128)(2,1)S(1)}, bf16[256,1792]{1,0:T(8,128)(2,1)S(1)}, u32[]{:S(2)}, u32[]{:S(2)}) collective-permute-start(bf16[256,1792]{1,0:T(8,128)(2,1)S(1)} %get-tuple-element.62.refs_0_.refs_2_), channel_id=1, source_target_pairs={{0,1},{1,0},{2,3},{3,2},{4,5},{5,4},{6,7},{7,6},{8,9},{9,8},{10,11... | collective-permute-start | bytes 2752520 | tf_op jit(solution)/shard_map/ppermute | solution.py:45
  8.2 3.3 %split.3 = (bf16[512,1792]{1,0:T(8,128)(2,1)S(1)}, bf16[512,1792]{1,0:T(8,128)(2,1)}) custom-call(s32[1]{0:T(128)} %bitcast.at_ref.refs_0_, bf16[512,3584]{1,0:T(8,128)(2,1)} %in_ref), custom_call_target="tpu_custom_call" | custom-call | bytes 6000000 | tf_op jit(solution)/shard_map/split/pallas_call | solution.py:82
  12.8 3.4 %outer_parts.1 = (bf16[4,256,256]{2,1,0:T(8,128)(2,1)S(1)}, bf16[4,256,256]{2,1,0:T(8,128)(2,1)S(1)}, f32[8,256,256]{2,1,0:T(8,128)S(1)}) custom-call(s32[1]{0:T(128)} %bitcast.10.at_ref, f32[256,3584]{1,0:T(8,128)} %bitcast.48), custom_call_target="tpu_custom_call" | custom-call | bytes 9000000 | tf_op jit(solution)/shard_map/outer_parts/pallas_call | solution.py:82
  23.3 3.6 %collective-permute-done.2.refs_3_.refs_5_ = bf16[256,1792]{1,0:T(8,128)(2,1)S(1)} collective-permute-done((bf16[256,1792]{1,0:T(8,128)(2,1)S(1)}, bf16[256,1792]{1,0:T(8,128)(2,1)S(1)}, u32[]{:S(2)}, u32[]{:S(2)}) %collective-permute-start.2) | collective-permute-done | bytes 917536 | tf_op jit(solution)/shard_map/ppermute | solution.py:45
  26.9 4.7 %collective-permute-done.refs_2_.refs_4_ = bf16[256,1792]{1,0:T(8,128)(2,1)} collective-permute-done((bf16[256,1792]{1,0:T(8,128)(2,1)S(1)}, bf16[256,1792]{1,0:T(8,128)(2,1)}, u32[]{:S(2)}, u32[]{:S(2)}) %collective-permute-start) | collective-permute-done | bytes 917536 | tf_op jit(solution)/shard_map/ppermute | solution.py:45
  31.7 2.7 %collective-permute-start.5 = (bf16[512,2048]{1,0:T(8,128)(2,1)}, bf16[512,2048]{1,0:T(8,128)(2,1)}, u32[]{:S(2)}, u32[]{:S(2)}) collective-permute-start(bf16[512,2048]{1,0:T(8,128)(2,1)} %own_ref.3), channel_id=1, source_target_pairs={{0,2},{1,3},{2,0},{3,1},{4,6},{5,7},{6,4},{7,5},{8,14},{9,15},{10,... | collective-permute-start | bytes 6291464 | tf_op jit(solution)/shard_map/ppermute | solution.py:45
  34.5 2.9 %collective-permute-start.9 = (bf16[256,1792]{1,0:T(8,128)(2,1)}, bf16[256,1792]{1,0:T(8,128)(2,1)}, u32[]{:S(2)}, u32[]{:S(2)}) collective-permute-start(bf16[256,1792]{1,0:T(8,128)(2,1)} %collective-permute-done.refs_2_.refs_4_), channel_id=1, source_target_pairs={{0,1},{1,0},{2,3},{3,2},{4,5},{5,4},{6,7},{7,6},{8,9},{9,8},{10,11... | collective-permute-start | bytes 2752520 | tf_op jit(solution)/shard_map/ppermute | solution.py:45
  42.6 15.8 %collective-permute-done.7.refs_5_.refs_7_ = bf16[256,1792]{1,0:T(8,128)(2,1)} collective-permute-done((bf16[256,1792]{1,0:T(8,128)(2,1)S(1)}, bf16[256,1792]{1,0:T(8,128)(2,1)}, u32[]{:S(2)}, u32[]{:S(2)}) %collective-permute-start.7) | collective-permute-done | bytes 917536 | tf_op jit(solution)/shard_map/ppermute | solution.py:45
  61.4 6.8 %collective-permute-done.5.partner_ref = bf16[512,2048]{1,0:T(8,128)(2,1)} collective-permute-done((bf16[512,2048]{1,0:T(8,128)(2,1)}, bf16[512,2048]{1,0:T(8,128)(2,1)}, u32[]{:S(2)}, u32[]{:S(2)}) %collective-permute-start.5) | collective-permute-done | bytes 2097184 | tf_op jit(solution)/shard_map/ppermute | solution.py:45
  68.3 4.1 %turn.1 = (bf16[2048,1024]{1,0:T(8,128)(2,1)S(1)}, bf16[1024,256]{1,0:T(8,128)(2,1)S(1)}) custom-call(s32[8]{0:T(128)S(1)} %stack.92.at_ref, bf16[512,2048]{1,0:T(8,128)(2,1)} %own_ref.3, bf16[512,2048]{1,0:T(8,128)(2,1)} %collective-permute-done.5.partner_ref), custom_call_target="tpu_custom_call" | custom-call | bytes 12000000 | tf_op jit(solution)/shard_map/turn/pallas_call | solution.py:82
  72.4 2.0 %copy-done = bf16[2048,1024]{1,0:T(8,128)(2,1)} copy-done((bf16[2048,1024]{1,0:T(8,128)(2,1)}, bf16[2048,1024]{1,0:T(8,128)(2,1)S(1)}, u32[]{:S(2)}) %copy-start) | copy-done | bytes 4194328
  74.3 2.4 %outer_sum.4 = (bf16[2,256,256]{2,1,0:T(8,128)(2,1)}, f32[2,256,256]{2,1,0:T(8,128)S(1)}) custom-call(s32[4]{0:T(128)S(1)} %copy-done.16, f32[4,256,256]{2,1,0:T(8,128)S(1)} %copy-done.10, bf16[4,256,256]{2,1,0:T(8,128)(2,1)} %collective-permute-done.8.refs_2_), custom_call_target="tpu_custom_call" | custom-call | bytes 3000000 | tf_op jit(solution)/shard_map/outer_sum/pallas_call | solution.py:82
  77.5 2.5 %collective-permute-start.10 = (bf16[2,256,256]{2,1,0:T(8,128)(2,1)}, bf16[2,256,256]{2,1,0:T(8,128)(2,1)S(1)}, u32[]{:S(2)}, u32[]{:S(2)}) collective-permute-start(bf16[2,256,256]{2,1,0:T(8,128)(2,1)} %get-tuple-element.80), channel_id=1, source_target_pairs={{0,48},{1,49},{2,50},{3,51},{4,52},{5,53},{6,54},{7,55},{8,56},{9,... | collective-permute-start | bytes 786440 | tf_op jit(solution)/shard_map/ppermute | solution.py:45
  81.4 10.8 %project.1.acc_ref = f32[1024,1792]{1,0:T(8,128)S(1)} custom-call(s32[9]{0:T(128)S(1)} %stack.90.at_ref.refs_0_, bf16[512,2048]{1,0:T(8,128)(2,1)} %own_ref.3, bf16[512,2048]{1,0:T(8,128)(2,1)} %collective-permute-done.5.partner_ref, bf16[256,1792]{1,0:T(8,128)(2,1)S(1)} %get-tuple-element.62.refs_0_.refs_2_, bf16[256,1792]{1,0:T(8,128)(2,1)S(1)} %copy-done.3, ...), custom_call_target="tpu_custom_call" | custom-call | bytes 42000000 | tf_op jit(solution)/shard_map/project/pallas_call | solution.py:82
  93.7 3.4 %collective-permute-done.11.block_ref.refs_9_ = bf16[256,1792]{1,0:T(8,128)(2,1)S(1)} collective-permute-done((bf16[256,1792]{1,0:T(8,128)(2,1)}, bf16[256,1792]{1,0:T(8,128)(2,1)S(1)}, u32[]{:S(2)}, u32[]{:S(2)}) %collective-permute-start.11) | collective-permute-done | bytes 917536 | tf_op jit(solution)/shard_map/ppermute | solution.py:45
  97.2 4.8 %row_stats.1.mine_ref = f32[8,8,128]{2,1,0:T(8,128)S(1)} custom-call(s32[9]{0:T(128)S(1)} %stack.90.at_ref.refs_0_, f32[1024,1792]{1,0:T(8,128)S(1)} %project.1.acc_ref, bf16[1024,256]{1,0:T(8,128)(2,1)S(1)} %get-tuple-element.86.slab_ref, bf16[256,1792]{1,0:T(8,128)(2,1)S(1)} %collective-permute-done.11.block_ref.refs_9_, bf16[512,1792]{1,0:T(8,128)(2,1)S(1)} %copy-done.6, ...), custom_call_target="tpu_custom_call" | custom-call | bytes 9000000 | tf_op jit(solution)/shard_map/row_stats/pallas_call | solution.py:82
  103.0 3.1 %collective-permute-done.13.theirs_ref = f32[8,8,128]{2,1,0:T(8,128)S(1)} collective-permute-done((f32[8,8,128]{2,1,0:T(8,128)S(1)}, f32[8,8,128]{2,1,0:T(8,128)S(1)}, u32[]{:S(2)}, u32[]{:S(2)}) %collective-permute-start.13) | collective-permute-done | bytes 32800 | tf_op jit(solution)/shard_map/ppermute | solution.py:45
  106.1 6.8 %grad_step.1 = (bf16[1024,1792]{1,0:T(8,128)(2,1)S(1)}, bf16[272,1792]{1,0:T(8,128)(2,1)S(1)}, bf16[256,1792]{1,0:T(8,128)(2,1)S(1)}) custom-call(s32[9]{0:T(128)S(1)} %stack.90.at_ref.refs_0_, f32[1024,1792]{1,0:T(8,128)S(1)} %project.1.acc_ref, bf16[1024,256]{1,0:T(8,128)(2,1)S(1)} %get-tuple-element.86.slab_ref, ...), custom_call_target="tpu_custom_call" | custom-call | bytes 18000000 | tf_op jit(solution)/shard_map/grad_step/pallas_call | solution.py:82
  113.1 4.7 %context_term.3 = bf16[256,2048]{1,0:T(8,128)(2,1)S(1)} custom-call(s32[9]{0:T(128)S(1)} %stack.90.at_ref.refs_0_, bf16[1024,1792]{1,0:T(8,128)(2,1)S(1)} %get-tuple-element.105.refs_1_.refs_2_, bf16[256,1792]{1,0:T(8,128)(2,1)S(1)} %get-tuple-element.62.refs_0_.refs_2_, bf16[256,1792]{1,0:T(8,128)(2,1)S(1)} %copy-done.4, ...), custom_call_target="tpu_custom_call" | custom-call | bytes 7500000 | tf_op jit(solution)/shard_map/context_term/pallas_call | solution.py:82
  118.0 2.1 %weight_terms.2 = (bf16[256,1792]{1,0:T(8,128)(2,1)S(1)}, bf16[256,1792]{1,0:T(8,128)(2,1)S(1)}) custom-call(s32[1]{0:T(128)} %bitcast.at_ref.refs_0_, bf16[2048,1024]{1,0:T(8,128)(2,1)S(1)} %copy-done.1, bf16[1024,1792]{1,0:T(8,128)(2,1)S(1)} %get-tuple-element.105.refs_1_.refs_2_), custom_call_target="tpu_custom_call" | custom-call | bytes 6000000 | tf_op jit(solution)/shard_map/weight_terms/pallas_call | solution.py:82
  120.1 3.0 %collective-permute-start.19 = (bf16[256,1792]{1,0:T(8,128)(2,1)S(1)}, bf16[256,1792]{1,0:T(8,128)(2,1)S(1)}, u32[]{:S(2)}, u32[]{:S(2)}) collective-permute-start(bf16[256,1792]{1,0:T(8,128)(2,1)S(1)} %get-tuple-element.108), channel_id=1, source_target_pairs={{0,1},{1,0},{2,3},{3,2},{4,5},{5,4},{6,7},{7,6},{8,9},{9,8},{10,11... | collective-permute-start | bytes 2752520 | tf_op jit(solution)/shard_map/ppermute | solution.py:45
  123.1 4.0 %weight_terms.3 = (f32[256,1792]{1,0:T(8,128)S(1)}, f32[256,1792]{1,0:T(8,128)S(1)}, f32[256,1792]{1,0:T(8,128)S(1)}, f32[256,1792]{1,0:T(8,128)S(1)}) custom-call(s32[1]{0:T(128)} %bitcast.at_ref.refs_0_, bf16[2048,1024]{1,0:T(8,128)(2,1)S(1)} %copy-done.1, bf16[1024,1792]{1,0:T(8,128)(2,1)S(1)} %get-tuple-element.105.refs_1_.refs_2_), custom_call_target="tpu_custom_call" | custom-call | bytes 12000000 | tf_op jit(solution)/shard_map/weight_terms/pallas_call | solution.py:82
  127.1 4.7 %context_term.4 = bf16[256,2048]{1,0:T(8,128)(2,1)S(1)} custom-call(s32[9]{0:T(128)S(1)} %stack.90.at_ref.refs_0_, bf16[1024,1792]{1,0:T(8,128)(2,1)S(1)} %get-tuple-element.105.refs_1_.refs_2_, bf16[256,1792]{1,0:T(8,128)(2,1)S(1)} %get-tuple-element.62.refs_0_.refs_2_, bf16[256,1792]{1,0:T(8,128)(2,1)S(1)} %copy-done.4, ...), custom_call_target="tpu_custom_call" | custom-call | bytes 7500000 | tf_op jit(solution)/shard_map/context_term/pallas_call | solution.py:82
  131.8 5.4 %collective-permute-done.15.refs_1_ = bf16[272,1792]{1,0:T(8,128)(2,1)S(1)} collective-permute-done((bf16[272,1792]{1,0:T(8,128)(2,1)S(1)}, bf16[272,1792]{1,0:T(8,128)(2,1)S(1)}, u32[]{:S(2)}, u32[]{:S(2)}) %collective-permute-start.15) | collective-permute-done | bytes 974880 | tf_op jit(solution)/shard_map/ppermute | solution.py:45
  139.2 2.6 %collective-permute-start.25 = (bf16[256,1792]{1,0:T(8,128)(2,1)S(1)}, bf16[256,1792]{1,0:T(8,128)(2,1)S(1)}, u32[]{:S(2)}, u32[]{:S(2)}) collective-permute-start(bf16[256,1792]{1,0:T(8,128)(2,1)S(1)} %add.137), channel_id=1, source_target_pairs={{0,1},{1,0},{2,3},{3,2},{4,5},{5,4},{6,7},{7,6},{8,9},{9,8},{10,11... | collective-permute-start | bytes 2752520 | tf_op jit(solution)/shard_map/ppermute | solution.py:45
  141.8 5.0 %collective-permute-done.17.refs_1_ = bf16[128,1792]{1,0:T(8,128)(2,1)S(1)} collective-permute-done((bf16[128,1792]{1,0:T(8,128)(2,1)S(1)}, bf16[128,1792]{1,0:T(8,128)(2,1)S(1)}, u32[]{:S(2)}, u32[]{:S(2)}) %collective-permute-start.17) | collective-permute-done | bytes 458784 | tf_op jit(solution)/shard_map/ppermute | solution.py:45
  147.0 6.7 %context_term.5.a_ref = f32[512,2048]{1,0:T(8,128)S(1)} custom-call(s32[9]{0:T(128)S(1)} %stack.90.at_ref.refs_0_, bf16[1024,1792]{1,0:T(8,128)(2,1)S(1)} %get-tuple-element.105.refs_1_.refs_2_, bf16[256,1792]{1,0:T(8,128)(2,1)S(1)} %get-tuple-element.62.refs_0_.refs_2_, bf16[256,1792]{1,0:T(8,128)(2,1)S(1)} %copy-done.4, ...), custom_call_target="tpu_custom_call" | custom-call | bytes 15000000 | tf_op jit(solution)/shard_map/context_term/pallas_call | solution.py:82
  153.7 3.2 %collective-permute-done.19.refs_3_ = bf16[256,1792]{1,0:T(8,128)(2,1)S(1)} collective-permute-done((bf16[256,1792]{1,0:T(8,128)(2,1)S(1)}, bf16[256,1792]{1,0:T(8,128)(2,1)S(1)}, u32[]{:S(2)}, u32[]{:S(2)}) %collective-permute-start.19) | collective-permute-done | bytes 917536 | tf_op jit(solution)/shard_map/ppermute | solution.py:45
  158.3 2.7 %collective-permute-start.22 = (bf16[128,1792]{1,0:T(8,128)(2,1)S(1)}, bf16[128,1792]{1,0:T(8,128)(2,1)S(1)}, u32[]{:S(2)}, u32[]{:S(2)}) collective-permute-start(bf16[128,1792]{1,0:T(8,128)(2,1)S(1)} %get-tuple-element.109), channel_id=1, source_target_pairs={{0,2},{1,3},{2,0},{3,1},{4,6},{5,7},{6,4},{7,5},{8,14},{9,15},{10,... | collective-permute-start | bytes 1376264 | tf_op jit(solution)/shard_map/ppermute | solution.py:45
  163.6 19.6 %collective-permute-done.22.high_ref = bf16[128,1792]{1,0:T(8,128)(2,1)S(1)} collective-permute-done((bf16[128,1792]{1,0:T(8,128)(2,1)S(1)}, bf16[128,1792]{1,0:T(8,128)(2,1)S(1)}, u32[]{:S(2)}, u32[]{:S(2)}) %collective-permute-start.22) | collective-permute-done | bytes 458784 | tf_op jit(solution)/shard_map/ppermute | solution.py:45
  183.2 2.4 %place_x.1 = (f32[256,3584]{1,0:T(8,128)}, f32[1,3584]{1,0:T(1,128)}) custom-call(s32[9]{0:T(128)S(1)} %stack.90.at_ref.refs_0_, bf16[128,1792]{1,0:T(8,128)(2,1)S(1)} %collective-permute-done.22.high_ref, bf16[144,1792]{1,0:T(8,128)(2,1)S(1)} %collective-permute-done.23.low_ref, bf16[144,1792]{1,0:T(8,128)(2,1)S(1)} %get-tuple-element.112.sent_ref), custom_call_target="tpu_custom_call" | custom-call | bytes 6000000 | tf_op jit(solution)/shard_map/place_x/pallas_call | solution.py:82
  185.6 2.4 %place_o.1 = f32[256,3584]{1,0:T(8,128)} custom-call(s32[9]{0:T(128)S(1)} %stack.90.at_ref.refs_0_, f32[256,3584]{1,0:T(8,128)} %get-tuple-element.113.out_in_ref, f32[256,1792]{1,0:T(8,128)S(1)} %get-tuple-element.114.a_ref, bf16[256,1792]{1,0:T(8,128)(2,1)S(1)} %collective-permute-done.24.b_ref, ...), custom_call_target="tpu_custom_call", output_to_operand_aliasing={{}: (1, {})} | custom-call | bytes 6000000 | tf_op jit(solution)/shard_map/place_o/pallas_call | solution.py:82
  (84 shorter events, 30.9 us)
Async XLA Ops:
  2.4 24.6 %collective-permute-start.2 = (bf16[256,1792]{1,0:T(8,128)(2,1)S(1)}, bf16[256,1792]{1,0:T(8,128)(2,1)S(1)}, u32[]{:S(2)}, u32[]{:S(2)}) collective-permute-start(bf16[256,1792]{1,0:T(8,128)(2,1)S(1)} %get-tuple-element.62.refs_0_.refs_2_), channel_id=1, source_target_pairs={{0,1},{1,0},{2,3},{3,2},{4,5},{5,4},{6,7},{7,6},{8,9},{9,8},{10,11... | collective-permute-start | bytes 2752520 | tf_op jit(solution)/shard_map/ppermute | solution.py:45
  6.9 20.1 %collective-permute-start.1 = (bf16[256,1792]{1,0:T(8,128)(2,1)S(1)}, bf16[256,1792]{1,0:T(8,128)(2,1)S(1)}, u32[]{:S(2)}, u32[]{:S(2)}) collective-permute-start(bf16[256,1792]{1,0:T(8,128)(2,1)S(1)} %get-tuple-element.62.refs_0_.refs_2_), channel_id=1, source_target_pairs={{0,6},{1,7},{2,4},{3,5},{4,2},{5,3},{6,0},{7,1},{8,10},{9,11},{10,... | collective-permute-start | bytes 2752520 | tf_op jit(solution)/shard_map/ppermute | solution.py:45
  17.5 14.2 %collective-permute-start = (bf16[256,1792]{1,0:T(8,128)(2,1)S(1)}, bf16[256,1792]{1,0:T(8,128)(2,1)}, u32[]{:S(2)}, u32[]{:S(2)}) collective-permute-start(bf16[256,1792]{1,0:T(8,128)(2,1)S(1)} %get-tuple-element.67), channel_id=1, source_target_pairs={{0,2},{1,3},{2,0},{3,1},{4,6},{5,7},{6,4},{7,5},{8,14},{9,15},{10,... | collective-permute-start | bytes 2752520 | tf_op jit(solution)/shard_map/ppermute | solution.py:45
  19.4 2.4 %collective-permute-start.3 = (bf16[4,256,256]{2,1,0:T(8,128)(2,1)S(1)}, bf16[4,256,256]{2,1,0:T(8,128)(2,1)S(1)}, u32[]{:S(2)}, u32[]{:S(2)}) collective-permute-start(bf16[4,256,256]{2,1,0:T(8,128)(2,1)S(1)} %get-tuple-element.68), channel_id=1, source_target_pairs={{0,8},{1,9},{2,10},{3,11},{4,12},{5,13},{6,14},{7,15},{8,0},{9,1},... | collective-permute-start | bytes 1572872 | tf_op jit(solution)/shard_map/ppermute | solution.py:45
  20.2 2.3 %collective-permute-start.4 = (bf16[4,256,256]{2,1,0:T(8,128)(2,1)S(1)}, bf16[4,256,256]{2,1,0:T(8,128)(2,1)S(1)}, u32[]{:S(2)}, u32[]{:S(2)}) collective-permute-start(bf16[4,256,256]{2,1,0:T(8,128)(2,1)S(1)} %get-tuple-element.66), channel_id=1, source_target_pairs={{0,8},{1,9},{2,10},{3,11},{4,12},{5,13},{6,14},{7,15},{8,0},{9,1},... | collective-permute-start | bytes 1572872 | tf_op jit(solution)/shard_map/ppermute | solution.py:45
  26.9 31.4 %copy-start.2 = (bf16[256,1792]{1,0:T(8,128)(2,1)}, bf16[256,1792]{1,0:T(8,128)(2,1)S(1)}, u32[]{:S(2)}) copy-start(bf16[256,1792]{1,0:T(8,128)(2,1)S(1)} %collective-permute-done.1.refs_1_.refs_3_) | copy-start | bytes 2752516
  31.7 36.6 %collective-permute-start.5 = (bf16[512,2048]{1,0:T(8,128)(2,1)}, bf16[512,2048]{1,0:T(8,128)(2,1)}, u32[]{:S(2)}, u32[]{:S(2)}) collective-permute-start(bf16[512,2048]{1,0:T(8,128)(2,1)} %own_ref.3), channel_id=1, source_target_pairs={{0,2},{1,3},{2,0},{3,1},{4,6},{5,7},{6,4},{7,5},{8,14},{9,15},{10,... | collective-permute-start | bytes 6291464 | tf_op jit(solution)/shard_map/ppermute | solution.py:45
  34.4 24.0 %collective-permute-start.7 = (bf16[256,1792]{1,0:T(8,128)(2,1)S(1)}, bf16[256,1792]{1,0:T(8,128)(2,1)}, u32[]{:S(2)}, u32[]{:S(2)}) collective-permute-start(bf16[256,1792]{1,0:T(8,128)(2,1)S(1)} %collective-permute-done.1.refs_1_.refs_3_), channel_id=1, source_target_pairs={{0,1},{1,0},{2,3},{3,2},{4,5},{5,4},{6,7},{7,6},{8,9},{9,8},{10,11... | collective-permute-start | bytes 2752520 | tf_op jit(solution)/shard_map/ppermute | solution.py:45
  34.4 24.0 %collective-permute-start.6 = (bf16[256,1792]{1,0:T(8,128)(2,1)}, bf16[256,1792]{1,0:T(8,128)(2,1)}, u32[]{:S(2)}, u32[]{:S(2)}) collective-permute-start(bf16[256,1792]{1,0:T(8,128)(2,1)} %collective-permute-done.refs_2_.refs_4_), channel_id=1, source_target_pairs={{0,6},{1,7},{2,4},{3,5},{4,2},{5,3},{6,0},{7,1},{8,10},{9,11},{10,... | collective-permute-start | bytes 2752520 | tf_op jit(solution)/shard_map/ppermute | solution.py:45
  34.4 62.8 %collective-permute-start.12 = (bf16[512,1792]{1,0:T(8,128)(2,1)}, bf16[512,1792]{1,0:T(8,128)(2,1)}, u32[]{:S(2)}, u32[]{:S(2)}) collective-permute-start(bf16[512,1792]{1,0:T(8,128)(2,1)} %get-tuple-element.88), channel_id=1, source_target_pairs={{0,2},{1,3},{2,0},{3,1},{4,6},{5,7},{6,4},{7,5},{8,14},{9,15},{10,... | collective-permute-start | bytes 5505032 | tf_op jit(solution)/shard_map/ppermute | solution.py:45
  34.5 45.7 %collective-permute-start.9 = (bf16[256,1792]{1,0:T(8,128)(2,1)}, bf16[256,1792]{1,0:T(8,128)(2,1)}, u32[]{:S(2)}, u32[]{:S(2)}) collective-permute-start(bf16[256,1792]{1,0:T(8,128)(2,1)} %collective-permute-done.refs_2_.refs_4_), channel_id=1, source_target_pairs={{0,1},{1,0},{2,3},{3,2},{4,5},{5,4},{6,7},{7,6},{8,9},{9,8},{10,11... | collective-permute-start | bytes 2752520 | tf_op jit(solution)/shard_map/ppermute | solution.py:45
  58.4 38.8 %collective-permute-start.11 = (bf16[256,1792]{1,0:T(8,128)(2,1)}, bf16[256,1792]{1,0:T(8,128)(2,1)S(1)}, u32[]{:S(2)}, u32[]{:S(2)}) collective-permute-start(bf16[256,1792]{1,0:T(8,128)(2,1)} %collective-permute-done.6.refs_4_.refs_6_), channel_id=1, source_target_pairs={{0,1},{1,0},{2,3},{3,2},{4,5},{5,4},{6,7},{7,6},{8,9},{9,8},{10,11... | collective-permute-start | bytes 2752520 | tf_op jit(solution)/shard_map/ppermute | solution.py:45
  60.1 14.2 %collective-permute-start.8 = (bf16[4,256,256]{2,1,0:T(8,128)(2,1)}, bf16[4,256,256]{2,1,0:T(8,128)(2,1)}, u32[]{:S(2)}, u32[]{:S(2)}) collective-permute-start(bf16[4,256,256]{2,1,0:T(8,128)(2,1)} %get-tuple-element.79), channel_id=1, source_target_pairs={{0,16},{1,17},{2,18},{3,19},{4,20},{5,21},{6,22},{7,23},{8,24},{9,... | collective-permute-start | bytes 1572872 | tf_op jit(solution)/shard_map/ppermute | solution.py:45
  61.4 12.9 %copy-start.10 = (f32[4,256,256]{2,1,0:T(8,128)S(1)}, f32[4,256,256]{2,1,0:T(8,128)}, u32[]{:S(2)}) copy-start(f32[4,256,256]{2,1,0:T(8,128)} %copy-done.9) | copy-start | bytes 3145732
  61.4 12.9 %copy-start.16 = (s32[4]{0:T(128)S(1)}, s32[4]{0:T(128)}, u32[]{:S(2)}) copy-start(s32[4]{0:T(128)} %constant.107.clone.1.refs_0_) | copy-start | bytes 52
  77.5 14.6 %collective-permute-start.10 = (bf16[2,256,256]{2,1,0:T(8,128)(2,1)}, bf16[2,256,256]{2,1,0:T(8,128)(2,1)S(1)}, u32[]{:S(2)}, u32[]{:S(2)}) collective-permute-start(bf16[2,256,256]{2,1,0:T(8,128)(2,1)} %get-tuple-element.80), channel_id=1, source_target_pairs={{0,48},{1,49},{2,50},{3,51},{4,52},{5,53},{6,54},{7,55},{8,56},{9,... | collective-permute-start | bytes 786440 | tf_op jit(solution)/shard_map/ppermute | solution.py:45
  81.4 10.8 %copy-start.12 = (f32[2,256,256]{2,1,0:T(8,128)S(1)}, f32[2,256,256]{2,1,0:T(8,128)}, u32[]{:S(2)}) copy-start(f32[2,256,256]{2,1,0:T(8,128)} %copy-done.11) | copy-start | bytes 1572868
  81.4 15.8 %copy-start.6 = (bf16[512,1792]{1,0:T(8,128)(2,1)S(1)}, bf16[512,1792]{1,0:T(8,128)(2,1)}, u32[]{:S(2)}) copy-start(bf16[512,1792]{1,0:T(8,128)(2,1)} %copy-done.5) | copy-start | bytes 5505028
  81.4 15.8 %copy-start.15 = (f32[1,3584]{1,0:T(1,128)S(1)}, f32[1,3584]{1,0:T(1,128)}, u32[]{:S(2)}) copy-start(f32[1,3584]{1,0:T(1,128)} %gain_ref.3) | copy-start | bytes 43012
  92.9 9.2 %collective-permute-start.14 = (bf16[1,256,256]{2,1,0:T(8,128)(2,1)S(1)}, bf16[1,256,256]{2,1,0:T(8,128)(2,1)S(1)}, u32[]{:S(2)}, u32[]{:S(2)}) collective-permute-start(bf16[1,256,256]{2,1,0:T(8,128)(2,1)S(1)} %get-tuple-element.84), channel_id=1, source_target_pairs={{0,64},{1,65},{2,66},{3,67},{4,68},{5,69},{6,70},{7,71},{8,72},{9,... | collective-permute-start | bytes 393224 | tf_op jit(solution)/shard_map/ppermute | solution.py:45
  102.0 4.1 %collective-permute-start.13 = (f32[8,8,128]{2,1,0:T(8,128)S(1)}, f32[8,8,128]{2,1,0:T(8,128)S(1)}, u32[]{:S(2)}, u32[]{:S(2)}) collective-permute-start(f32[8,8,128]{2,1,0:T(8,128)S(1)} %row_stats.1.mine_ref), channel_id=1, source_target_pairs={{0,2},{1,3},{2,0},{3,1},{4,6},{5,7},{6,4},{7,5},{8,14},{9,15},{10,... | collective-permute-start | bytes 98312 | tf_op jit(solution)/shard_map/ppermute | solution.py:45
  112.9 24.4 %collective-permute-start.15 = (bf16[272,1792]{1,0:T(8,128)(2,1)S(1)}, bf16[272,1792]{1,0:T(8,128)(2,1)S(1)}, u32[]{:S(2)}, u32[]{:S(2)}) collective-permute-start(bf16[272,1792]{1,0:T(8,128)(2,1)S(1)} %get-tuple-element.98.refs_0_), channel_id=1, source_target_pairs={{0,1},{1,0},{2,3},{3,2},{4,5},{5,4},{6,7},{7,6},{8,9},{9,8},{10,11... | collective-permute-start | bytes 2924552 | tf_op jit(solution)/shard_map/ppermute | solution.py:45
  113.0 18.9 %collective-permute-start.16 = (bf16[256,1792]{1,0:T(8,128)(2,1)S(1)}, bf16[256,1792]{1,0:T(8,128)(2,1)S(1)}, u32[]{:S(2)}, u32[]{:S(2)}) collective-permute-start(bf16[256,1792]{1,0:T(8,128)(2,1)S(1)} %get-tuple-element.101), channel_id=1, source_target_pairs={{0,6},{1,7},{2,4},{3,5},{4,2},{5,3},{6,0},{7,1},{8,10},{9,11},{10,... | collective-permute-start | bytes 2752520 | tf_op jit(solution)/shard_map/ppermute | solution.py:45
  117.8 21.4 %collective-permute-start.20 = (bf16[256,2048]{1,0:T(8,128)(2,1)S(1)}, bf16[256,2048]{1,0:T(8,128)(2,1)S(1)}, u32[]{:S(2)}, u32[]{:S(2)}) collective-permute-start(bf16[256,2048]{1,0:T(8,128)(2,1)S(1)} %context_term.3), channel_id=1, source_target_pairs={{0,2},{1,3},{2,0},{3,1},{4,6},{5,7},{6,4},{7,5},{8,14},{9,15},{10,... | collective-permute-start | bytes 3145736 | tf_op jit(solution)/shard_map/ppermute | solution.py:45
  120.1 36.8 %collective-permute-start.19 = (bf16[256,1792]{1,0:T(8,128)(2,1)S(1)}, bf16[256,1792]{1,0:T(8,128)(2,1)S(1)}, u32[]{:S(2)}, u32[]{:S(2)}) collective-permute-start(bf16[256,1792]{1,0:T(8,128)(2,1)S(1)} %get-tuple-element.108), channel_id=1, source_target_pairs={{0,1},{1,0},{2,3},{3,2},{4,5},{5,4},{6,7},{7,6},{8,9},{9,8},{10,11... | collective-permute-start | bytes 2752520 | tf_op jit(solution)/shard_map/ppermute | solution.py:45
  137.5 9.4 %collective-permute-start.17 = (bf16[128,1792]{1,0:T(8,128)(2,1)S(1)}, bf16[128,1792]{1,0:T(8,128)(2,1)S(1)}, u32[]{:S(2)}, u32[]{:S(2)}) collective-permute-start(bf16[128,1792]{1,0:T(8,128)(2,1)S(1)} %get-tuple-element.103), channel_id=1, source_target_pairs={{0,6},{1,7},{2,4},{3,5},{4,2},{5,3},{6,0},{7,1},{8,10},{9,11},{10,... | collective-permute-start | bytes 1376264 | tf_op jit(solution)/shard_map/ppermute | solution.py:45
  137.6 24.1 %collective-permute-start.21 = (bf16[256,2048]{1,0:T(8,128)(2,1)S(1)}, bf16[256,2048]{1,0:T(8,128)(2,1)S(1)}, u32[]{:S(2)}, u32[]{:S(2)}) collective-permute-start(bf16[256,2048]{1,0:T(8,128)(2,1)S(1)} %context_term.4), channel_id=1, source_target_pairs={{0,2},{1,3},{2,0},{3,1},{4,6},{5,7},{6,4},{7,5},{8,14},{9,15},{10,... | collective-permute-start | bytes 3145736 | tf_op jit(solution)/shard_map/ppermute | solution.py:45
  137.7 20.2 %collective-permute-start.18 = (bf16[144,1792]{1,0:T(8,128)(2,1)S(1)}, bf16[144,1792]{1,0:T(8,128)(2,1)S(1)}, u32[]{:S(2)}, u32[]{:S(2)}) collective-permute-start(bf16[144,1792]{1,0:T(8,128)(2,1)S(1)} %get-tuple-element.106.refs_0_), channel_id=1, source_target_pairs={{0,6},{1,7},{2,4},{3,5},{4,2},{5,3},{6,0},{7,1},{8,10},{9,11},{10,... | collective-permute-start | bytes 1548296 | tf_op jit(solution)/shard_map/ppermute | solution.py:45
  139.2 46.4 %collective-permute-start.25 = (bf16[256,1792]{1,0:T(8,128)(2,1)S(1)}, bf16[256,1792]{1,0:T(8,128)(2,1)S(1)}, u32[]{:S(2)}, u32[]{:S(2)}) collective-permute-start(bf16[256,1792]{1,0:T(8,128)(2,1)S(1)} %add.137), channel_id=1, source_target_pairs={{0,1},{1,0},{2,3},{3,2},{4,5},{5,4},{6,7},{7,6},{8,9},{9,8},{10,11... | collective-permute-start | bytes 2752520 | tf_op jit(solution)/shard_map/ppermute | solution.py:45
  146.9 38.7 %collective-permute-start.24 = (bf16[256,1792]{1,0:T(8,128)(2,1)S(1)}, bf16[256,1792]{1,0:T(8,128)(2,1)S(1)}, u32[]{:S(2)}, u32[]{:S(2)}) collective-permute-start(bf16[256,1792]{1,0:T(8,128)(2,1)S(1)} %get-tuple-element.115), channel_id=1, source_target_pairs={{0,6},{1,7},{2,4},{3,5},{4,2},{5,3},{6,0},{7,1},{8,10},{9,11},{10,... | collective-permute-start | bytes 2752520 | tf_op jit(solution)/shard_map/ppermute | solution.py:45
  158.3 25.0 %collective-permute-start.23 = (bf16[144,1792]{1,0:T(8,128)(2,1)S(1)}, bf16[144,1792]{1,0:T(8,128)(2,1)S(1)}, u32[]{:S(2)}, u32[]{:S(2)}) collective-permute-start(bf16[144,1792]{1,0:T(8,128)(2,1)S(1)} %get-tuple-element.112.sent_ref), channel_id=1, source_target_pairs={{0,2},{1,3},{2,0},{3,1},{4,6},{5,7},{6,4},{7,5},{8,14},{9,15},{10,... | collective-permute-start | bytes 1548296 | tf_op jit(solution)/shard_map/ppermute | solution.py:45
  158.3 24.9 %collective-permute-start.22 = (bf16[128,1792]{1,0:T(8,128)(2,1)S(1)}, bf16[128,1792]{1,0:T(8,128)(2,1)S(1)}, u32[]{:S(2)}, u32[]{:S(2)}) collective-permute-start(bf16[128,1792]{1,0:T(8,128)(2,1)S(1)} %get-tuple-element.109), channel_id=1, source_target_pairs={{0,2},{1,3},{2,0},{3,1},{4,6},{5,7},{6,4},{7,5},{8,14},{9,15},{10,... | collective-permute-start | bytes 1376264 | tf_op jit(solution)/shard_map/ppermute | solution.py:45
  (13 other events, 36.7 us)

commit v3 on v2

--- a/solution.py
+++ b/solution.py
@@ -112,14 +112,14 @@
     )(which, array)
 
 
-def turn_kernel(at_ref, own_ref, partner_ref, out_ref, slab_ref):
-    for k in range(8):
-        at = pl.ds(pl.multiple_of(at_ref[k] * 256, 256), 256)
-        out_ref[k * 256 : (k + 1) * 256, :512] = jnp.transpose(own_ref[:, at])
-        out_ref[k * 256 : (k + 1) * 256, 512:] = jnp.transpose(partner_ref[:, at])
-    at = pl.ds(pl.multiple_of(at_ref[0] * 256, 256), 256)
-    slab_ref[:512] = own_ref[:, at]
-    slab_ref[512:] = partner_ref[:, at]
+def turn_kernel(at_ref, own_ref, high_ref, low_ref, out_ref, slab_ref):
+    pieces = ((own_ref, 0, 512), (high_ref, 512, 768), (low_ref, 768, 1024))
+    for ref, start, stop in pieces:
+        for k in range(8):
+            at = pl.ds(pl.multiple_of(at_ref[k] * 256, 256), 256)
+            out_ref[k * 256 : (k + 1) * 256, start:stop] = jnp.transpose(ref[:, at])
+        at = pl.ds(pl.multiple_of(at_ref[0] * 256, 256), 256)
+        slab_ref[start:stop] = ref[:, at]
 
 
 def turn(at, context, context_p):
@@ -128,9 +128,9 @@
         "turn", 4,
         [pltpu.VMEM((2048, 1024), BF16), pltpu.VMEM((1024, 256), BF16)],
         (1,),
+        [HELD, HELD, HELD],
         [HELD, HELD],
-        [HELD, HELD],
-    )(at, context, context_p)
+    )(at, context, *context_p)
 
 
 def outer_parts_kernel(at_ref, delta_ref, low_ref, high_ref, kept_ref):
@@ -180,7 +180,7 @@
 
     return call(
         kernel,
-        "outer_sum", 1,
+        "outer_sum", 4,
         [pltpu.VMEM((n, 256, WIDE), BF16), pltpu.VMEM((n, 256, WIDE), F32)],
         (1,),
         [HELD] * (1 + len(got)),
@@ -196,18 +196,19 @@
             k += 1
 
 
-def project_kernel(at_ref, own_ref, partner_ref, *refs):
+def project_kernel(at_ref, own_ref, high_ref, low_ref, *refs):
     *block_refs, out_ref = refs
+    pieces = ((own_ref, 0, 512), (high_ref, 512, 768), (low_ref, 768, 1024))
     for j in range(TILES):
         lanes = slice(j * TILE, (j + 1) * TILE)
-        for s, rows_ref in enumerate((own_ref, partner_ref)):
+        for rows_ref, start, stop in pieces:
             total = None
             for ref, row, at in slabs(at_ref, block_refs):
                 term = jnp.dot(
                     rows_ref[:, at], ref[row : row + 256, lanes], preferred_element_type=F32
                 )
                 total = term if total is None else total + term
-            out_ref[s * 512 : (s + 1) * 512, lanes] = total
+            out_ref[start:stop, lanes] = total
 
 
 def project(at, context, context_p, blocks):
@@ -216,20 +217,22 @@
         "project", 14,
         pltpu.VMEM((1024, HALF), F32),
         (1,),
-        [HELD] * (2 + len(blocks)),
+        [HELD] * (3 + len(blocks)),
         HELD,
-    )(at, context, context_p, *blocks)
+    )(at, context, *context_p, *blocks)
 
 
 def gain_lanes(at_ref, j):
     return pl.ds(pl.multiple_of(at_ref[8] * HALF + j * TILE, TILE), TILE)
 
 
-def stats_kernel(at_ref, acc_ref, slab_ref, block_ref, cot_ref, cot_p_ref, gain_ref, out_ref):
+def stats_kernel(
+    at_ref, acc_ref, slab_ref, block_ref, cot_ref, high_ref, low_ref, gain_ref, out_ref
+):
     for s in range(4):
         rows = slice(s * 256, (s + 1) * 256)
-        part = slice((s % 2) * 256, (s % 2 + 1) * 256)
-        c_ref = cot_ref if s < 2 else cot_p_ref
+        part = rows if s < 2 else slice(None)
+        c_ref = (cot_ref, cot_ref, high_ref, low_ref)[s]
         squares = jnp.zeros((256, 128), F32)
         products = jnp.zeros((256, 128), F32)
         for j in range(TILES):
@@ -254,9 +257,9 @@
         "row_stats", 3,
         pltpu.VMEM((8, 8, 128), F32),
         (1,),
-        [HELD] * 6,
+        [HELD] * 7,
         HELD,
-    )(at, acc, slab, block, cot, cot_p, gain)
+    )(at, acc, slab, block, cot, *cot_p, gain)
 
 
 def two_parts(value):
@@ -270,8 +273,8 @@
 
 
 def grad_kernel(
-    at_ref, acc_ref, slab_ref, block_ref, cot_ref, cot_p_ref, gain_ref, mine_ref, theirs_ref,
-    turned_ref,
+    at_ref, acc_ref, slab_ref, block_ref, cot_ref, high_ref, low_ref, gain_ref, mine_ref,
+    theirs_ref, turned_ref,
     g_ref, x_mate_ref, o_z_ref, a_ref, b_ref,
 ):
     for i in range(8):
@@ -289,8 +292,8 @@
         gain_total = jnp.zeros((8, TILE), F32)
         for i in range(4):
             rows = slice(i * 256, (i + 1) * 256)
-            part = slice((i % 2) * 256, (i % 2 + 1) * 256)
-            c_ref = cot_ref if i < 2 else cot_p_ref
+            part = rows if i < 2 else slice(None)
+            c_ref = (cot_ref, cot_ref, high_ref, low_ref)[i]
             p = acc_ref[rows, lanes] + jnp.dot(slab_ref[rows], block, preferred_element_type=F32)
             inverse = jnp.concatenate([a_ref[rows]] * 2, axis=1)
             coupling = jnp.concatenate([b_ref[rows]] * 2, axis=1)
@@ -314,10 +317,10 @@
             pltpu.VMEM((256, HALF), BF16),
         ),
         (1,),
-        [HELD] * 9,
+        [HELD] * 10,
         [HELD] * 3,
         [pltpu.VMEM((1024, 128), F32), pltpu.VMEM((1024, 128), F32)],
-    )(at, acc, slab, block, cot, cot_p, gain, mine, theirs, turned)
+    )(at, acc, slab, block, cot, *cot_p, gain, mine, theirs, turned)
 
 
 def weight_kernel(at_ref, turned_ref, g_ref, *out_refs, first):
@@ -439,55 +442,49 @@
     )(at, own, *got)
 
 
-def place_x_kernel(at_ref, high_ref, low_ref, sent_ref, out_ref, gain_ref):
-    step = pl.program_id(0)
-    rows = pl.ds(pl.multiple_of((step % 2) * 64, 64), 64)
-
-    @pl.when(step < 2)
-    def _():
-        out_ref[...] = high_ref[rows, :].astype(F32)
-
-    @pl.when(step >= 2)
-    def _():
-        out_ref[...] = low_ref[rows, :].astype(F32)
-
-    @pl.when(step == 0)
-    def _():
-        own = pl.ds(pl.multiple_of(at_ref[8] * HALF, 256), HALF)
-        other = pl.ds(pl.multiple_of((1 - at_ref[8]) * HALF, 256), HALF)
-        gain_ref[:, own] = one_value(sent_ref[128:])
-        gain_ref[:, other] = one_value(low_ref[128:])
-
-
-def place_x(at, high, low, sent):
-    return call(
-        place_x_kernel,
-        "place_x", 2,
+def finish_kernel(
+    at_ref, high_ref, low_ref, sent_ref, o_ref, o_mate_ref, o_z_ref,
+    out_ref, gain_ref, own_stage, other_stage, sems,
+):
+    own = pl.ds(pl.multiple_of(at_ref[8] * HALF, 256), HALF)
+    other = pl.ds(pl.multiple_of((1 - at_ref[8]) * HALF, 256), HALF)
+    copies = []
+    for i in range(4):
+        rows = slice(i * 64, (i + 1) * 64)
+        x_ref, part = (high_ref, rows) if i < 2 else (low_ref, slice(i * 64 - 128, i * 64 - 64))
+        other_stage[rows] = x_ref[part].astype(F32)
+        own_stage[rows] = (
+            o_ref[rows] + o_mate_ref[rows].astype(F32) + o_z_ref[rows].astype(F32)
+        )
+        for s, (stage, lanes) in enumerate(((other_stage, other), (own_stage, own))):
+            part = pl.ds(i * 64, 64)
+            copies.append(
+                pltpu.make_async_copy(stage.at[part], out_ref.at[part, lanes], sems.at[s, i])
+            )
+            copies[-1].start()
+    gain_ref[:, own] = one_value(sent_ref[128:])
+    gain_ref[:, other] = one_value(low_ref[128:])
+    for copy in copies:
+        copy.wait()
+
+
+def finish(at, high, low, sent, o, o_mate, o_z):
+    return call(
+        finish_kernel,
+        "finish", 2,
         [jax.ShapeDtypeStruct((256, 2 * HALF), F32), jax.ShapeDtypeStruct((1, 2 * HALF), F32)],
-        (4,),
-        [HELD, HELD, HELD],
+        (1,),
+        [HELD] * 6,
         [
-            pl.BlockSpec((64, HALF), lambda i, at: (i, 1 - at[8])),
+            pl.BlockSpec(memory_space=pl.ANY),
             pl.BlockSpec((1, 2 * HALF), lambda i, at: (0, 0)),
         ],
-    )(at, high, low, sent)
-
-
-def place_o_kernel(at_ref, out_in_ref, a_ref, b_ref, c_ref, out_ref):
-    rows = pl.ds(pl.multiple_of(pl.program_id(0) * 64, 64), 64)
-    out_ref[...] = a_ref[rows, :] + b_ref[rows, :].astype(F32) + c_ref[rows, :].astype(F32)
-
-
-def place_o(at, out, a, b, c):
-    return call(
-        place_o_kernel,
-        "place_o", 2,
-        jax.ShapeDtypeStruct((256, 2 * HALF), F32),
-        (4,),
-        [pl.BlockSpec(memory_space=pl.ANY), HELD, HELD, HELD],
-        pl.BlockSpec((64, HALF), lambda i, at: (i, at[8])),
-        aliases={1: 0},
-    )(at, out, a, b, c)
+        [
+            pltpu.VMEM((256, HALF), F32),
+            pltpu.VMEM((256, HALF), F32),
+            pltpu.SemaphoreType.DMA((2, 4)),
+        ],
+    )(at, high, low, sent, o, o_mate, o_z)
 
 
 def per_device(context, cotangent, weight, gain, delta, anchor, momentum):
@@ -551,32 +548,28 @@
     from_partner = after(from_partner, from_mate)
     from_opposite = send(from_partner, TO_MATE)
     partner_z = send(from_partner, TO_Z)
-    context_p = send(after(context, from_partner), TO_PARTNER)
-    cot_p = send(after(cot_away, from_partner), TO_PARTNER)
-    x1_away, x1_kept = outer_sum(x1_at, after(core_kept, from_partner), *core_got)
-    from_opposite = after(from_opposite, mate_z, x1_away)
+    context_p = [
+        send(after(context[:256], core_high), TO_PARTNER),
+        send(after(context[256:], core_high), TO_PARTNER),
+    ]
+    x1_away, x1_kept = outer_sum(x1_at, after(core_kept, from_partner, mate_z), *core_got)
+    from_opposite = after(from_opposite, mate_z, x1_away, context_p[0])
 
     x1_got = send(after(x1_away, from_opposite), TO_X1)
     opposite_z = send(from_opposite, TO_Z)
+    cot_p = [
+        send(after(cot_away[:256], from_opposite), TO_PARTNER),
+        send(after(cot_away[256:], from_opposite), TO_PARTNER),
+    ]
 
     turned, slab = turn(turn_order, context, context_p)
-    x3_away, x3_kept = outer_sum(x3_at, after(x1_kept, turned), x1_got)
-    x3_got = send(x3_away, TO_X3)
     blocks = [own, from_mate, from_partner, own_z, from_opposite, mate_z, partner_z, opposite_z]
-    acc = project(at, context, after(context_p, turned, x3_away), blocks[:-1])
-    zlo_away, zlo_kept = outer_sum(zlo_at, after(x3_kept, acc), x3_got, turned=True)
-    zlo_got = send(zlo_away, TO_ZLO)
-
-    last = (at, after(acc, zlo_away), slab, opposite_z, cot, cot_p, gain)
+    acc = project(at, after(context, turned), context_p, blocks[:-1])
+    last = (at, acc, slab, opposite_z, cot, cot_p, gain)
     mine = row_stats(*last)
     theirs = send(mine, TO_PARTNER)
-
-    outer_grad = (after(zlo_kept, mine)[0, :COLS] + zlo_got[0, :COLS].astype(F32)) / 16
-    new_momentum = 0.9 * momentum.T + outer_grad
-    new_anchor = anchor.T - 0.7 * (outer_grad + 0.9 * new_momentum)
-    new_momentum, new_anchor = new_momentum.T, new_anchor.T
-
-    theirs = after(theirs, new_anchor, new_momentum)
+    x3_away, x3_kept = outer_sum(x3_at, after(x1_kept, mine), x1_got)
+    theirs = after(theirs, x3_away)
     g, x_mate_away, o_mate_z = grad_step(*last, mine, theirs, turned)
 
     x_mate_z = send(x_mate_away, TO_Z)
@@ -596,16 +589,29 @@
     x_from_mate = [send(piece, TO_MATE) for piece in x_mate]
     o_self_z = add(which, after(o_self_z_own, x_mate[0]), o_mate_z)
     o_from_z = send(o_self_z, TO_Z)
-    own_context = context_term(at, after(g, o_self_z), 0, blocks, F32, 2)
+    x3_got = send(x3_away, TO_X3)
+    zlo_away, zlo_kept = outer_sum(zlo_at, after(x3_kept, o_self_z), x3_got, turned=True)
+    zlo_got = send(zlo_away, TO_ZLO)
+    own_context = context_term(at, after(g, zlo_away), 0, blocks, F32, 2)
     o_mate = send(after(o_mate, x_mate[0], got_high), TO_MATE)
 
     x_self = add_x(
-        which, x_self_own, x_mate[1], after(x_from_mate[0], own_context), x_from_mate[1], x_self_z
+        which,
+        x_self_own,
+        x_mate[1],
+        after(x_from_mate[0], own_context),
+        x_from_mate[1],
+        x_self_z,
     )
     x_got = [send(piece, TO_PARTNER) for piece in x_self]
     grad_context = end_context(which, after(own_context, x_self[0]), got_high, got_low)
-    grad_weight, grad_gain = place_x(at, after(x_got[0], grad_context), x_got[1], x_self[1])
-    grad_weight = place_o(at, grad_weight, o_self_own, o_mate, o_from_z)
+    outer_grad = (after(zlo_kept, grad_context)[0, :COLS] + zlo_got[0, :COLS].astype(F32)) / 16
+    new_momentum = 0.9 * momentum.T + outer_grad
+    new_anchor = anchor.T - 0.7 * (outer_grad + 0.9 * new_momentum)
+    new_momentum, new_anchor = new_momentum.T, new_anchor.T
+    grad_weight, grad_gain = finish(
+        at, after(x_got[0], new_anchor, new_momentum), x_got[1], x_self[1], o_self_own, o_mate, o_from_z
+    )
     return (grad_context, grad_weight[None], grad_gain, new_anchor, new_momentum)
 
 

time: 188 us -> 183 us (0.973); the launches traced: 188 us -> 181 us
  waiting for transfers between devices: 74.7 us -> 50.1 us
  starting transfers between devices: 31.1 us -> 39.1 us
  local copies, waits for them, and re-layouts: 11.3 us -> 19 us
    ppermute x26 -> x28, waiting for transfers between devices: 74.7 us -> 50.1 us  [send(): return lax.ppermute(value, BOTH, pairs)]
    ppermute x26 -> x28, starting transfers between devices: 31.1 us -> 39.1 us  [send(): return lax.ppermute(value, BOTH, pairs)]
    slice x0 -> x2, local copies, waits for them, and re-layouts: none -> 4.38 us  [the longest x1 2.94 us: per_device(): cot_away[256:]]
    unnamed x38 -> x74, local copies, waits for them, and re-layouts: 11 us -> 14.4 us
    pallas_call x21 -> x20, Pallas kernels: 68.9 us -> 70.5 us  [run(): return built(at, *placed)]
  transfers between devices with their start and end apart: 26 -> 28, of which waited for: 14 -> 13; matrix products, arithmetic and copies ran while one was open for 1% -> 3% of each run, Pallas kernels for 31% -> 32%
where the time goes in v3:
time: 183 us; the launch traced here: 181 us
  Pallas kernels  70.5 us (39%)
  waiting for transfers between devices  50.1 us (27%)
  starting transfers between devices  39.1 us (21%)
  local copies, waits for them, and re-layouts  19 us (10%)
    pallas_call x20, Pallas kernels, run(): return built(at, *placed)  70.5 us
    ppermute x28, waiting for transfers between devices, send(): return lax.ppermute(value, BOTH, pairs)  50.1 us
    ppermute x28, starting transfers between devices, send(): return lax.ppermute(value, BOTH, pairs)  39.1 us
    unnamed x74, local copies, waits for them, and re-layouts  14.4 us
  transfers between devices with their start and end apart: 28, of which 13 were waited for; matrix products, arithmetic and copies ran while one was open for 3% of the time, Pallas kernels for 32%

profile of v3, /device:TPU:1, one launch (start us, length us, event | category | flops | bytes accessed | tf_op | source)
XLA Modules:
  0.0 180.8 jit_solution(17608637474473445415)
XLA Ops:
  2.4 4.5 %collective-permute-start.3 = (bf16[256,1792]{1,0:T(8,128)(2,1)S(1)}, bf16[256,1792]{1,0:T(8,128)(2,1)S(1)}, u32[]{:S(2)}, u32[]{:S(2)}) collective-permute-start(bf16[256,1792]{1,0:T(8,128)(2,1)S(1)} %get-tuple-element.62.refs_0_.refs_2_), channel_id=1, source_target_pairs={{0,1},{1,0},{2,3},{3,2},{4,5},{5,4},{6,7},{7,6},{8,9},{9,8},{10,11... | collective-permute-start | bytes 2752520 | tf_op jit(solution)/shard_map/ppermute | solution.py:45
  8.2 2.1 %split.3 = (bf16[512,1792]{1,0:T(8,128)(2,1)S(1)}, bf16[512,1792]{1,0:T(8,128)(2,1)S(1)}) custom-call(s32[1]{0:T(128)} %bitcast.at_ref.refs_0_, bf16[512,3584]{1,0:T(8,128)(2,1)} %in_ref), custom_call_target="tpu_custom_call" | custom-call | bytes 6000000 | tf_op jit(solution)/shard_map/split/pallas_call | solution.py:82
  12.8 3.5 %outer_parts.1 = (bf16[4,256,256]{2,1,0:T(8,128)(2,1)S(1)}, bf16[4,256,256]{2,1,0:T(8,128)(2,1)S(1)}, f32[8,256,256]{2,1,0:T(8,128)S(1)}) custom-call(s32[1]{0:T(128)} %bitcast.9.at_ref, f32[256,3584]{1,0:T(8,128)} %bitcast.48), custom_call_target="tpu_custom_call" | custom-call | bytes 9000000 | tf_op jit(solution)/shard_map/outer_parts/pallas_call | solution.py:82
  17.7 1.9 %collective-permute-start.6 = (bf16[256,1792]{1,0:T(8,128)(2,1)S(1)}, bf16[256,1792]{1,0:T(8,128)(2,1)}, u32[]{:S(2)}, u32[]{:S(2)}) collective-permute-start(bf16[256,1792]{1,0:T(8,128)(2,1)S(1)} %get-tuple-element.74), channel_id=1, source_target_pairs={{0,2},{1,3},{2,0},{3,1},{4,6},{5,7},{6,4},{7,5},{8,14},{9,15},{10,... | collective-permute-start | bytes 2752520 | tf_op jit(solution)/shard_map/ppermute | solution.py:45
  24.3 2.7 %collective-permute-done.3.refs_3_.refs_5_ = bf16[256,1792]{1,0:T(8,128)(2,1)S(1)} collective-permute-done((bf16[256,1792]{1,0:T(8,128)(2,1)S(1)}, bf16[256,1792]{1,0:T(8,128)(2,1)S(1)}, u32[]{:S(2)}, u32[]{:S(2)}) %collective-permute-start.3) | collective-permute-done | bytes 917536 | tf_op jit(solution)/shard_map/ppermute | solution.py:45
  27.9 2.6 %collective-permute-start.8 = (bf16[256,1792]{1,0:T(8,128)(2,1)S(1)}, bf16[256,1792]{1,0:T(8,128)(2,1)}, u32[]{:S(2)}, u32[]{:S(2)}) collective-permute-start(bf16[256,1792]{1,0:T(8,128)(2,1)S(1)} %collective-permute-done.2.refs_1_.refs_3_), channel_id=1, source_target_pairs={{0,1},{1,0},{2,3},{3,2},{4,5},{5,4},{6,7},{7,6},{8,9},{9,8},{10,11... | collective-permute-start | bytes 2752520 | tf_op jit(solution)/shard_map/ppermute | solution.py:45
  32.1 2.4 %collective-permute-start.1 = (bf16[256,2048]{1,0:T(8,128)(2,1)}, bf16[256,2048]{1,0:T(8,128)(2,1)}, u32[]{:S(2)}, u32[]{:S(2)}) collective-permute-start(bf16[256,2048]{1,0:T(8,128)(2,1)} %get-tuple-element.66), channel_id=1, source_target_pairs={{0,2},{1,3},{2,0},{3,1},{4,6},{5,7},{6,4},{7,5},{8,14},{9,15},{10,... | collective-permute-start | bytes 3145736 | tf_op jit(solution)/shard_map/ppermute | solution.py:45
  34.5 2.9 %fusion.5 = (bf16[256,1792]{1,0:T(8,128)(2,1)}, bf16[256,1792]{1,0:T(8,128)(2,1)}) fusion(bf16[512,1792]{1,0:T(8,128)(2,1)} %copy-done.18), kind=kLoop, calls=%fused_computation.9 | loop fusion | bytes 3670016 | tf_op jit(solution)/shard_map/slice | solution.py:562
  37.5 12.7 %collective-permute-done.8.refs_5_.refs_7_ = bf16[256,1792]{1,0:T(8,128)(2,1)} collective-permute-done((bf16[256,1792]{1,0:T(8,128)(2,1)S(1)}, bf16[256,1792]{1,0:T(8,128)(2,1)}, u32[]{:S(2)}, u32[]{:S(2)}) %collective-permute-start.8) | collective-permute-done | bytes 917536 | tf_op jit(solution)/shard_map/ppermute | solution.py:45
  55.0 2.7 %collective-permute-start.11 = (bf16[256,1792]{1,0:T(8,128)(2,1)}, bf16[256,1792]{1,0:T(8,128)(2,1)}, u32[]{:S(2)}, u32[]{:S(2)}) collective-permute-start(bf16[256,1792]{1,0:T(8,128)(2,1)} %get-tuple-element.82), channel_id=1, source_target_pairs={{0,2},{1,3},{2,0},{3,1},{4,6},{5,7},{6,4},{7,5},{8,14},{9,15},{10,... | collective-permute-start | bytes 2752520 | tf_op jit(solution)/shard_map/ppermute | solution.py:45
  57.7 6.5 %collective-permute-done.1.low_ref = bf16[256,2048]{1,0:T(8,128)(2,1)} collective-permute-done((bf16[256,2048]{1,0:T(8,128)(2,1)}, bf16[256,2048]{1,0:T(8,128)(2,1)}, u32[]{:S(2)}, u32[]{:S(2)}) %collective-permute-start.1) | collective-permute-done | bytes 1048608 | tf_op jit(solution)/shard_map/ppermute | solution.py:45
  65.7 3.6 %turn.1 = (bf16[2048,1024]{1,0:T(8,128)(2,1)S(1)}, bf16[1024,256]{1,0:T(8,128)(2,1)S(1)}) custom-call(s32[8]{0:T(128)S(1)} %stack.91.at_ref, bf16[512,2048]{1,0:T(8,128)(2,1)S(1)} %copy-done.2, bf16[256,2048]{1,0:T(8,128)(2,1)} %collective-permute-done.high_ref, bf16[256,2048]{1,0:T(8,128)(2,1)} %collective-permute-done.1.low_ref), custom_call_target="tpu_custom_call" | custom-call | bytes 12000000 | tf_op jit(solution)/shard_map/turn/pallas_call | solution.py:82
  69.8 10.1 %project.1.acc_ref = f32[1024,1792]{1,0:T(8,128)S(1)} custom-call(s32[9]{0:T(128)S(1)} %stack.90.at_ref.refs_0_, bf16[512,2048]{1,0:T(8,128)(2,1)S(1)} %copy-done.2, bf16[256,2048]{1,0:T(8,128)(2,1)} %collective-permute-done.high_ref, bf16[256,2048]{1,0:T(8,128)(2,1)} %collective-permute-done.1.low_ref, bf16[256,1792]{1,0:T(8,128)(2,1)S(1)} %copy-done.4, ...), custom_call_target="tpu_custom_call" | custom-call | bytes 42000000 | tf_op jit(solution)/shard_map/project/pallas_call | solution.py:82
  79.9 9.4 %collective-permute-done.10.block_ref.refs_9_ = bf16[256,1792]{1,0:T(8,128)(2,1)S(1)} collective-permute-done((bf16[256,1792]{1,0:T(8,128)(2,1)}, bf16[256,1792]{1,0:T(8,128)(2,1)S(1)}, u32[]{:S(2)}, u32[]{:S(2)}) %collective-permute-start.10) | collective-permute-done | bytes 917536 | tf_op jit(solution)/shard_map/ppermute | solution.py:45
  89.4 4.1 %row_stats.1.mine_ref = f32[8,8,128]{2,1,0:T(8,128)S(1)} custom-call(s32[9]{0:T(128)S(1)} %stack.90.at_ref.refs_0_, f32[1024,1792]{1,0:T(8,128)S(1)} %project.1.acc_ref, bf16[1024,256]{1,0:T(8,128)(2,1)S(1)} %get-tuple-element.80.slab_ref, bf16[256,1792]{1,0:T(8,128)(2,1)S(1)} %collective-permute-done.10.block_ref.refs_9_, bf16[512,1792]{1,0:T(8,128)(2,1)S(1)} %copy-done.13, ...), custom_call_target="tpu_custom_call" | custom-call | bytes 9000000 | tf_op jit(solution)/shard_map/row_stats/pallas_call | solution.py:82
  93.5 3.0 %collective-permute-start.13 = (f32[8,8,128]{2,1,0:T(8,128)S(1)}, f32[8,8,128]{2,1,0:T(8,128)S(1)}, u32[]{:S(2)}, u32[]{:S(2)}) collective-permute-start(f32[8,8,128]{2,1,0:T(8,128)S(1)} %row_stats.1.mine_ref), channel_id=1, source_target_pairs={{0,2},{1,3},{2,0},{3,1},{4,6},{5,7},{6,4},{7,5},{8,14},{9,15},{10,... | collective-permute-start | bytes 98312 | tf_op jit(solution)/shard_map/ppermute | solution.py:45
  98.0 6.1 %grad_step.1 = (bf16[1024,1792]{1,0:T(8,128)(2,1)S(1)}, bf16[272,1792]{1,0:T(8,128)(2,1)S(1)}, bf16[256,1792]{1,0:T(8,128)(2,1)S(1)}) custom-call(s32[9]{0:T(128)S(1)} %stack.90.at_ref.refs_0_, f32[1024,1792]{1,0:T(8,128)S(1)} %project.1.acc_ref, bf16[1024,256]{1,0:T(8,128)(2,1)S(1)} %get-tuple-element.80.slab_ref, ...), custom_call_target="tpu_custom_call" | custom-call | bytes 18000000 | tf_op jit(solution)/shard_map/grad_step/pallas_call | solution.py:82
  104.1 2.4 %collective-permute-start.15 = (bf16[272,1792]{1,0:T(8,128)(2,1)S(1)}, bf16[272,1792]{1,0:T(8,128)(2,1)S(1)}, u32[]{:S(2)}, u32[]{:S(2)}) collective-permute-start(bf16[272,1792]{1,0:T(8,128)(2,1)S(1)} %get-tuple-element.96.refs_0_), channel_id=1, source_target_pairs={{0,1},{1,0},{2,3},{3,2},{4,5},{5,4},{6,7},{7,6},{8,9},{9,8},{10,11... | collective-permute-start | bytes 2924552 | tf_op jit(solution)/shard_map/ppermute | solution.py:45
  106.5 4.7 %context_term.3 = bf16[256,2048]{1,0:T(8,128)(2,1)S(1)} custom-call(s32[9]{0:T(128)S(1)} %stack.90.at_ref.refs_0_, bf16[1024,1792]{1,0:T(8,128)(2,1)S(1)} %get-tuple-element.105.refs_1_.refs_2_, bf16[256,1792]{1,0:T(8,128)(2,1)S(1)} %copy-done.4, bf16[256,1792]{1,0:T(8,128)(2,1)S(1)} %copy-done.10, bf16[256,1792]{1,0:T(8,128)(2,1)} %collective-permute-done.6.refs_2_.refs_4_, ...), custom_call_target="tpu_custom_call" | custom-call | bytes 7500000 | tf_op jit(solution)/shard_map/context_term/pallas_call | solution.py:82
  111.2 2.6 %collective-permute-start.21 = (bf16[256,2048]{1,0:T(8,128)(2,1)S(1)}, bf16[256,2048]{1,0:T(8,128)(2,1)S(1)}, u32[]{:S(2)}, u32[]{:S(2)}) collective-permute-start(bf16[256,2048]{1,0:T(8,128)(2,1)S(1)} %context_term.3), channel_id=1, source_target_pairs={{0,2},{1,3},{2,0},{3,1},{4,6},{5,7},{6,4},{7,5},{8,14},{9,15},{10,... | collective-permute-start | bytes 3145736 | tf_op jit(solution)/shard_map/ppermute | solution.py:45
  113.8 3.2 %weight_terms.2 = (bf16[256,1792]{1,0:T(8,128)(2,1)}, bf16[256,1792]{1,0:T(8,128)(2,1)}) custom-call(s32[1]{0:T(128)} %bitcast.at_ref.refs_0_, bf16[2048,1024]{1,0:T(8,128)(2,1)S(1)} %get-tuple-element.67.turned_ref.refs_1_, bf16[1024,1792]{1,0:T(8,128)(2,1)S(1)} %get-tuple-element.105.refs_1_.refs_2_), custom_call_target="tpu_custom_call" | custom-call | bytes 6000000 | tf_op jit(solution)/shard_map/weight_terms/pallas_call | solution.py:82
  117.0 4.0 %weight_terms.3 = (f32[256,1792]{1,0:T(8,128)S(1)}, f32[256,1792]{1,0:T(8,128)S(1)}, f32[256,1792]{1,0:T(8,128)S(1)}, f32[256,1792]{1,0:T(8,128)S(1)}) custom-call(s32[1]{0:T(128)} %bitcast.at_ref.refs_0_, bf16[2048,1024]{1,0:T(8,128)(2,1)S(1)} %get-tuple-element.67.turned_ref.refs_1_, bf16[1024,1792]{1,0:T(8,128)(2,1)S(1)} %get-tuple-element.105.refs_1_.refs_2_), custom_call_target="tpu_custom_call" | custom-call | bytes 12000000 | tf_op jit(solution)/shard_map/weight_terms/pallas_call | solution.py:82
  122.2 5.8 %context_term.4 = bf16[256,2048]{1,0:T(8,128)(2,1)} custom-call(s32[9]{0:T(128)S(1)} %stack.90.at_ref.refs_0_, bf16[1024,1792]{1,0:T(8,128)(2,1)S(1)} %get-tuple-element.105.refs_1_.refs_2_, bf16[256,1792]{1,0:T(8,128)(2,1)S(1)} %copy-done.4, bf16[256,1792]{1,0:T(8,128)(2,1)S(1)} %copy-done.10, bf16[256,1792]{1,0:T(8,128)(2,1)} %collective-permute-done.6.refs_2_.refs_4_, ...), custom_call_target="tpu_custom_call" | custom-call | bytes 7500000 | tf_op jit(solution)/shard_map/context_term/pallas_call | solution.py:82
  130.5 2.5 %collective-permute-start.17 = (bf16[2,256,256]{2,1,0:T(8,128)(2,1)S(1)}, bf16[2,256,256]{2,1,0:T(8,128)(2,1)S(1)}, u32[]{:S(2)}, u32[]{:S(2)}) collective-permute-start(bf16[2,256,256]{2,1,0:T(8,128)(2,1)S(1)} %get-tuple-element.87), channel_id=1, source_target_pairs={{0,48},{1,49},{2,50},{3,51},{4,52},{5,53},{6,54},{7,55},{8,56},{9,... | collective-permute-start | bytes 786440 | tf_op jit(solution)/shard_map/ppermute | solution.py:45
  137.6 2.6 %collective-permute-start.27 = (bf16[256,1792]{1,0:T(8,128)(2,1)}, bf16[256,1792]{1,0:T(8,128)(2,1)}, u32[]{:S(2)}, u32[]{:S(2)}) collective-permute-start(bf16[256,1792]{1,0:T(8,128)(2,1)} %add.137), channel_id=1, source_target_pairs={{0,1},{1,0},{2,3},{3,2},{4,5},{5,4},{6,7},{7,6},{8,9},{9,8},{10,11... | collective-permute-start | bytes 2752520 | tf_op jit(solution)/shard_map/ppermute | solution.py:45
  143.5 2.0 %copy-done.1 = bf16[1024,1792]{1,0:T(8,128)(2,1)S(1)} copy-done((bf16[1024,1792]{1,0:T(8,128)(2,1)S(1)}, bf16[1024,1792]{1,0:T(8,128)(2,1)}, u32[]{:S(2)}) %copy-start.1) | copy-done | bytes 3670040
  146.7 6.9 %context_term.5.a_ref = f32[512,2048]{1,0:T(8,128)S(1)} custom-call(s32[9]{0:T(128)S(1)} %stack.90.at_ref.refs_0_, bf16[1024,1792]{1,0:T(8,128)(2,1)S(1)} %copy-done.1, bf16[256,1792]{1,0:T(8,128)(2,1)S(1)} %copy-done.5, bf16[256,1792]{1,0:T(8,128)(2,1)S(1)} %copy-done.11, bf16[256,1792]{1,0:T(8,128)(2,1)} %collective-permute-done.6.refs_2_.refs_4_, ...), custom_call_target="tpu_custom_call" | custom-call | bytes 15000000 | tf_op jit(solution)/shard_map/context_term/pallas_call | solution.py:82
  155.5 3.7 %collective-permute-start.25 = (bf16[144,1792]{1,0:T(8,128)(2,1)S(1)}, bf16[144,1792]{1,0:T(8,128)(2,1)S(1)}, u32[]{:S(2)}, u32[]{:S(2)}) collective-permute-start(bf16[144,1792]{1,0:T(8,128)(2,1)S(1)} %get-tuple-element.114.sent_ref), channel_id=1, source_target_pairs={{0,2},{1,3},{2,0},{3,1},{4,6},{5,7},{6,4},{7,5},{8,14},{9,15},{10,... | collective-permute-start | bytes 1548296 | tf_op jit(solution)/shard_map/ppermute | solution.py:45
  160.1 3.3 %end_context.1 = bf16[512,2048]{1,0:T(8,128)(2,1)} custom-call(s32[1]{0:T(128)} %bitcast.at_ref.refs_0_, f32[512,2048]{1,0:T(8,128)S(1)} %context_term.5.a_ref, bf16[256,2048]{1,0:T(8,128)(2,1)S(1)} %copy-done.22, bf16[256,2048]{1,0:T(8,128)(2,1)} %collective-permute-done.22.c_ref), custom_call_target="tpu_custom_call" | custom-call | bytes 6000000 | tf_op jit(solution)/shard_map/end_context/pallas_call | solution.py:82
  163.5 4.7 %collective-permute-done.24 = bf16[1,256,256]{2,1,0:T(8,128)(2,1)S(1)} collective-permute-done((bf16[1,256,256]{2,1,0:T(8,128)(2,1)S(1)}, bf16[1,256,256]{2,1,0:T(8,128)(2,1)S(1)}, u32[]{:S(2)}, u32[]{:S(2)}) %collective-permute-start.24) | collective-permute-done | bytes 131104 | tf_op jit(solution)/shard_map/ppermute | solution.py:45
  169.1 7.1 %collective-permute-done.23.high_ref = bf16[128,1792]{1,0:T(8,128)(2,1)S(1)} collective-permute-done((bf16[128,1792]{1,0:T(8,128)(2,1)S(1)}, bf16[128,1792]{1,0:T(8,128)(2,1)S(1)}, u32[]{:S(2)}, u32[]{:S(2)}) %collective-permute-start.23) | collective-permute-done | bytes 458784 | tf_op jit(solution)/shard_map/ppermute | solution.py:45
  176.1 4.5 %finish.1 = (f32[256,3584]{1,0:T(8,128)}, f32[1,3584]{1,0:T(1,128)}) custom-call(s32[9]{0:T(128)S(1)} %stack.90.at_ref.refs_0_, bf16[128,1792]{1,0:T(8,128)(2,1)S(1)} %collective-permute-done.23.high_ref, bf16[144,1792]{1,0:T(8,128)(2,1)S(1)} %collective-permute-done.25.low_ref, bf16[144,1792]{1,0:T(8,128)(2,1)S(1)} %get-tuple-element.114.sent_ref, ...), custom_call_target="tpu_custom_call" | custom-call | bytes 6000000 | tf_op jit(solution)/shard_map/finish/pallas_call | solution.py:82
  (125 shorter events, 38.7 us)
Async XLA Ops:
  2.4 24.6 %collective-permute-start.3 = (bf16[256,1792]{1,0:T(8,128)(2,1)S(1)}, bf16[256,1792]{1,0:T(8,128)(2,1)S(1)}, u32[]{:S(2)}, u32[]{:S(2)}) collective-permute-start(bf16[256,1792]{1,0:T(8,128)(2,1)S(1)} %get-tuple-element.62.refs_0_.refs_2_), channel_id=1, source_target_pairs={{0,1},{1,0},{2,3},{3,2},{4,5},{5,4},{6,7},{7,6},{8,9},{9,8},{10,11... | collective-permute-start | bytes 2752520 | tf_op jit(solution)/shard_map/ppermute | solution.py:45
  6.9 21.0 %collective-permute-start.2 = (bf16[256,1792]{1,0:T(8,128)(2,1)S(1)}, bf16[256,1792]{1,0:T(8,128)(2,1)S(1)}, u32[]{:S(2)}, u32[]{:S(2)}) collective-permute-start(bf16[256,1792]{1,0:T(8,128)(2,1)S(1)} %get-tuple-element.62.refs_0_.refs_2_), channel_id=1, source_target_pairs={{0,6},{1,7},{2,4},{3,5},{4,2},{5,3},{6,0},{7,1},{8,10},{9,11},{10,... | collective-permute-start | bytes 2752520 | tf_op jit(solution)/shard_map/ppermute | solution.py:45
  17.7 14.0 %collective-permute-start.6 = (bf16[256,1792]{1,0:T(8,128)(2,1)S(1)}, bf16[256,1792]{1,0:T(8,128)(2,1)}, u32[]{:S(2)}, u32[]{:S(2)}) collective-permute-start(bf16[256,1792]{1,0:T(8,128)(2,1)S(1)} %get-tuple-element.74), channel_id=1, source_target_pairs={{0,2},{1,3},{2,0},{3,1},{4,6},{5,7},{6,4},{7,5},{8,14},{9,15},{10,... | collective-permute-start | bytes 2752520 | tf_op jit(solution)/shard_map/ppermute | solution.py:45
  19.6 4.7 %collective-permute-start.5 = (bf16[4,256,256]{2,1,0:T(8,128)(2,1)S(1)}, bf16[4,256,256]{2,1,0:T(8,128)(2,1)S(1)}, u32[]{:S(2)}, u32[]{:S(2)}) collective-permute-start(bf16[4,256,256]{2,1,0:T(8,128)(2,1)S(1)} %get-tuple-element.64), channel_id=1, source_target_pairs={{0,8},{1,9},{2,10},{3,11},{4,12},{5,13},{6,14},{7,15},{8,0},{9,1},... | collective-permute-start | bytes 1572872 | tf_op jit(solution)/shard_map/ppermute | solution.py:45
  20.4 2.3 %collective-permute-start.4 = (bf16[4,256,256]{2,1,0:T(8,128)(2,1)S(1)}, bf16[4,256,256]{2,1,0:T(8,128)(2,1)S(1)}, u32[]{:S(2)}, u32[]{:S(2)}) collective-permute-start(bf16[4,256,256]{2,1,0:T(8,128)(2,1)S(1)} %get-tuple-element.69), channel_id=1, source_target_pairs={{0,8},{1,9},{2,10},{3,11},{4,12},{5,13},{6,14},{7,15},{8,0},{9,1},... | collective-permute-start | bytes 1572872 | tf_op jit(solution)/shard_map/ppermute | solution.py:45
  23.5 29.1 %collective-permute-start = (bf16[256,2048]{1,0:T(8,128)(2,1)}, bf16[256,2048]{1,0:T(8,128)(2,1)}, u32[]{:S(2)}, u32[]{:S(2)}) collective-permute-start(bf16[256,2048]{1,0:T(8,128)(2,1)} %get-tuple-element.65), channel_id=1, source_target_pairs={{0,2},{1,3},{2,0},{3,1},{4,6},{5,7},{6,4},{7,5},{8,14},{9,15},{10,... | collective-permute-start | bytes 3145736 | tf_op jit(solution)/shard_map/ppermute | solution.py:45
  27.9 23.8 %copy-start.9 = (bf16[256,1792]{1,0:T(8,128)(2,1)}, bf16[256,1792]{1,0:T(8,128)(2,1)S(1)}, u32[]{:S(2)}) copy-start(bf16[256,1792]{1,0:T(8,128)(2,1)S(1)} %collective-permute-done.2.refs_1_.refs_3_) | copy-start | bytes 2752516
  27.9 22.2 %collective-permute-start.8 = (bf16[256,1792]{1,0:T(8,128)(2,1)S(1)}, bf16[256,1792]{1,0:T(8,128)(2,1)}, u32[]{:S(2)}, u32[]{:S(2)}) collective-permute-start(bf16[256,1792]{1,0:T(8,128)(2,1)S(1)} %collective-permute-done.2.refs_1_.refs_3_), channel_id=1, source_target_pairs={{0,1},{1,0},{2,3},{3,2},{4,5},{5,4},{6,7},{7,6},{8,9},{9,8},{10,11... | collective-permute-start | bytes 2752520 | tf_op jit(solution)/shard_map/ppermute | solution.py:45
  31.7 22.8 %collective-permute-start.7 = (bf16[256,1792]{1,0:T(8,128)(2,1)}, bf16[256,1792]{1,0:T(8,128)(2,1)}, u32[]{:S(2)}, u32[]{:S(2)}) collective-permute-start(bf16[256,1792]{1,0:T(8,128)(2,1)} %collective-permute-done.6.refs_2_.refs_4_), channel_id=1, source_target_pairs={{0,6},{1,7},{2,4},{3,5},{4,2},{5,3},{6,0},{7,1},{8,10},{9,11},{10,... | collective-permute-start | bytes 2752520 | tf_op jit(solution)/shard_map/ppermute | solution.py:45
  32.1 32.2 %collective-permute-start.1 = (bf16[256,2048]{1,0:T(8,128)(2,1)}, bf16[256,2048]{1,0:T(8,128)(2,1)}, u32[]{:S(2)}, u32[]{:S(2)}) collective-permute-start(bf16[256,2048]{1,0:T(8,128)(2,1)} %get-tuple-element.66), channel_id=1, source_target_pairs={{0,2},{1,3},{2,0},{3,1},{4,6},{5,7},{6,4},{7,5},{8,14},{9,15},{10,... | collective-permute-start | bytes 3145736 | tf_op jit(solution)/shard_map/ppermute | solution.py:45
  37.5 32.3 %collective-permute-start.9 = (bf16[256,1792]{1,0:T(8,128)(2,1)}, bf16[256,1792]{1,0:T(8,128)(2,1)}, u32[]{:S(2)}, u32[]{:S(2)}) collective-permute-start(bf16[256,1792]{1,0:T(8,128)(2,1)} %collective-permute-done.6.refs_2_.refs_4_), channel_id=1, source_target_pairs={{0,1},{1,0},{2,3},{3,2},{4,5},{5,4},{6,7},{7,6},{8,9},{9,8},{10,11... | collective-permute-start | bytes 2752520 | tf_op jit(solution)/shard_map/ppermute | solution.py:45
  54.4 34.9 %collective-permute-start.10 = (bf16[256,1792]{1,0:T(8,128)(2,1)}, bf16[256,1792]{1,0:T(8,128)(2,1)S(1)}, u32[]{:S(2)}, u32[]{:S(2)}) collective-permute-start(bf16[256,1792]{1,0:T(8,128)(2,1)} %collective-permute-done.7.refs_4_.refs_6_), channel_id=1, source_target_pairs={{0,1},{1,0},{2,3},{3,2},{4,5},{5,4},{6,7},{7,6},{8,9},{9,8},{10,11... | collective-permute-start | bytes 2752520 | tf_op jit(solution)/shard_map/ppermute | solution.py:45
  55.0 34.4 %collective-permute-start.11 = (bf16[256,1792]{1,0:T(8,128)(2,1)}, bf16[256,1792]{1,0:T(8,128)(2,1)}, u32[]{:S(2)}, u32[]{:S(2)}) collective-permute-start(bf16[256,1792]{1,0:T(8,128)(2,1)} %get-tuple-element.82), channel_id=1, source_target_pairs={{0,2},{1,3},{2,0},{3,1},{4,6},{5,7},{6,4},{7,5},{8,14},{9,15},{10,... | collective-permute-start | bytes 2752520 | tf_op jit(solution)/shard_map/ppermute | solution.py:45
  57.7 31.6 %collective-permute-start.12 = (bf16[256,1792]{1,0:T(8,128)(2,1)}, bf16[256,1792]{1,0:T(8,128)(2,1)}, u32[]{:S(2)}, u32[]{:S(2)}) collective-permute-start(bf16[256,1792]{1,0:T(8,128)(2,1)} %get-tuple-element.83), channel_id=1, source_target_pairs={{0,2},{1,3},{2,0},{3,1},{4,6},{5,7},{6,4},{7,5},{8,14},{9,15},{10,... | collective-permute-start | bytes 2752520 | tf_op jit(solution)/shard_map/ppermute | solution.py:45
  64.3 32.3 %collective-permute-start.14 = (bf16[4,256,256]{2,1,0:T(8,128)(2,1)}, bf16[4,256,256]{2,1,0:T(8,128)(2,1)S(1)}, u32[]{:S(2)}, u32[]{:S(2)}) collective-permute-start(bf16[4,256,256]{2,1,0:T(8,128)(2,1)} %get-tuple-element.86), channel_id=1, source_target_pairs={{0,16},{1,17},{2,18},{3,19},{4,20},{5,21},{6,22},{7,23},{8,24},{9,... | collective-permute-start | bytes 1572872 | tf_op jit(solution)/shard_map/ppermute | solution.py:45
  69.3 20.0 %copy-start.13 = (bf16[512,1792]{1,0:T(8,128)(2,1)S(1)}, bf16[512,1792]{1,0:T(8,128)(2,1)}, u32[]{:S(2)}) copy-start(bf16[512,1792]{1,0:T(8,128)(2,1)} %copy-done.12) | copy-start | bytes 5505028
  69.3 20.0 %copy-start.33 = (f32[1,3584]{1,0:T(1,128)S(1)}, f32[1,3584]{1,0:T(1,128)}, u32[]{:S(2)}) copy-start(f32[1,3584]{1,0:T(1,128)} %gain_ref.3) | copy-start | bytes 43012
  93.5 4.5 %collective-permute-start.13 = (f32[8,8,128]{2,1,0:T(8,128)S(1)}, f32[8,8,128]{2,1,0:T(8,128)S(1)}, u32[]{:S(2)}, u32[]{:S(2)}) collective-permute-start(f32[8,8,128]{2,1,0:T(8,128)S(1)} %row_stats.1.mine_ref), channel_id=1, source_target_pairs={{0,2},{1,3},{2,0},{3,1},{4,6},{5,7},{6,4},{7,5},{8,14},{9,15},{10,... | collective-permute-start | bytes 98312 | tf_op jit(solution)/shard_map/ppermute | solution.py:45
  104.1 18.1 %copy-start = (bf16[1024,1792]{1,0:T(8,128)(2,1)}, bf16[1024,1792]{1,0:T(8,128)(2,1)S(1)}, u32[]{:S(2)}) copy-start(bf16[1024,1792]{1,0:T(8,128)(2,1)S(1)} %get-tuple-element.105.refs_1_.refs_2_) | copy-start | bytes 11010052
  104.1 24.7 %collective-permute-start.15 = (bf16[272,1792]{1,0:T(8,128)(2,1)S(1)}, bf16[272,1792]{1,0:T(8,128)(2,1)S(1)}, u32[]{:S(2)}, u32[]{:S(2)}) collective-permute-start(bf16[272,1792]{1,0:T(8,128)(2,1)S(1)} %get-tuple-element.96.refs_0_), channel_id=1, source_target_pairs={{0,1},{1,0},{2,3},{3,2},{4,5},{5,4},{6,7},{7,6},{8,9},{9,8},{10,11... | collective-permute-start | bytes 2924552 | tf_op jit(solution)/shard_map/ppermute | solution.py:45
  106.5 22.3 %collective-permute-start.16 = (bf16[256,1792]{1,0:T(8,128)(2,1)S(1)}, bf16[256,1792]{1,0:T(8,128)(2,1)S(1)}, u32[]{:S(2)}, u32[]{:S(2)}) collective-permute-start(bf16[256,1792]{1,0:T(8,128)(2,1)S(1)} %get-tuple-element.99), channel_id=1, source_target_pairs={{0,6},{1,7},{2,4},{3,5},{4,2},{5,3},{6,0},{7,1},{8,10},{9,11},{10,... | collective-permute-start | bytes 2752520 | tf_op jit(solution)/shard_map/ppermute | solution.py:45
  111.2 22.9 %collective-permute-start.21 = (bf16[256,2048]{1,0:T(8,128)(2,1)S(1)}, bf16[256,2048]{1,0:T(8,128)(2,1)S(1)}, u32[]{:S(2)}, u32[]{:S(2)}) collective-permute-start(bf16[256,2048]{1,0:T(8,128)(2,1)S(1)} %context_term.3), channel_id=1, source_target_pairs={{0,2},{1,3},{2,0},{3,1},{4,6},{5,7},{6,4},{7,5},{8,14},{9,15},{10,... | collective-permute-start | bytes 3145736 | tf_op jit(solution)/shard_map/ppermute | solution.py:45
  128.0 31.4 %collective-permute-start.22 = (bf16[256,2048]{1,0:T(8,128)(2,1)}, bf16[256,2048]{1,0:T(8,128)(2,1)}, u32[]{:S(2)}, u32[]{:S(2)}) collective-permute-start(bf16[256,2048]{1,0:T(8,128)(2,1)} %context_term.4), channel_id=1, source_target_pairs={{0,2},{1,3},{2,0},{3,1},{4,6},{5,7},{6,4},{7,5},{8,14},{9,15},{10,... | collective-permute-start | bytes 3145736 | tf_op jit(solution)/shard_map/ppermute | solution.py:45
  128.2 25.4 %collective-permute-start.20 = (bf16[256,1792]{1,0:T(8,128)(2,1)}, bf16[256,1792]{1,0:T(8,128)(2,1)}, u32[]{:S(2)}, u32[]{:S(2)}) collective-permute-start(bf16[256,1792]{1,0:T(8,128)(2,1)} %get-tuple-element.108), channel_id=1, source_target_pairs={{0,1},{1,0},{2,3},{3,2},{4,5},{5,4},{6,7},{7,6},{8,9},{9,8},{10,11... | collective-permute-start | bytes 2752520 | tf_op jit(solution)/shard_map/ppermute | solution.py:45
  129.8 10.6 %collective-permute-start.18 = (bf16[128,1792]{1,0:T(8,128)(2,1)S(1)}, bf16[128,1792]{1,0:T(8,128)(2,1)S(1)}, u32[]{:S(2)}, u32[]{:S(2)}) collective-permute-start(bf16[128,1792]{1,0:T(8,128)(2,1)S(1)} %get-tuple-element.101), channel_id=1, source_target_pairs={{0,6},{1,7},{2,4},{3,5},{4,2},{5,3},{6,0},{7,1},{8,10},{9,11},{10,... | collective-permute-start | bytes 1376264 | tf_op jit(solution)/shard_map/ppermute | solution.py:45
  130.5 6.4 %collective-permute-start.17 = (bf16[2,256,256]{2,1,0:T(8,128)(2,1)S(1)}, bf16[2,256,256]{2,1,0:T(8,128)(2,1)S(1)}, u32[]{:S(2)}, u32[]{:S(2)}) collective-permute-start(bf16[2,256,256]{2,1,0:T(8,128)(2,1)S(1)} %get-tuple-element.87), channel_id=1, source_target_pairs={{0,48},{1,49},{2,50},{3,51},{4,52},{5,53},{6,54},{7,55},{8,56},{9,... | collective-permute-start | bytes 786440 | tf_op jit(solution)/shard_map/ppermute | solution.py:45
  134.1 19.5 %collective-permute-start.19 = (bf16[144,1792]{1,0:T(8,128)(2,1)}, bf16[144,1792]{1,0:T(8,128)(2,1)}, u32[]{:S(2)}, u32[]{:S(2)}) collective-permute-start(bf16[144,1792]{1,0:T(8,128)(2,1)} %get-tuple-element.106.refs_0_), channel_id=1, source_target_pairs={{0,6},{1,7},{2,4},{3,5},{4,2},{5,3},{6,0},{7,1},{8,10},{9,11},{10,... | collective-permute-start | bytes 1548296 | tf_op jit(solution)/shard_map/ppermute | solution.py:45
  137.6 38.5 %collective-permute-start.27 = (bf16[256,1792]{1,0:T(8,128)(2,1)}, bf16[256,1792]{1,0:T(8,128)(2,1)}, u32[]{:S(2)}, u32[]{:S(2)}) collective-permute-start(bf16[256,1792]{1,0:T(8,128)(2,1)} %add.137), channel_id=1, source_target_pairs={{0,1},{1,0},{2,3},{3,2},{4,5},{5,4},{6,7},{7,6},{8,9},{9,8},{10,11... | collective-permute-start | bytes 2752520 | tf_op jit(solution)/shard_map/ppermute | solution.py:45
  141.1 35.0 %collective-permute-start.26 = (bf16[256,1792]{1,0:T(8,128)(2,1)}, bf16[256,1792]{1,0:T(8,128)(2,1)}, u32[]{:S(2)}, u32[]{:S(2)}) collective-permute-start(bf16[256,1792]{1,0:T(8,128)(2,1)} %get-tuple-element.116), channel_id=1, source_target_pairs={{0,6},{1,7},{2,4},{3,5},{4,2},{5,3},{6,0},{7,1},{8,10},{9,11},{10,... | collective-permute-start | bytes 2752520 | tf_op jit(solution)/shard_map/ppermute | solution.py:45
  155.5 20.6 %collective-permute-start.25 = (bf16[144,1792]{1,0:T(8,128)(2,1)S(1)}, bf16[144,1792]{1,0:T(8,128)(2,1)S(1)}, u32[]{:S(2)}, u32[]{:S(2)}) collective-permute-start(bf16[144,1792]{1,0:T(8,128)(2,1)S(1)} %get-tuple-element.114.sent_ref), channel_id=1, source_target_pairs={{0,2},{1,3},{2,0},{3,1},{4,6},{5,7},{6,4},{7,5},{8,14},{9,15},{10,... | collective-permute-start | bytes 1548296 | tf_op jit(solution)/shard_map/ppermute | solution.py:45
  159.3 16.8 %collective-permute-start.23 = (bf16[128,1792]{1,0:T(8,128)(2,1)S(1)}, bf16[128,1792]{1,0:T(8,128)(2,1)S(1)}, u32[]{:S(2)}, u32[]{:S(2)}) collective-permute-start(bf16[128,1792]{1,0:T(8,128)(2,1)S(1)} %get-tuple-element.109), channel_id=1, source_target_pairs={{0,2},{1,3},{2,0},{3,1},{4,6},{5,7},{6,4},{7,5},{8,14},{9,15},{10,... | collective-permute-start | bytes 1376264 | tf_op jit(solution)/shard_map/ppermute | solution.py:45
  159.4 8.8 %collective-permute-start.24 = (bf16[1,256,256]{2,1,0:T(8,128)(2,1)S(1)}, bf16[1,256,256]{2,1,0:T(8,128)(2,1)S(1)}, u32[]{:S(2)}, u32[]{:S(2)}) collective-permute-start(bf16[1,256,256]{2,1,0:T(8,128)(2,1)S(1)} %get-tuple-element.104), channel_id=1, source_target_pairs={{0,64},{1,65},{2,66},{3,67},{4,68},{5,69},{6,70},{7,71},{8,72},{9,... | collective-permute-start | bytes 393224 | tf_op jit(solution)/shard_map/ppermute | solution.py:45
  (33 other events, 185.7 us)

commit v4 on v3

--- a/solution.py
+++ b/solution.py
@@ -592,19 +592,19 @@
     x3_got = send(x3_away, TO_X3)
     zlo_away, zlo_kept = outer_sum(zlo_at, after(x3_kept, o_self_z), x3_got, turned=True)
     zlo_got = send(zlo_away, TO_ZLO)
-    own_context = context_term(at, after(g, zlo_away), 0, blocks, F32, 2)
     o_mate = send(after(o_mate, x_mate[0], got_high), TO_MATE)
 
     x_self = add_x(
         which,
         x_self_own,
         x_mate[1],
-        after(x_from_mate[0], own_context),
+        after(x_from_mate[0], zlo_away),
         x_from_mate[1],
         x_self_z,
     )
     x_got = [send(piece, TO_PARTNER) for piece in x_self]
-    grad_context = end_context(which, after(own_context, x_self[0]), got_high, got_low)
+    own_context = context_term(at, after(g, x_self[0]), 0, blocks, F32, 2)
+    grad_context = end_context(which, own_context, got_high, got_low)
     outer_grad = (after(zlo_kept, grad_context)[0, :COLS] + zlo_got[0, :COLS].astype(F32)) / 16
     new_momentum = 0.9 * momentum.T + outer_grad
     new_anchor = anchor.T - 0.7 * (outer_grad + 0.9 * new_momentum)

time: 183 us -> 181 us (0.989); the launches traced: 181 us -> 181 us
  local copies, waits for them, and re-layouts: 19 us -> 15.5 us
  waiting for transfers between devices: 50.1 us -> 53.2 us
    unnamed x74 -> x70, local copies, waits for them, and re-layouts: 14.4 us -> 10.8 us
    ppermute x28, waiting for transfers between devices: 50.1 us -> 53.2 us  [send(): return lax.ppermute(value, BOTH, pairs)]
  transfers between devices with their start and end apart: 28 -> 28, of which waited for: 13 -> 14; matrix products, arithmetic and copies ran while one was open for 3% -> 3% of each run, Pallas kernels for 32% -> 32%
where the time goes in v4:
time: 181 us
  Pallas kernels  70.9 us (39%)
  waiting for transfers between devices  53.2 us (29%)
  starting transfers between devices  39 us (22%)
  local copies, waits for them, and re-layouts  15.5 us (9%)
    pallas_call x20, Pallas kernels, run(): return built(at, *placed)  70.9 us
    ppermute x28, waiting for transfers between devices, send(): return lax.ppermute(value, BOTH, pairs)  53.2 us
    ppermute x28, starting transfers between devices, send(): return lax.ppermute(value, BOTH, pairs)  39 us
    unnamed x70, local copies, waits for them, and re-layouts  10.8 us
  transfers between devices with their start and end apart: 28, of which 14 were waited for; matrix products, arithmetic and copies ran while one was open for 3% of the time, Pallas kernels for 32%

profile of v4, /device:TPU:1, one launch (start us, length us, event | category | flops | bytes accessed | tf_op | source)
XLA Modules:
  0.0 180.8 jit_solution(14276876404669907943)
XLA Ops:
  2.4 4.5 %collective-permute-start.3 = (bf16[256,1792]{1,0:T(8,128)(2,1)S(1)}, bf16[256,1792]{1,0:T(8,128)(2,1)S(1)}, u32[]{:S(2)}, u32[]{:S(2)}) collective-permute-start(bf16[256,1792]{1,0:T(8,128)(2,1)S(1)} %get-tuple-element.61.refs_0_.refs_2_), channel_id=1, source_target_pairs={{0,1},{1,0},{2,3},{3,2},{4,5},{5,4},{6,7},{7,6},{8,9},{9,8},{10,11... | collective-permute-start | bytes 2752520 | tf_op jit(solution)/shard_map/ppermute | solution.py:45
  8.2 2.1 %split.3 = (bf16[512,1792]{1,0:T(8,128)(2,1)S(1)}, bf16[512,1792]{1,0:T(8,128)(2,1)S(1)}) custom-call(s32[1]{0:T(128)} %bitcast.at_ref.refs_0_, bf16[512,3584]{1,0:T(8,128)(2,1)} %in_ref), custom_call_target="tpu_custom_call" | custom-call | bytes 6000000 | tf_op jit(solution)/shard_map/split/pallas_call | solution.py:82
  12.8 3.5 %outer_parts.1 = (bf16[4,256,256]{2,1,0:T(8,128)(2,1)S(1)}, bf16[4,256,256]{2,1,0:T(8,128)(2,1)S(1)}, f32[8,256,256]{2,1,0:T(8,128)S(1)}) custom-call(s32[1]{0:T(128)} %bitcast.9.at_ref, f32[256,3584]{1,0:T(8,128)} %bitcast.48), custom_call_target="tpu_custom_call" | custom-call | bytes 9000000 | tf_op jit(solution)/shard_map/outer_parts/pallas_call | solution.py:82
  17.7 1.9 %collective-permute-start.6 = (bf16[256,1792]{1,0:T(8,128)(2,1)S(1)}, bf16[256,1792]{1,0:T(8,128)(2,1)}, u32[]{:S(2)}, u32[]{:S(2)}) collective-permute-start(bf16[256,1792]{1,0:T(8,128)(2,1)S(1)} %get-tuple-element.73), channel_id=1, source_target_pairs={{0,2},{1,3},{2,0},{3,1},{4,6},{5,7},{6,4},{7,5},{8,14},{9,15},{10,... | collective-permute-start | bytes 2752520 | tf_op jit(solution)/shard_map/ppermute | solution.py:45
  24.3 2.7 %collective-permute-done.3.refs_3_.refs_5_ = bf16[256,1792]{1,0:T(8,128)(2,1)S(1)} collective-permute-done((bf16[256,1792]{1,0:T(8,128)(2,1)S(1)}, bf16[256,1792]{1,0:T(8,128)(2,1)S(1)}, u32[]{:S(2)}, u32[]{:S(2)}) %collective-permute-start.3) | collective-permute-done | bytes 917536 | tf_op jit(solution)/shard_map/ppermute | solution.py:45
  27.9 2.6 %collective-permute-start.8 = (bf16[256,1792]{1,0:T(8,128)(2,1)S(1)}, bf16[256,1792]{1,0:T(8,128)(2,1)}, u32[]{:S(2)}, u32[]{:S(2)}) collective-permute-start(bf16[256,1792]{1,0:T(8,128)(2,1)S(1)} %collective-permute-done.2.refs_1_.refs_3_), channel_id=1, source_target_pairs={{0,1},{1,0},{2,3},{3,2},{4,5},{5,4},{6,7},{7,6},{8,9},{9,8},{10,11... | collective-permute-start | bytes 2752520 | tf_op jit(solution)/shard_map/ppermute | solution.py:45
  32.1 2.4 %collective-permute-start.1 = (bf16[256,2048]{1,0:T(8,128)(2,1)}, bf16[256,2048]{1,0:T(8,128)(2,1)}, u32[]{:S(2)}, u32[]{:S(2)}) collective-permute-start(bf16[256,2048]{1,0:T(8,128)(2,1)} %get-tuple-element.65), channel_id=1, source_target_pairs={{0,2},{1,3},{2,0},{3,1},{4,6},{5,7},{6,4},{7,5},{8,14},{9,15},{10,... | collective-permute-start | bytes 3145736 | tf_op jit(solution)/shard_map/ppermute | solution.py:45
  34.5 3.0 %fusion.5 = (bf16[256,1792]{1,0:T(8,128)(2,1)}, bf16[256,1792]{1,0:T(8,128)(2,1)}) fusion(bf16[512,1792]{1,0:T(8,128)(2,1)} %copy-done.16), kind=kLoop, calls=%fused_computation.9 | loop fusion | bytes 3670016 | tf_op jit(solution)/shard_map/slice | solution.py:562
  37.5 12.7 %collective-permute-done.8.refs_5_.refs_7_ = bf16[256,1792]{1,0:T(8,128)(2,1)} collective-permute-done((bf16[256,1792]{1,0:T(8,128)(2,1)S(1)}, bf16[256,1792]{1,0:T(8,128)(2,1)}, u32[]{:S(2)}, u32[]{:S(2)}) %collective-permute-start.8) | collective-permute-done | bytes 917536 | tf_op jit(solution)/shard_map/ppermute | solution.py:45
  55.0 2.7 %collective-permute-start.11 = (bf16[256,1792]{1,0:T(8,128)(2,1)}, bf16[256,1792]{1,0:T(8,128)(2,1)}, u32[]{:S(2)}, u32[]{:S(2)}) collective-permute-start(bf16[256,1792]{1,0:T(8,128)(2,1)} %get-tuple-element.81), channel_id=1, source_target_pairs={{0,2},{1,3},{2,0},{3,1},{4,6},{5,7},{6,4},{7,5},{8,14},{9,15},{10,... | collective-permute-start | bytes 2752520 | tf_op jit(solution)/shard_map/ppermute | solution.py:45
  57.7 6.5 %collective-permute-done.1.low_ref = bf16[256,2048]{1,0:T(8,128)(2,1)} collective-permute-done((bf16[256,2048]{1,0:T(8,128)(2,1)}, bf16[256,2048]{1,0:T(8,128)(2,1)}, u32[]{:S(2)}, u32[]{:S(2)}) %collective-permute-start.1) | collective-permute-done | bytes 1048608 | tf_op jit(solution)/shard_map/ppermute | solution.py:45
  65.7 3.6 %turn.1 = (bf16[2048,1024]{1,0:T(8,128)(2,1)S(1)}, bf16[1024,256]{1,0:T(8,128)(2,1)S(1)}) custom-call(s32[8]{0:T(128)S(1)} %stack.91.at_ref, bf16[512,2048]{1,0:T(8,128)(2,1)S(1)} %copy-done.2, bf16[256,2048]{1,0:T(8,128)(2,1)} %collective-permute-done.high_ref, bf16[256,2048]{1,0:T(8,128)(2,1)} %collective-permute-done.1.low_ref), custom_call_target="tpu_custom_call" | custom-call | bytes 12000000 | tf_op jit(solution)/shard_map/turn/pallas_call | solution.py:82
  69.8 10.1 %project.1.acc_ref = f32[1024,1792]{1,0:T(8,128)S(1)} custom-call(s32[9]{0:T(128)S(1)} %stack.90.at_ref.refs_0_, bf16[512,2048]{1,0:T(8,128)(2,1)S(1)} %copy-done.2, bf16[256,2048]{1,0:T(8,128)(2,1)} %collective-permute-done.high_ref, bf16[256,2048]{1,0:T(8,128)(2,1)} %collective-permute-done.1.low_ref, bf16[256,1792]{1,0:T(8,128)(2,1)S(1)} %copy-done.4, ...), custom_call_target="tpu_custom_call" | custom-call | bytes 42000000 | tf_op jit(solution)/shard_map/project/pallas_call | solution.py:82
  79.9 9.4 %collective-permute-done.10.block_ref.refs_9_ = bf16[256,1792]{1,0:T(8,128)(2,1)S(1)} collective-permute-done((bf16[256,1792]{1,0:T(8,128)(2,1)}, bf16[256,1792]{1,0:T(8,128)(2,1)S(1)}, u32[]{:S(2)}, u32[]{:S(2)}) %collective-permute-start.10) | collective-permute-done | bytes 917536 | tf_op jit(solution)/shard_map/ppermute | solution.py:45
  89.4 4.1 %row_stats.1.mine_ref = f32[8,8,128]{2,1,0:T(8,128)S(1)} custom-call(s32[9]{0:T(128)S(1)} %stack.90.at_ref.refs_0_, f32[1024,1792]{1,0:T(8,128)S(1)} %project.1.acc_ref, bf16[1024,256]{1,0:T(8,128)(2,1)S(1)} %get-tuple-element.79.slab_ref, bf16[256,1792]{1,0:T(8,128)(2,1)S(1)} %collective-permute-done.10.block_ref.refs_9_, bf16[512,1792]{1,0:T(8,128)(2,1)S(1)} %copy-done.13, ...), custom_call_target="tpu_custom_call" | custom-call | bytes 9000000 | tf_op jit(solution)/shard_map/row_stats/pallas_call | solution.py:82
  93.5 3.0 %collective-permute-start.13 = (f32[8,8,128]{2,1,0:T(8,128)S(1)}, f32[8,8,128]{2,1,0:T(8,128)S(1)}, u32[]{:S(2)}, u32[]{:S(2)}) collective-permute-start(f32[8,8,128]{2,1,0:T(8,128)S(1)} %row_stats.1.mine_ref), channel_id=1, source_target_pairs={{0,2},{1,3},{2,0},{3,1},{4,6},{5,7},{6,4},{7,5},{8,14},{9,15},{10,... | collective-permute-start | bytes 98312 | tf_op jit(solution)/shard_map/ppermute | solution.py:45
  98.0 6.1 %grad_step.1 = (bf16[1024,1792]{1,0:T(8,128)(2,1)S(1)}, bf16[272,1792]{1,0:T(8,128)(2,1)S(1)}, bf16[256,1792]{1,0:T(8,128)(2,1)S(1)}) custom-call(s32[9]{0:T(128)S(1)} %stack.90.at_ref.refs_0_, f32[1024,1792]{1,0:T(8,128)S(1)} %project.1.acc_ref, bf16[1024,256]{1,0:T(8,128)(2,1)S(1)} %get-tuple-element.79.slab_ref, ...), custom_call_target="tpu_custom_call" | custom-call | bytes 18000000 | tf_op jit(solution)/shard_map/grad_step/pallas_call | solution.py:82
  104.1 2.4 %collective-permute-start.15 = (bf16[272,1792]{1,0:T(8,128)(2,1)S(1)}, bf16[272,1792]{1,0:T(8,128)(2,1)S(1)}, u32[]{:S(2)}, u32[]{:S(2)}) collective-permute-start(bf16[272,1792]{1,0:T(8,128)(2,1)S(1)} %get-tuple-element.94.refs_0_), channel_id=1, source_target_pairs={{0,1},{1,0},{2,3},{3,2},{4,5},{5,4},{6,7},{7,6},{8,9},{9,8},{10,11... | collective-permute-start | bytes 2924552 | tf_op jit(solution)/shard_map/ppermute | solution.py:45
  106.6 4.7 %context_term.3 = bf16[256,2048]{1,0:T(8,128)(2,1)S(1)} custom-call(s32[9]{0:T(128)S(1)} %stack.90.at_ref.refs_0_, bf16[1024,1792]{1,0:T(8,128)(2,1)S(1)} %get-tuple-element.108.refs_1_.refs_2_, bf16[256,1792]{1,0:T(8,128)(2,1)S(1)} %copy-done.4, bf16[256,1792]{1,0:T(8,128)(2,1)S(1)} %copy-done.10, bf16[256,1792]{1,0:T(8,128)(2,1)} %collective-permute-done.6.refs_2_.refs_4_, ...), custom_call_target="tpu_custom_call" | custom-call | bytes 7500000 | tf_op jit(solution)/shard_map/context_term/pallas_call | solution.py:82
  111.2 2.5 %collective-permute-start.21 = (bf16[256,2048]{1,0:T(8,128)(2,1)S(1)}, bf16[256,2048]{1,0:T(8,128)(2,1)S(1)}, u32[]{:S(2)}, u32[]{:S(2)}) collective-permute-start(bf16[256,2048]{1,0:T(8,128)(2,1)S(1)} %context_term.3), channel_id=1, source_target_pairs={{0,2},{1,3},{2,0},{3,1},{4,6},{5,7},{6,4},{7,5},{8,14},{9,15},{10,... | collective-permute-start | bytes 3145736 | tf_op jit(solution)/shard_map/ppermute | solution.py:45
  113.8 3.3 %weight_terms.2 = (bf16[256,1792]{1,0:T(8,128)(2,1)}, bf16[256,1792]{1,0:T(8,128)(2,1)}) custom-call(s32[1]{0:T(128)} %bitcast.at_ref.refs_0_, bf16[2048,1024]{1,0:T(8,128)(2,1)S(1)} %get-tuple-element.66.turned_ref.refs_1_, bf16[1024,1792]{1,0:T(8,128)(2,1)S(1)} %get-tuple-element.108.refs_1_.refs_2_), custom_call_target="tpu_custom_call" | custom-call | bytes 6000000 | tf_op jit(solution)/shard_map/weight_terms/pallas_call | solution.py:82
  117.0 4.0 %weight_terms.3 = (f32[256,1792]{1,0:T(8,128)S(1)}, f32[256,1792]{1,0:T(8,128)S(1)}, f32[256,1792]{1,0:T(8,128)S(1)}, f32[256,1792]{1,0:T(8,128)S(1)}) custom-call(s32[1]{0:T(128)} %bitcast.at_ref.refs_0_, bf16[2048,1024]{1,0:T(8,128)(2,1)S(1)} %get-tuple-element.66.turned_ref.refs_1_, bf16[1024,1792]{1,0:T(8,128)(2,1)S(1)} %get-tuple-element.108.refs_1_.refs_2_), custom_call_target="tpu_custom_call" | custom-call | bytes 12000000 | tf_op jit(solution)/shard_map/weight_terms/pallas_call | solution.py:82
  121.0 6.4 %context_term.4 = bf16[256,2048]{1,0:T(8,128)(2,1)} custom-call(s32[9]{0:T(128)S(1)} %stack.90.at_ref.refs_0_, bf16[1024,1792]{1,0:T(8,128)(2,1)S(1)} %get-tuple-element.108.refs_1_.refs_2_, bf16[256,1792]{1,0:T(8,128)(2,1)S(1)} %copy-done.4, bf16[256,1792]{1,0:T(8,128)(2,1)S(1)} %copy-done.10, bf16[256,1792]{1,0:T(8,128)(2,1)} %collective-permute-done.6.refs_2_.refs_4_, ...), custom_call_target="tpu_custom_call" | custom-call | bytes 7500000 | tf_op jit(solution)/shard_map/context_term/pallas_call | solution.py:82
  130.0 2.5 %collective-permute-start.18 = (bf16[2,256,256]{2,1,0:T(8,128)(2,1)S(1)}, bf16[2,256,256]{2,1,0:T(8,128)(2,1)S(1)}, u32[]{:S(2)}, u32[]{:S(2)}) collective-permute-start(bf16[2,256,256]{2,1,0:T(8,128)(2,1)S(1)} %get-tuple-element.86), channel_id=1, source_target_pairs={{0,48},{1,49},{2,50},{3,51},{4,52},{5,53},{6,54},{7,55},{8,56},{9,... | collective-permute-start | bytes 786440 | tf_op jit(solution)/shard_map/ppermute | solution.py:45
  136.4 2.6 %collective-permute-start.27 = (bf16[256,1792]{1,0:T(8,128)(2,1)}, bf16[256,1792]{1,0:T(8,128)(2,1)}, u32[]{:S(2)}, u32[]{:S(2)}) collective-permute-start(bf16[256,1792]{1,0:T(8,128)(2,1)} %add.137), channel_id=1, source_target_pairs={{0,1},{1,0},{2,3},{3,2},{4,5},{5,4},{6,7},{7,6},{8,9},{9,8},{10,11... | collective-permute-start | bytes 2752520 | tf_op jit(solution)/shard_map/ppermute | solution.py:45
  141.4 5.1 %collective-permute-done.20.refs_3_ = bf16[256,1792]{1,0:T(8,128)(2,1)} collective-permute-done((bf16[256,1792]{1,0:T(8,128)(2,1)}, bf16[256,1792]{1,0:T(8,128)(2,1)}, u32[]{:S(2)}, u32[]{:S(2)}) %collective-permute-start.20) | collective-permute-done | bytes 917536 | tf_op jit(solution)/shard_map/ppermute | solution.py:45
  146.5 4.4 %collective-permute-done.19.refs_2_ = bf16[144,1792]{1,0:T(8,128)(2,1)} collective-permute-done((bf16[144,1792]{1,0:T(8,128)(2,1)}, bf16[144,1792]{1,0:T(8,128)(2,1)}, u32[]{:S(2)}, u32[]{:S(2)}) %collective-permute-start.19) | collective-permute-done | bytes 516128 | tf_op jit(solution)/shard_map/ppermute | solution.py:45
  155.2 4.3 %collective-permute-start.25 = (bf16[144,1792]{1,0:T(8,128)(2,1)S(1)}, bf16[144,1792]{1,0:T(8,128)(2,1)S(1)}, u32[]{:S(2)}, u32[]{:S(2)}) collective-permute-start(bf16[144,1792]{1,0:T(8,128)(2,1)S(1)} %get-tuple-element.112.sent_ref), channel_id=1, source_target_pairs={{0,2},{1,3},{2,0},{3,1},{4,6},{5,7},{6,4},{7,5},{8,14},{9,15},{10,... | collective-permute-start | bytes 1548296 | tf_op jit(solution)/shard_map/ppermute | solution.py:45
  160.4 6.7 %context_term.5.a_ref = f32[512,2048]{1,0:T(8,128)S(1)} custom-call(s32[9]{0:T(128)S(1)} %stack.90.at_ref.refs_0_, bf16[1024,1792]{1,0:T(8,128)(2,1)S(1)} %copy-done.1, bf16[256,1792]{1,0:T(8,128)(2,1)S(1)} %copy-done.5, bf16[256,1792]{1,0:T(8,128)(2,1)S(1)} %copy-done.11, bf16[256,1792]{1,0:T(8,128)(2,1)} %collective-permute-done.6.refs_2_.refs_4_, ...), custom_call_target="tpu_custom_call" | custom-call | bytes 15000000 | tf_op jit(solution)/shard_map/context_term/pallas_call | solution.py:82
  167.2 3.4 %end_context.1 = bf16[512,2048]{1,0:T(8,128)(2,1)} custom-call(s32[1]{0:T(128)} %bitcast.at_ref.refs_0_, f32[512,2048]{1,0:T(8,128)S(1)} %context_term.5.a_ref, bf16[256,2048]{1,0:T(8,128)(2,1)S(1)} %copy-done.22, bf16[256,2048]{1,0:T(8,128)(2,1)} %collective-permute-done.22.c_ref), custom_call_target="tpu_custom_call" | custom-call | bytes 6000000 | tf_op jit(solution)/shard_map/end_context/pallas_call | solution.py:82
  171.4 4.7 %collective-permute-done.23.high_ref = bf16[128,1792]{1,0:T(8,128)(2,1)S(1)} collective-permute-done((bf16[128,1792]{1,0:T(8,128)(2,1)S(1)}, bf16[128,1792]{1,0:T(8,128)(2,1)S(1)}, u32[]{:S(2)}, u32[]{:S(2)}) %collective-permute-start.23) | collective-permute-done | bytes 458784 | tf_op jit(solution)/shard_map/ppermute | solution.py:45
  176.1 4.5 %finish.1 = (f32[256,3584]{1,0:T(8,128)}, f32[1,3584]{1,0:T(1,128)}) custom-call(s32[9]{0:T(128)S(1)} %stack.90.at_ref.refs_0_, bf16[128,1792]{1,0:T(8,128)(2,1)S(1)} %collective-permute-done.23.high_ref, bf16[144,1792]{1,0:T(8,128)(2,1)S(1)} %collective-permute-done.25.low_ref, bf16[144,1792]{1,0:T(8,128)(2,1)S(1)} %get-tuple-element.112.sent_ref, ...), custom_call_target="tpu_custom_call" | custom-call | bytes 6000000 | tf_op jit(solution)/shard_map/finish/pallas_call | solution.py:82
  (121 shorter events, 37.2 us)
Async XLA Ops:
  2.4 24.6 %collective-permute-start.3 = (bf16[256,1792]{1,0:T(8,128)(2,1)S(1)}, bf16[256,1792]{1,0:T(8,128)(2,1)S(1)}, u32[]{:S(2)}, u32[]{:S(2)}) collective-permute-start(bf16[256,1792]{1,0:T(8,128)(2,1)S(1)} %get-tuple-element.61.refs_0_.refs_2_), channel_id=1, source_target_pairs={{0,1},{1,0},{2,3},{3,2},{4,5},{5,4},{6,7},{7,6},{8,9},{9,8},{10,11... | collective-permute-start | bytes 2752520 | tf_op jit(solution)/shard_map/ppermute | solution.py:45
  6.9 21.0 %collective-permute-start.2 = (bf16[256,1792]{1,0:T(8,128)(2,1)S(1)}, bf16[256,1792]{1,0:T(8,128)(2,1)S(1)}, u32[]{:S(2)}, u32[]{:S(2)}) collective-permute-start(bf16[256,1792]{1,0:T(8,128)(2,1)S(1)} %get-tuple-element.61.refs_0_.refs_2_), channel_id=1, source_target_pairs={{0,6},{1,7},{2,4},{3,5},{4,2},{5,3},{6,0},{7,1},{8,10},{9,11},{10,... | collective-permute-start | bytes 2752520 | tf_op jit(solution)/shard_map/ppermute | solution.py:45
  17.7 14.0 %collective-permute-start.6 = (bf16[256,1792]{1,0:T(8,128)(2,1)S(1)}, bf16[256,1792]{1,0:T(8,128)(2,1)}, u32[]{:S(2)}, u32[]{:S(2)}) collective-permute-start(bf16[256,1792]{1,0:T(8,128)(2,1)S(1)} %get-tuple-element.73), channel_id=1, source_target_pairs={{0,2},{1,3},{2,0},{3,1},{4,6},{5,7},{6,4},{7,5},{8,14},{9,15},{10,... | collective-permute-start | bytes 2752520 | tf_op jit(solution)/shard_map/ppermute | solution.py:45
  19.6 4.7 %collective-permute-start.5 = (bf16[4,256,256]{2,1,0:T(8,128)(2,1)S(1)}, bf16[4,256,256]{2,1,0:T(8,128)(2,1)S(1)}, u32[]{:S(2)}, u32[]{:S(2)}) collective-permute-start(bf16[4,256,256]{2,1,0:T(8,128)(2,1)S(1)} %get-tuple-element.63), channel_id=1, source_target_pairs={{0,8},{1,9},{2,10},{3,11},{4,12},{5,13},{6,14},{7,15},{8,0},{9,1},... | collective-permute-start | bytes 1572872 | tf_op jit(solution)/shard_map/ppermute | solution.py:45
  20.4 2.3 %collective-permute-start.4 = (bf16[4,256,256]{2,1,0:T(8,128)(2,1)S(1)}, bf16[4,256,256]{2,1,0:T(8,128)(2,1)S(1)}, u32[]{:S(2)}, u32[]{:S(2)}) collective-permute-start(bf16[4,256,256]{2,1,0:T(8,128)(2,1)S(1)} %get-tuple-element.68), channel_id=1, source_target_pairs={{0,8},{1,9},{2,10},{3,11},{4,12},{5,13},{6,14},{7,15},{8,0},{9,1},... | collective-permute-start | bytes 1572872 | tf_op jit(solution)/shard_map/ppermute | solution.py:45
  23.5 29.1 %collective-permute-start = (bf16[256,2048]{1,0:T(8,128)(2,1)}, bf16[256,2048]{1,0:T(8,128)(2,1)}, u32[]{:S(2)}, u32[]{:S(2)}) collective-permute-start(bf16[256,2048]{1,0:T(8,128)(2,1)} %get-tuple-element.64), channel_id=1, source_target_pairs={{0,2},{1,3},{2,0},{3,1},{4,6},{5,7},{6,4},{7,5},{8,14},{9,15},{10,... | collective-permute-start | bytes 3145736 | tf_op jit(solution)/shard_map/ppermute | solution.py:45
  27.9 23.8 %copy-start.9 = (bf16[256,1792]{1,0:T(8,128)(2,1)}, bf16[256,1792]{1,0:T(8,128)(2,1)S(1)}, u32[]{:S(2)}) copy-start(bf16[256,1792]{1,0:T(8,128)(2,1)S(1)} %collective-permute-done.2.refs_1_.refs_3_) | copy-start | bytes 2752516
  27.9 22.2 %collective-permute-start.8 = (bf16[256,1792]{1,0:T(8,128)(2,1)S(1)}, bf16[256,1792]{1,0:T(8,128)(2,1)}, u32[]{:S(2)}, u32[]{:S(2)}) collective-permute-start(bf16[256,1792]{1,0:T(8,128)(2,1)S(1)} %collective-permute-done.2.refs_1_.refs_3_), channel_id=1, source_target_pairs={{0,1},{1,0},{2,3},{3,2},{4,5},{5,4},{6,7},{7,6},{8,9},{9,8},{10,11... | collective-permute-start | bytes 2752520 | tf_op jit(solution)/shard_map/ppermute | solution.py:45
  31.7 22.7 %collective-permute-start.7 = (bf16[256,1792]{1,0:T(8,128)(2,1)}, bf16[256,1792]{1,0:T(8,128)(2,1)}, u32[]{:S(2)}, u32[]{:S(2)}) collective-permute-start(bf16[256,1792]{1,0:T(8,128)(2,1)} %collective-permute-done.6.refs_2_.refs_4_), channel_id=1, source_target_pairs={{0,6},{1,7},{2,4},{3,5},{4,2},{5,3},{6,0},{7,1},{8,10},{9,11},{10,... | collective-permute-start | bytes 2752520 | tf_op jit(solution)/shard_map/ppermute | solution.py:45
  32.1 32.2 %collective-permute-start.1 = (bf16[256,2048]{1,0:T(8,128)(2,1)}, bf16[256,2048]{1,0:T(8,128)(2,1)}, u32[]{:S(2)}, u32[]{:S(2)}) collective-permute-start(bf16[256,2048]{1,0:T(8,128)(2,1)} %get-tuple-element.65), channel_id=1, source_target_pairs={{0,2},{1,3},{2,0},{3,1},{4,6},{5,7},{6,4},{7,5},{8,14},{9,15},{10,... | collective-permute-start | bytes 3145736 | tf_op jit(solution)/shard_map/ppermute | solution.py:45
  37.5 32.3 %collective-permute-start.9 = (bf16[256,1792]{1,0:T(8,128)(2,1)}, bf16[256,1792]{1,0:T(8,128)(2,1)}, u32[]{:S(2)}, u32[]{:S(2)}) collective-permute-start(bf16[256,1792]{1,0:T(8,128)(2,1)} %collective-permute-done.6.refs_2_.refs_4_), channel_id=1, source_target_pairs={{0,1},{1,0},{2,3},{3,2},{4,5},{5,4},{6,7},{7,6},{8,9},{9,8},{10,11... | collective-permute-start | bytes 2752520 | tf_op jit(solution)/shard_map/ppermute | solution.py:45
  54.4 34.9 %collective-permute-start.10 = (bf16[256,1792]{1,0:T(8,128)(2,1)}, bf16[256,1792]{1,0:T(8,128)(2,1)S(1)}, u32[]{:S(2)}, u32[]{:S(2)}) collective-permute-start(bf16[256,1792]{1,0:T(8,128)(2,1)} %collective-permute-done.7.refs_4_.refs_6_), channel_id=1, source_target_pairs={{0,1},{1,0},{2,3},{3,2},{4,5},{5,4},{6,7},{7,6},{8,9},{9,8},{10,11... | collective-permute-start | bytes 2752520 | tf_op jit(solution)/shard_map/ppermute | solution.py:45
  55.0 34.4 %collective-permute-start.11 = (bf16[256,1792]{1,0:T(8,128)(2,1)}, bf16[256,1792]{1,0:T(8,128)(2,1)}, u32[]{:S(2)}, u32[]{:S(2)}) collective-permute-start(bf16[256,1792]{1,0:T(8,128)(2,1)} %get-tuple-element.81), channel_id=1, source_target_pairs={{0,2},{1,3},{2,0},{3,1},{4,6},{5,7},{6,4},{7,5},{8,14},{9,15},{10,... | collective-permute-start | bytes 2752520 | tf_op jit(solution)/shard_map/ppermute | solution.py:45
  57.7 31.7 %collective-permute-start.12 = (bf16[256,1792]{1,0:T(8,128)(2,1)}, bf16[256,1792]{1,0:T(8,128)(2,1)}, u32[]{:S(2)}, u32[]{:S(2)}) collective-permute-start(bf16[256,1792]{1,0:T(8,128)(2,1)} %get-tuple-element.82), channel_id=1, source_target_pairs={{0,2},{1,3},{2,0},{3,1},{4,6},{5,7},{6,4},{7,5},{8,14},{9,15},{10,... | collective-permute-start | bytes 2752520 | tf_op jit(solution)/shard_map/ppermute | solution.py:45
  64.3 32.3 %collective-permute-start.14 = (bf16[4,256,256]{2,1,0:T(8,128)(2,1)}, bf16[4,256,256]{2,1,0:T(8,128)(2,1)S(1)}, u32[]{:S(2)}, u32[]{:S(2)}) collective-permute-start(bf16[4,256,256]{2,1,0:T(8,128)(2,1)} %get-tuple-element.85), channel_id=1, source_target_pairs={{0,16},{1,17},{2,18},{3,19},{4,20},{5,21},{6,22},{7,23},{8,24},{9,... | collective-permute-start | bytes 1572872 | tf_op jit(solution)/shard_map/ppermute | solution.py:45
  69.3 20.0 %copy-start.13 = (bf16[512,1792]{1,0:T(8,128)(2,1)S(1)}, bf16[512,1792]{1,0:T(8,128)(2,1)}, u32[]{:S(2)}) copy-start(bf16[512,1792]{1,0:T(8,128)(2,1)} %copy-done.12) | copy-start | bytes 5505028
  93.5 4.5 %collective-permute-start.13 = (f32[8,8,128]{2,1,0:T(8,128)S(1)}, f32[8,8,128]{2,1,0:T(8,128)S(1)}, u32[]{:S(2)}, u32[]{:S(2)}) collective-permute-start(f32[8,8,128]{2,1,0:T(8,128)S(1)} %row_stats.1.mine_ref), channel_id=1, source_target_pairs={{0,2},{1,3},{2,0},{3,1},{4,6},{5,7},{6,4},{7,5},{8,14},{9,15},{10,... | collective-permute-start | bytes 98312 | tf_op jit(solution)/shard_map/ppermute | solution.py:45
  104.1 24.2 %collective-permute-start.15 = (bf16[272,1792]{1,0:T(8,128)(2,1)S(1)}, bf16[272,1792]{1,0:T(8,128)(2,1)S(1)}, u32[]{:S(2)}, u32[]{:S(2)}) collective-permute-start(bf16[272,1792]{1,0:T(8,128)(2,1)S(1)} %get-tuple-element.94.refs_0_), channel_id=1, source_target_pairs={{0,1},{1,0},{2,3},{3,2},{4,5},{5,4},{6,7},{7,6},{8,9},{9,8},{10,11... | collective-permute-start | bytes 2924552 | tf_op jit(solution)/shard_map/ppermute | solution.py:45
  106.5 21.7 %collective-permute-start.16 = (bf16[256,1792]{1,0:T(8,128)(2,1)S(1)}, bf16[256,1792]{1,0:T(8,128)(2,1)S(1)}, u32[]{:S(2)}, u32[]{:S(2)}) collective-permute-start(bf16[256,1792]{1,0:T(8,128)(2,1)S(1)} %get-tuple-element.96), channel_id=1, source_target_pairs={{0,6},{1,7},{2,4},{3,5},{4,2},{5,3},{6,0},{7,1},{8,10},{9,11},{10,... | collective-permute-start | bytes 2752520 | tf_op jit(solution)/shard_map/ppermute | solution.py:45
  111.2 22.9 %collective-permute-start.21 = (bf16[256,2048]{1,0:T(8,128)(2,1)S(1)}, bf16[256,2048]{1,0:T(8,128)(2,1)S(1)}, u32[]{:S(2)}, u32[]{:S(2)}) collective-permute-start(bf16[256,2048]{1,0:T(8,128)(2,1)S(1)} %context_term.3), channel_id=1, source_target_pairs={{0,2},{1,3},{2,0},{3,1},{4,6},{5,7},{6,4},{7,5},{8,14},{9,15},{10,... | collective-permute-start | bytes 3145736 | tf_op jit(solution)/shard_map/ppermute | solution.py:45
  127.4 32.2 %collective-permute-start.22 = (bf16[256,2048]{1,0:T(8,128)(2,1)}, bf16[256,2048]{1,0:T(8,128)(2,1)}, u32[]{:S(2)}, u32[]{:S(2)}) collective-permute-start(bf16[256,2048]{1,0:T(8,128)(2,1)} %context_term.4), channel_id=1, source_target_pairs={{0,2},{1,3},{2,0},{3,1},{4,6},{5,7},{6,4},{7,5},{8,14},{9,15},{10,... | collective-permute-start | bytes 3145736 | tf_op jit(solution)/shard_map/ppermute | solution.py:45
  127.6 18.9 %collective-permute-start.20 = (bf16[256,1792]{1,0:T(8,128)(2,1)}, bf16[256,1792]{1,0:T(8,128)(2,1)}, u32[]{:S(2)}, u32[]{:S(2)}) collective-permute-start(bf16[256,1792]{1,0:T(8,128)(2,1)} %get-tuple-element.106), channel_id=1, source_target_pairs={{0,1},{1,0},{2,3},{3,2},{4,5},{5,4},{6,7},{7,6},{8,9},{9,8},{10,11... | collective-permute-start | bytes 2752520 | tf_op jit(solution)/shard_map/ppermute | solution.py:45
  129.2 10.6 %collective-permute-start.17 = (bf16[128,1792]{1,0:T(8,128)(2,1)S(1)}, bf16[128,1792]{1,0:T(8,128)(2,1)S(1)}, u32[]{:S(2)}, u32[]{:S(2)}) collective-permute-start(bf16[128,1792]{1,0:T(8,128)(2,1)S(1)} %get-tuple-element.99), channel_id=1, source_target_pairs={{0,6},{1,7},{2,4},{3,5},{4,2},{5,3},{6,0},{7,1},{8,10},{9,11},{10,... | collective-permute-start | bytes 1376264 | tf_op jit(solution)/shard_map/ppermute | solution.py:45
  130.0 6.4 %collective-permute-start.18 = (bf16[2,256,256]{2,1,0:T(8,128)(2,1)S(1)}, bf16[2,256,256]{2,1,0:T(8,128)(2,1)S(1)}, u32[]{:S(2)}, u32[]{:S(2)}) collective-permute-start(bf16[2,256,256]{2,1,0:T(8,128)(2,1)S(1)} %get-tuple-element.86), channel_id=1, source_target_pairs={{0,48},{1,49},{2,50},{3,51},{4,52},{5,53},{6,54},{7,55},{8,56},{9,... | collective-permute-start | bytes 786440 | tf_op jit(solution)/shard_map/ppermute | solution.py:45
  134.1 16.8 %collective-permute-start.19 = (bf16[144,1792]{1,0:T(8,128)(2,1)}, bf16[144,1792]{1,0:T(8,128)(2,1)}, u32[]{:S(2)}, u32[]{:S(2)}) collective-permute-start(bf16[144,1792]{1,0:T(8,128)(2,1)} %get-tuple-element.98.refs_0_), channel_id=1, source_target_pairs={{0,6},{1,7},{2,4},{3,5},{4,2},{5,3},{6,0},{7,1},{8,10},{9,11},{10,... | collective-permute-start | bytes 1548296 | tf_op jit(solution)/shard_map/ppermute | solution.py:45
  134.2 26.2 %copy-start.8 = (bf16[256,1792]{1,0:T(8,128)(2,1)S(1)}, bf16[256,1792]{1,0:T(8,128)(2,1)}, u32[]{:S(2)}) copy-start(bf16[256,1792]{1,0:T(8,128)(2,1)} %copy-done.6) | copy-start | bytes 2752516
  134.2 26.2 %copy-start.11 = (bf16[256,1792]{1,0:T(8,128)(2,1)S(1)}, bf16[256,1792]{1,0:T(8,128)(2,1)}, u32[]{:S(2)}) copy-start(bf16[256,1792]{1,0:T(8,128)(2,1)} %copy-done.9) | copy-start | bytes 2752516
  136.4 39.7 %collective-permute-start.27 = (bf16[256,1792]{1,0:T(8,128)(2,1)}, bf16[256,1792]{1,0:T(8,128)(2,1)}, u32[]{:S(2)}, u32[]{:S(2)}) collective-permute-start(bf16[256,1792]{1,0:T(8,128)(2,1)} %add.137), channel_id=1, source_target_pairs={{0,1},{1,0},{2,3},{3,2},{4,5},{5,4},{6,7},{7,6},{8,9},{9,8},{10,11... | collective-permute-start | bytes 2752520 | tf_op jit(solution)/shard_map/ppermute | solution.py:45
  140.6 35.5 %collective-permute-start.26 = (bf16[256,1792]{1,0:T(8,128)(2,1)}, bf16[256,1792]{1,0:T(8,128)(2,1)}, u32[]{:S(2)}, u32[]{:S(2)}) collective-permute-start(bf16[256,1792]{1,0:T(8,128)(2,1)} %get-tuple-element.114), channel_id=1, source_target_pairs={{0,6},{1,7},{2,4},{3,5},{4,2},{5,3},{6,0},{7,1},{8,10},{9,11},{10,... | collective-permute-start | bytes 2752520 | tf_op jit(solution)/shard_map/ppermute | solution.py:45
  155.2 20.9 %collective-permute-start.25 = (bf16[144,1792]{1,0:T(8,128)(2,1)S(1)}, bf16[144,1792]{1,0:T(8,128)(2,1)S(1)}, u32[]{:S(2)}, u32[]{:S(2)}) collective-permute-start(bf16[144,1792]{1,0:T(8,128)(2,1)S(1)} %get-tuple-element.112.sent_ref), channel_id=1, source_target_pairs={{0,2},{1,3},{2,0},{3,1},{4,6},{5,7},{6,4},{7,5},{8,14},{9,15},{10,... | collective-permute-start | bytes 1548296 | tf_op jit(solution)/shard_map/ppermute | solution.py:45
  159.5 16.6 %collective-permute-start.23 = (bf16[128,1792]{1,0:T(8,128)(2,1)S(1)}, bf16[128,1792]{1,0:T(8,128)(2,1)S(1)}, u32[]{:S(2)}, u32[]{:S(2)}) collective-permute-start(bf16[128,1792]{1,0:T(8,128)(2,1)S(1)} %get-tuple-element.107), channel_id=1, source_target_pairs={{0,2},{1,3},{2,0},{3,1},{4,6},{5,7},{6,4},{7,5},{8,14},{9,15},{10,... | collective-permute-start | bytes 1376264 | tf_op jit(solution)/shard_map/ppermute | solution.py:45
  159.6 10.9 %collective-permute-start.24 = (bf16[1,256,256]{2,1,0:T(8,128)(2,1)S(1)}, bf16[1,256,256]{2,1,0:T(8,128)(2,1)S(1)}, u32[]{:S(2)}, u32[]{:S(2)}) collective-permute-start(bf16[1,256,256]{2,1,0:T(8,128)(2,1)S(1)} %get-tuple-element.104), channel_id=1, source_target_pairs={{0,64},{1,65},{2,66},{3,67},{4,68},{5,69},{6,70},{7,71},{8,72},{9,... | collective-permute-start | bytes 393224 | tf_op jit(solution)/shard_map/ppermute | solution.py:45
  (31 other events, 214.8 us)

commit v5 on v4

--- a/solution.py
+++ b/solution.py
@@ -582,12 +582,12 @@
         which, turned, after(g, o_mate), 4, 4, F32
     )
 
-    part_p = context_term(at, after(g, x_self_own), 768, blocks, BF16, 1)
+
+    x_mate = add_x(which, x_mate_own, x_mate_away, after(x_mate_z, x_self_own, o_mate_z))
+    x_from_mate = [send(piece, TO_MATE) for piece in x_mate]
+    part_p = context_term(at, after(g, x_mate[0]), 768, blocks, BF16, 1)
     got_low = send(part_p, TO_PARTNER)
-
-    x_mate = add_x(which, x_mate_own, x_mate_away, after(x_mate_z, part_p, o_mate_z))
-    x_from_mate = [send(piece, TO_MATE) for piece in x_mate]
-    o_self_z = add(which, after(o_self_z_own, x_mate[0]), o_mate_z)
+    o_self_z = add(which, after(o_self_z_own, part_p), o_mate_z)
     o_from_z = send(o_self_z, TO_Z)
     x3_got = send(x3_away, TO_X3)
     zlo_away, zlo_kept = outer_sum(zlo_at, after(x3_kept, o_self_z), x3_got, turned=True)

time: 181 us -> 187 us (1.033)
  waiting for transfers between devices: 53.2 us -> 58.3 us
    ppermute x28, waiting for transfers between devices: 53.2 us -> 58.3 us  [send(): return lax.ppermute(value, BOTH, pairs)]
  transfers between devices with their start and end apart: 28 -> 28, of which waited for: 14 -> 14; matrix products, arithmetic and copies ran while one was open for 3% -> 3% of each run, Pallas kernels for 32% -> 31%
where the time goes in v5:
time: 187 us; the launch traced here: 186 us
  Pallas kernels  70.1 us (37%)
  waiting for transfers between devices  58.3 us (31%)
  starting transfers between devices  40.3 us (22%)
  local copies, waits for them, and re-layouts  15.5 us (8%)
    pallas_call x20, Pallas kernels, run(): return built(at, *placed)  70.1 us
    ppermute x28, waiting for transfers between devices, send(): return lax.ppermute(value, BOTH, pairs)  58.3 us
    ppermute x28, starting transfers between devices, send(): return lax.ppermute(value, BOTH, pairs)  40.3 us
    unnamed x70, local copies, waits for them, and re-layouts  10.8 us
  transfers between devices with their start and end apart: 28, of which 14 were waited for; matrix products, arithmetic and copies ran while one was open for 3% of the time, Pallas kernels for 31%

profile of v5, /device:TPU:1, one launch (start us, length us, event | category | flops | bytes accessed | tf_op | source)
XLA Modules:
  0.0 186.4 jit_solution(5988704793700024506)
XLA Ops:
  2.4 4.5 %collective-permute-start.3 = (bf16[256,1792]{1,0:T(8,128)(2,1)S(1)}, bf16[256,1792]{1,0:T(8,128)(2,1)S(1)}, u32[]{:S(2)}, u32[]{:S(2)}) collective-permute-start(bf16[256,1792]{1,0:T(8,128)(2,1)S(1)} %get-tuple-element.61.refs_0_.refs_2_), channel_id=1, source_target_pairs={{0,1},{1,0},{2,3},{3,2},{4,5},{5,4},{6,7},{7,6},{8,9},{9,8},{10,11... | collective-permute-start | bytes 2752520 | tf_op jit(solution)/shard_map/ppermute | solution.py:45
  8.2 2.1 %split.3 = (bf16[512,1792]{1,0:T(8,128)(2,1)S(1)}, bf16[512,1792]{1,0:T(8,128)(2,1)S(1)}) custom-call(s32[1]{0:T(128)} %bitcast.at_ref.refs_0_, bf16[512,3584]{1,0:T(8,128)(2,1)} %in_ref), custom_call_target="tpu_custom_call" | custom-call | bytes 6000000 | tf_op jit(solution)/shard_map/split/pallas_call | solution.py:82
  12.8 3.5 %outer_parts.1 = (bf16[4,256,256]{2,1,0:T(8,128)(2,1)S(1)}, bf16[4,256,256]{2,1,0:T(8,128)(2,1)S(1)}, f32[8,256,256]{2,1,0:T(8,128)S(1)}) custom-call(s32[1]{0:T(128)} %bitcast.9.at_ref, f32[256,3584]{1,0:T(8,128)} %bitcast.48), custom_call_target="tpu_custom_call" | custom-call | bytes 9000000 | tf_op jit(solution)/shard_map/outer_parts/pallas_call | solution.py:82
  24.3 2.7 %collective-permute-done.3.refs_3_.refs_5_ = bf16[256,1792]{1,0:T(8,128)(2,1)S(1)} collective-permute-done((bf16[256,1792]{1,0:T(8,128)(2,1)S(1)}, bf16[256,1792]{1,0:T(8,128)(2,1)S(1)}, u32[]{:S(2)}, u32[]{:S(2)}) %collective-permute-start.3) | collective-permute-done | bytes 917536 | tf_op jit(solution)/shard_map/ppermute | solution.py:45
  27.9 2.6 %collective-permute-start.8 = (bf16[256,1792]{1,0:T(8,128)(2,1)S(1)}, bf16[256,1792]{1,0:T(8,128)(2,1)}, u32[]{:S(2)}, u32[]{:S(2)}) collective-permute-start(bf16[256,1792]{1,0:T(8,128)(2,1)S(1)} %collective-permute-done.2.refs_1_.refs_3_), channel_id=1, source_target_pairs={{0,1},{1,0},{2,3},{3,2},{4,5},{5,4},{6,7},{7,6},{8,9},{9,8},{10,11... | collective-permute-start | bytes 2752520 | tf_op jit(solution)/shard_map/ppermute | solution.py:45
  32.1 2.4 %collective-permute-start.1 = (bf16[256,2048]{1,0:T(8,128)(2,1)}, bf16[256,2048]{1,0:T(8,128)(2,1)}, u32[]{:S(2)}, u32[]{:S(2)}) collective-permute-start(bf16[256,2048]{1,0:T(8,128)(2,1)} %get-tuple-element.65), channel_id=1, source_target_pairs={{0,2},{1,3},{2,0},{3,1},{4,6},{5,7},{6,4},{7,5},{8,14},{9,15},{10,... | collective-permute-start | bytes 3145736 | tf_op jit(solution)/shard_map/ppermute | solution.py:45
  34.5 3.0 %fusion.5 = (bf16[256,1792]{1,0:T(8,128)(2,1)}, bf16[256,1792]{1,0:T(8,128)(2,1)}) fusion(bf16[512,1792]{1,0:T(8,128)(2,1)} %copy-done.16), kind=kLoop, calls=%fused_computation.9 | loop fusion | bytes 3670016 | tf_op jit(solution)/shard_map/slice | solution.py:562
  37.5 12.7 %collective-permute-done.8.refs_5_.refs_7_ = bf16[256,1792]{1,0:T(8,128)(2,1)} collective-permute-done((bf16[256,1792]{1,0:T(8,128)(2,1)S(1)}, bf16[256,1792]{1,0:T(8,128)(2,1)}, u32[]{:S(2)}, u32[]{:S(2)}) %collective-permute-start.8) | collective-permute-done | bytes 917536 | tf_op jit(solution)/shard_map/ppermute | solution.py:45
  55.0 2.7 %collective-permute-start.11 = (bf16[256,1792]{1,0:T(8,128)(2,1)}, bf16[256,1792]{1,0:T(8,128)(2,1)}, u32[]{:S(2)}, u32[]{:S(2)}) collective-permute-start(bf16[256,1792]{1,0:T(8,128)(2,1)} %get-tuple-element.81), channel_id=1, source_target_pairs={{0,2},{1,3},{2,0},{3,1},{4,6},{5,7},{6,4},{7,5},{8,14},{9,15},{10,... | collective-permute-start | bytes 2752520 | tf_op jit(solution)/shard_map/ppermute | solution.py:45
  57.7 6.5 %collective-permute-done.1.low_ref = bf16[256,2048]{1,0:T(8,128)(2,1)} collective-permute-done((bf16[256,2048]{1,0:T(8,128)(2,1)}, bf16[256,2048]{1,0:T(8,128)(2,1)}, u32[]{:S(2)}, u32[]{:S(2)}) %collective-permute-start.1) | collective-permute-done | bytes 1048608 | tf_op jit(solution)/shard_map/ppermute | solution.py:45
  65.7 3.6 %turn.1 = (bf16[2048,1024]{1,0:T(8,128)(2,1)S(1)}, bf16[1024,256]{1,0:T(8,128)(2,1)S(1)}) custom-call(s32[8]{0:T(128)S(1)} %stack.91.at_ref, bf16[512,2048]{1,0:T(8,128)(2,1)S(1)} %copy-done.2, bf16[256,2048]{1,0:T(8,128)(2,1)} %collective-permute-done.high_ref, bf16[256,2048]{1,0:T(8,128)(2,1)} %collective-permute-done.1.low_ref), custom_call_target="tpu_custom_call" | custom-call | bytes 12000000 | tf_op jit(solution)/shard_map/turn/pallas_call | solution.py:82
  69.8 10.1 %project.1.acc_ref = f32[1024,1792]{1,0:T(8,128)S(1)} custom-call(s32[9]{0:T(128)S(1)} %stack.90.at_ref.refs_0_, bf16[512,2048]{1,0:T(8,128)(2,1)S(1)} %copy-done.2, bf16[256,2048]{1,0:T(8,128)(2,1)} %collective-permute-done.high_ref, bf16[256,2048]{1,0:T(8,128)(2,1)} %collective-permute-done.1.low_ref, bf16[256,1792]{1,0:T(8,128)(2,1)S(1)} %copy-done.4, ...), custom_call_target="tpu_custom_call" | custom-call | bytes 42000000 | tf_op jit(solution)/shard_map/project/pallas_call | solution.py:82
  79.9 9.4 %collective-permute-done.10.block_ref.refs_9_ = bf16[256,1792]{1,0:T(8,128)(2,1)S(1)} collective-permute-done((bf16[256,1792]{1,0:T(8,128)(2,1)}, bf16[256,1792]{1,0:T(8,128)(2,1)S(1)}, u32[]{:S(2)}, u32[]{:S(2)}) %collective-permute-start.10) | collective-permute-done | bytes 917536 | tf_op jit(solution)/shard_map/ppermute | solution.py:45
  89.4 4.1 %row_stats.1.mine_ref = f32[8,8,128]{2,1,0:T(8,128)S(1)} custom-call(s32[9]{0:T(128)S(1)} %stack.90.at_ref.refs_0_, f32[1024,1792]{1,0:T(8,128)S(1)} %project.1.acc_ref, bf16[1024,256]{1,0:T(8,128)(2,1)S(1)} %get-tuple-element.79.slab_ref, bf16[256,1792]{1,0:T(8,128)(2,1)S(1)} %collective-permute-done.10.block_ref.refs_9_, bf16[512,1792]{1,0:T(8,128)(2,1)S(1)} %copy-done.13, ...), custom_call_target="tpu_custom_call" | custom-call | bytes 9000000 | tf_op jit(solution)/shard_map/row_stats/pallas_call | solution.py:82
  93.5 3.0 %collective-permute-start.13 = (f32[8,8,128]{2,1,0:T(8,128)S(1)}, f32[8,8,128]{2,1,0:T(8,128)S(1)}, u32[]{:S(2)}, u32[]{:S(2)}) collective-permute-start(f32[8,8,128]{2,1,0:T(8,128)S(1)} %row_stats.1.mine_ref), channel_id=1, source_target_pairs={{0,2},{1,3},{2,0},{3,1},{4,6},{5,7},{6,4},{7,5},{8,14},{9,15},{10,... | collective-permute-start | bytes 98312 | tf_op jit(solution)/shard_map/ppermute | solution.py:45
  98.0 6.1 %grad_step.1 = (bf16[1024,1792]{1,0:T(8,128)(2,1)S(1)}, bf16[272,1792]{1,0:T(8,128)(2,1)S(1)}, bf16[256,1792]{1,0:T(8,128)(2,1)S(1)}) custom-call(s32[9]{0:T(128)S(1)} %stack.90.at_ref.refs_0_, f32[1024,1792]{1,0:T(8,128)S(1)} %project.1.acc_ref, bf16[1024,256]{1,0:T(8,128)(2,1)S(1)} %get-tuple-element.79.slab_ref, ...), custom_call_target="tpu_custom_call" | custom-call | bytes 18000000 | tf_op jit(solution)/shard_map/grad_step/pallas_call | solution.py:82
  104.1 2.4 %collective-permute-start.15 = (bf16[272,1792]{1,0:T(8,128)(2,1)S(1)}, bf16[272,1792]{1,0:T(8,128)(2,1)S(1)}, u32[]{:S(2)}, u32[]{:S(2)}) collective-permute-start(bf16[272,1792]{1,0:T(8,128)(2,1)S(1)} %get-tuple-element.94.refs_0_), channel_id=1, source_target_pairs={{0,1},{1,0},{2,3},{3,2},{4,5},{5,4},{6,7},{7,6},{8,9},{9,8},{10,11... | collective-permute-start | bytes 2924552 | tf_op jit(solution)/shard_map/ppermute | solution.py:45
  106.5 4.7 %context_term.3 = bf16[256,2048]{1,0:T(8,128)(2,1)S(1)} custom-call(s32[9]{0:T(128)S(1)} %stack.90.at_ref.refs_0_, bf16[1024,1792]{1,0:T(8,128)(2,1)S(1)} %get-tuple-element.108.refs_1_.refs_2_, bf16[256,1792]{1,0:T(8,128)(2,1)S(1)} %copy-done.4, bf16[256,1792]{1,0:T(8,128)(2,1)S(1)} %copy-done.10, bf16[256,1792]{1,0:T(8,128)(2,1)} %collective-permute-done.6.refs_2_.refs_4_, ...), custom_call_target="tpu_custom_call" | custom-call | bytes 7500000 | tf_op jit(solution)/shard_map/context_term/pallas_call | solution.py:82
  111.2 2.8 %collective-permute-start.21 = (bf16[256,2048]{1,0:T(8,128)(2,1)S(1)}, bf16[256,2048]{1,0:T(8,128)(2,1)S(1)}, u32[]{:S(2)}, u32[]{:S(2)}) collective-permute-start(bf16[256,2048]{1,0:T(8,128)(2,1)S(1)} %context_term.3), channel_id=1, source_target_pairs={{0,2},{1,3},{2,0},{3,1},{4,6},{5,7},{6,4},{7,5},{8,14},{9,15},{10,... | collective-permute-start | bytes 3145736 | tf_op jit(solution)/shard_map/ppermute | solution.py:45
  114.0 3.3 %weight_terms.2 = (bf16[256,1792]{1,0:T(8,128)(2,1)}, bf16[256,1792]{1,0:T(8,128)(2,1)}) custom-call(s32[1]{0:T(128)} %bitcast.at_ref.refs_0_, bf16[2048,1024]{1,0:T(8,128)(2,1)S(1)} %get-tuple-element.66.turned_ref.refs_1_, bf16[1024,1792]{1,0:T(8,128)(2,1)S(1)} %get-tuple-element.108.refs_1_.refs_2_), custom_call_target="tpu_custom_call" | custom-call | bytes 6000000 | tf_op jit(solution)/shard_map/weight_terms/pallas_call | solution.py:82
  117.3 4.0 %weight_terms.3 = (f32[256,1792]{1,0:T(8,128)S(1)}, f32[256,1792]{1,0:T(8,128)S(1)}, f32[256,1792]{1,0:T(8,128)S(1)}, f32[256,1792]{1,0:T(8,128)S(1)}) custom-call(s32[1]{0:T(128)} %bitcast.at_ref.refs_0_, bf16[2048,1024]{1,0:T(8,128)(2,1)S(1)} %get-tuple-element.66.turned_ref.refs_1_, bf16[1024,1792]{1,0:T(8,128)(2,1)S(1)} %get-tuple-element.108.refs_1_.refs_2_), custom_call_target="tpu_custom_call" | custom-call | bytes 12000000 | tf_op jit(solution)/shard_map/weight_terms/pallas_call | solution.py:82
  121.3 5.6 %collective-permute-done.15.refs_1_ = bf16[272,1792]{1,0:T(8,128)(2,1)S(1)} collective-permute-done((bf16[272,1792]{1,0:T(8,128)(2,1)S(1)}, bf16[272,1792]{1,0:T(8,128)(2,1)S(1)}, u32[]{:S(2)}, u32[]{:S(2)}) %collective-permute-start.15) | collective-permute-done | bytes 974880 | tf_op jit(solution)/shard_map/ppermute | solution.py:45
  127.9 5.7 %context_term.4 = bf16[256,2048]{1,0:T(8,128)(2,1)} custom-call(s32[9]{0:T(128)S(1)} %stack.90.at_ref.refs_0_, bf16[1024,1792]{1,0:T(8,128)(2,1)S(1)} %get-tuple-element.108.refs_1_.refs_2_, bf16[256,1792]{1,0:T(8,128)(2,1)S(1)} %copy-done.4, bf16[256,1792]{1,0:T(8,128)(2,1)S(1)} %copy-done.10, bf16[256,1792]{1,0:T(8,128)(2,1)} %collective-permute-done.6.refs_2_.refs_4_, ...), custom_call_target="tpu_custom_call" | custom-call | bytes 7500000 | tf_op jit(solution)/shard_map/context_term/pallas_call | solution.py:82
  133.6 2.3 %collective-permute-start.22 = (bf16[256,2048]{1,0:T(8,128)(2,1)}, bf16[256,2048]{1,0:T(8,128)(2,1)}, u32[]{:S(2)}, u32[]{:S(2)}) collective-permute-start(bf16[256,2048]{1,0:T(8,128)(2,1)} %context_term.4), channel_id=1, source_target_pairs={{0,2},{1,3},{2,0},{3,1},{4,6},{5,7},{6,4},{7,5},{8,14},{9,15},{10,... | collective-permute-start | bytes 3145736 | tf_op jit(solution)/shard_map/ppermute | solution.py:45
  137.9 2.5 %collective-permute-start.18 = (bf16[2,256,256]{2,1,0:T(8,128)(2,1)S(1)}, bf16[2,256,256]{2,1,0:T(8,128)(2,1)S(1)}, u32[]{:S(2)}, u32[]{:S(2)}) collective-permute-start(bf16[2,256,256]{2,1,0:T(8,128)(2,1)S(1)} %get-tuple-element.86), channel_id=1, source_target_pairs={{0,48},{1,49},{2,50},{3,51},{4,52},{5,53},{6,54},{7,55},{8,56},{9,... | collective-permute-start | bytes 786440 | tf_op jit(solution)/shard_map/ppermute | solution.py:45
  145.5 4.3 %collective-permute-done.17.refs_1_ = bf16[128,1792]{1,0:T(8,128)(2,1)S(1)} collective-permute-done((bf16[128,1792]{1,0:T(8,128)(2,1)S(1)}, bf16[128,1792]{1,0:T(8,128)(2,1)S(1)}, u32[]{:S(2)}, u32[]{:S(2)}) %collective-permute-start.17) | collective-permute-done | bytes 458784 | tf_op jit(solution)/shard_map/ppermute | solution.py:45
  151.7 5.6 %collective-permute-done.20.refs_3_ = bf16[256,1792]{1,0:T(8,128)(2,1)} collective-permute-done((bf16[256,1792]{1,0:T(8,128)(2,1)}, bf16[256,1792]{1,0:T(8,128)(2,1)}, u32[]{:S(2)}, u32[]{:S(2)}) %collective-permute-start.20) | collective-permute-done | bytes 917536 | tf_op jit(solution)/shard_map/ppermute | solution.py:45
  157.3 3.6 %collective-permute-done.19.refs_2_ = bf16[144,1792]{1,0:T(8,128)(2,1)} collective-permute-done((bf16[144,1792]{1,0:T(8,128)(2,1)}, bf16[144,1792]{1,0:T(8,128)(2,1)}, u32[]{:S(2)}, u32[]{:S(2)}) %collective-permute-start.19) | collective-permute-done | bytes 516128 | tf_op jit(solution)/shard_map/ppermute | solution.py:45
  165.3 2.7 %collective-permute-start.23 = (bf16[128,1792]{1,0:T(8,128)(2,1)S(1)}, bf16[128,1792]{1,0:T(8,128)(2,1)S(1)}, u32[]{:S(2)}, u32[]{:S(2)}) collective-permute-start(bf16[128,1792]{1,0:T(8,128)(2,1)S(1)} %get-tuple-element.107), channel_id=1, source_target_pairs={{0,2},{1,3},{2,0},{3,1},{4,6},{5,7},{6,4},{7,5},{8,14},{9,15},{10,... | collective-permute-start | bytes 1376264 | tf_op jit(solution)/shard_map/ppermute | solution.py:45
  168.7 6.7 %context_term.5.a_ref = f32[512,2048]{1,0:T(8,128)S(1)} custom-call(s32[9]{0:T(128)S(1)} %stack.90.at_ref.refs_0_, bf16[1024,1792]{1,0:T(8,128)(2,1)S(1)} %copy-done.1, bf16[256,1792]{1,0:T(8,128)(2,1)S(1)} %copy-done.5, bf16[256,1792]{1,0:T(8,128)(2,1)S(1)} %copy-done.11, bf16[256,1792]{1,0:T(8,128)(2,1)} %collective-permute-done.6.refs_2_.refs_4_, ...), custom_call_target="tpu_custom_call" | custom-call | bytes 15000000 | tf_op jit(solution)/shard_map/context_term/pallas_call | solution.py:82
  175.5 3.4 %end_context.1 = bf16[512,2048]{1,0:T(8,128)(2,1)} custom-call(s32[1]{0:T(128)} %bitcast.at_ref.refs_0_, f32[512,2048]{1,0:T(8,128)S(1)} %context_term.5.a_ref, bf16[256,2048]{1,0:T(8,128)(2,1)S(1)} %copy-done.22, bf16[256,2048]{1,0:T(8,128)(2,1)} %collective-permute-done.22.c_ref), custom_call_target="tpu_custom_call" | custom-call | bytes 6000000 | tf_op jit(solution)/shard_map/end_context/pallas_call | solution.py:82
  181.6 4.5 %finish.1 = (f32[256,3584]{1,0:T(8,128)}, f32[1,3584]{1,0:T(1,128)}) custom-call(s32[9]{0:T(128)S(1)} %stack.90.at_ref.refs_0_, bf16[128,1792]{1,0:T(8,128)(2,1)S(1)} %collective-permute-done.23.high_ref, bf16[144,1792]{1,0:T(8,128)(2,1)S(1)} %collective-permute-done.25.low_ref, bf16[144,1792]{1,0:T(8,128)(2,1)S(1)} %get-tuple-element.112.sent_ref, ...), custom_call_target="tpu_custom_call" | custom-call | bytes 6000000 | tf_op jit(solution)/shard_map/finish/pallas_call | solution.py:82
  (121 shorter events, 42.1 us)
Async XLA Ops:
  2.4 24.6 %collective-permute-start.3 = (bf16[256,1792]{1,0:T(8,128)(2,1)S(1)}, bf16[256,1792]{1,0:T(8,128)(2,1)S(1)}, u32[]{:S(2)}, u32[]{:S(2)}) collective-permute-start(bf16[256,1792]{1,0:T(8,128)(2,1)S(1)} %get-tuple-element.61.refs_0_.refs_2_), channel_id=1, source_target_pairs={{0,1},{1,0},{2,3},{3,2},{4,5},{5,4},{6,7},{7,6},{8,9},{9,8},{10,11... | collective-permute-start | bytes 2752520 | tf_op jit(solution)/shard_map/ppermute | solution.py:45
  6.9 21.0 %collective-permute-start.2 = (bf16[256,1792]{1,0:T(8,128)(2,1)S(1)}, bf16[256,1792]{1,0:T(8,128)(2,1)S(1)}, u32[]{:S(2)}, u32[]{:S(2)}) collective-permute-start(bf16[256,1792]{1,0:T(8,128)(2,1)S(1)} %get-tuple-element.61.refs_0_.refs_2_), channel_id=1, source_target_pairs={{0,6},{1,7},{2,4},{3,5},{4,2},{5,3},{6,0},{7,1},{8,10},{9,11},{10,... | collective-permute-start | bytes 2752520 | tf_op jit(solution)/shard_map/ppermute | solution.py:45
  17.7 14.0 %collective-permute-start.6 = (bf16[256,1792]{1,0:T(8,128)(2,1)S(1)}, bf16[256,1792]{1,0:T(8,128)(2,1)}, u32[]{:S(2)}, u32[]{:S(2)}) collective-permute-start(bf16[256,1792]{1,0:T(8,128)(2,1)S(1)} %get-tuple-element.73), channel_id=1, source_target_pairs={{0,2},{1,3},{2,0},{3,1},{4,6},{5,7},{6,4},{7,5},{8,14},{9,15},{10,... | collective-permute-start | bytes 2752520 | tf_op jit(solution)/shard_map/ppermute | solution.py:45
  19.6 4.7 %collective-permute-start.5 = (bf16[4,256,256]{2,1,0:T(8,128)(2,1)S(1)}, bf16[4,256,256]{2,1,0:T(8,128)(2,1)S(1)}, u32[]{:S(2)}, u32[]{:S(2)}) collective-permute-start(bf16[4,256,256]{2,1,0:T(8,128)(2,1)S(1)} %get-tuple-element.63), channel_id=1, source_target_pairs={{0,8},{1,9},{2,10},{3,11},{4,12},{5,13},{6,14},{7,15},{8,0},{9,1},... | collective-permute-start | bytes 1572872 | tf_op jit(solution)/shard_map/ppermute | solution.py:45
  20.4 2.3 %collective-permute-start.4 = (bf16[4,256,256]{2,1,0:T(8,128)(2,1)S(1)}, bf16[4,256,256]{2,1,0:T(8,128)(2,1)S(1)}, u32[]{:S(2)}, u32[]{:S(2)}) collective-permute-start(bf16[4,256,256]{2,1,0:T(8,128)(2,1)S(1)} %get-tuple-element.68), channel_id=1, source_target_pairs={{0,8},{1,9},{2,10},{3,11},{4,12},{5,13},{6,14},{7,15},{8,0},{9,1},... | collective-permute-start | bytes 1572872 | tf_op jit(solution)/shard_map/ppermute | solution.py:45
  23.5 29.1 %collective-permute-start = (bf16[256,2048]{1,0:T(8,128)(2,1)}, bf16[256,2048]{1,0:T(8,128)(2,1)}, u32[]{:S(2)}, u32[]{:S(2)}) collective-permute-start(bf16[256,2048]{1,0:T(8,128)(2,1)} %get-tuple-element.64), channel_id=1, source_target_pairs={{0,2},{1,3},{2,0},{3,1},{4,6},{5,7},{6,4},{7,5},{8,14},{9,15},{10,... | collective-permute-start | bytes 3145736 | tf_op jit(solution)/shard_map/ppermute | solution.py:45
  27.9 23.8 %copy-start.9 = (bf16[256,1792]{1,0:T(8,128)(2,1)}, bf16[256,1792]{1,0:T(8,128)(2,1)S(1)}, u32[]{:S(2)}) copy-start(bf16[256,1792]{1,0:T(8,128)(2,1)S(1)} %collective-permute-done.2.refs_1_.refs_3_) | copy-start | bytes 2752516
  27.9 22.2 %collective-permute-start.8 = (bf16[256,1792]{1,0:T(8,128)(2,1)S(1)}, bf16[256,1792]{1,0:T(8,128)(2,1)}, u32[]{:S(2)}, u32[]{:S(2)}) collective-permute-start(bf16[256,1792]{1,0:T(8,128)(2,1)S(1)} %collective-permute-done.2.refs_1_.refs_3_), channel_id=1, source_target_pairs={{0,1},{1,0},{2,3},{3,2},{4,5},{5,4},{6,7},{7,6},{8,9},{9,8},{10,11... | collective-permute-start | bytes 2752520 | tf_op jit(solution)/shard_map/ppermute | solution.py:45
  31.7 22.7 %collective-permute-start.7 = (bf16[256,1792]{1,0:T(8,128)(2,1)}, bf16[256,1792]{1,0:T(8,128)(2,1)}, u32[]{:S(2)}, u32[]{:S(2)}) collective-permute-start(bf16[256,1792]{1,0:T(8,128)(2,1)} %collective-permute-done.6.refs_2_.refs_4_), channel_id=1, source_target_pairs={{0,6},{1,7},{2,4},{3,5},{4,2},{5,3},{6,0},{7,1},{8,10},{9,11},{10,... | collective-permute-start | bytes 2752520 | tf_op jit(solution)/shard_map/ppermute | solution.py:45
  32.1 32.2 %collective-permute-start.1 = (bf16[256,2048]{1,0:T(8,128)(2,1)}, bf16[256,2048]{1,0:T(8,128)(2,1)}, u32[]{:S(2)}, u32[]{:S(2)}) collective-permute-start(bf16[256,2048]{1,0:T(8,128)(2,1)} %get-tuple-element.65), channel_id=1, source_target_pairs={{0,2},{1,3},{2,0},{3,1},{4,6},{5,7},{6,4},{7,5},{8,14},{9,15},{10,... | collective-permute-start | bytes 3145736 | tf_op jit(solution)/shard_map/ppermute | solution.py:45
  37.5 32.3 %collective-permute-start.9 = (bf16[256,1792]{1,0:T(8,128)(2,1)}, bf16[256,1792]{1,0:T(8,128)(2,1)}, u32[]{:S(2)}, u32[]{:S(2)}) collective-permute-start(bf16[256,1792]{1,0:T(8,128)(2,1)} %collective-permute-done.6.refs_2_.refs_4_), channel_id=1, source_target_pairs={{0,1},{1,0},{2,3},{3,2},{4,5},{5,4},{6,7},{7,6},{8,9},{9,8},{10,11... | collective-permute-start | bytes 2752520 | tf_op jit(solution)/shard_map/ppermute | solution.py:45
  54.4 34.9 %collective-permute-start.10 = (bf16[256,1792]{1,0:T(8,128)(2,1)}, bf16[256,1792]{1,0:T(8,128)(2,1)S(1)}, u32[]{:S(2)}, u32[]{:S(2)}) collective-permute-start(bf16[256,1792]{1,0:T(8,128)(2,1)} %collective-permute-done.7.refs_4_.refs_6_), channel_id=1, source_target_pairs={{0,1},{1,0},{2,3},{3,2},{4,5},{5,4},{6,7},{7,6},{8,9},{9,8},{10,11... | collective-permute-start | bytes 2752520 | tf_op jit(solution)/shard_map/ppermute | solution.py:45
  55.0 34.4 %collective-permute-start.11 = (bf16[256,1792]{1,0:T(8,128)(2,1)}, bf16[256,1792]{1,0:T(8,128)(2,1)}, u32[]{:S(2)}, u32[]{:S(2)}) collective-permute-start(bf16[256,1792]{1,0:T(8,128)(2,1)} %get-tuple-element.81), channel_id=1, source_target_pairs={{0,2},{1,3},{2,0},{3,1},{4,6},{5,7},{6,4},{7,5},{8,14},{9,15},{10,... | collective-permute-start | bytes 2752520 | tf_op jit(solution)/shard_map/ppermute | solution.py:45
  57.7 31.7 %collective-permute-start.12 = (bf16[256,1792]{1,0:T(8,128)(2,1)}, bf16[256,1792]{1,0:T(8,128)(2,1)}, u32[]{:S(2)}, u32[]{:S(2)}) collective-permute-start(bf16[256,1792]{1,0:T(8,128)(2,1)} %get-tuple-element.82), channel_id=1, source_target_pairs={{0,2},{1,3},{2,0},{3,1},{4,6},{5,7},{6,4},{7,5},{8,14},{9,15},{10,... | collective-permute-start | bytes 2752520 | tf_op jit(solution)/shard_map/ppermute | solution.py:45
  64.3 32.3 %collective-permute-start.14 = (bf16[4,256,256]{2,1,0:T(8,128)(2,1)}, bf16[4,256,256]{2,1,0:T(8,128)(2,1)S(1)}, u32[]{:S(2)}, u32[]{:S(2)}) collective-permute-start(bf16[4,256,256]{2,1,0:T(8,128)(2,1)} %get-tuple-element.85), channel_id=1, source_target_pairs={{0,16},{1,17},{2,18},{3,19},{4,20},{5,21},{6,22},{7,23},{8,24},{9,... | collective-permute-start | bytes 1572872 | tf_op jit(solution)/shard_map/ppermute | solution.py:45
  93.5 4.5 %collective-permute-start.13 = (f32[8,8,128]{2,1,0:T(8,128)S(1)}, f32[8,8,128]{2,1,0:T(8,128)S(1)}, u32[]{:S(2)}, u32[]{:S(2)}) collective-permute-start(f32[8,8,128]{2,1,0:T(8,128)S(1)} %row_stats.1.mine_ref), channel_id=1, source_target_pairs={{0,2},{1,3},{2,0},{3,1},{4,6},{5,7},{6,4},{7,5},{8,14},{9,15},{10,... | collective-permute-start | bytes 98312 | tf_op jit(solution)/shard_map/ppermute | solution.py:45
  104.1 23.8 %copy-start = (bf16[1024,1792]{1,0:T(8,128)(2,1)}, bf16[1024,1792]{1,0:T(8,128)(2,1)S(1)}, u32[]{:S(2)}) copy-start(bf16[1024,1792]{1,0:T(8,128)(2,1)S(1)} %get-tuple-element.108.refs_1_.refs_2_) | copy-start | bytes 11010052
  104.1 22.8 %collective-permute-start.15 = (bf16[272,1792]{1,0:T(8,128)(2,1)S(1)}, bf16[272,1792]{1,0:T(8,128)(2,1)S(1)}, u32[]{:S(2)}, u32[]{:S(2)}) collective-permute-start(bf16[272,1792]{1,0:T(8,128)(2,1)S(1)} %get-tuple-element.94.refs_0_), channel_id=1, source_target_pairs={{0,1},{1,0},{2,3},{3,2},{4,5},{5,4},{6,7},{7,6},{8,9},{9,8},{10,11... | collective-permute-start | bytes 2924552 | tf_op jit(solution)/shard_map/ppermute | solution.py:45
  106.5 14.7 %collective-permute-start.16 = (bf16[256,1792]{1,0:T(8,128)(2,1)S(1)}, bf16[256,1792]{1,0:T(8,128)(2,1)S(1)}, u32[]{:S(2)}, u32[]{:S(2)}) collective-permute-start(bf16[256,1792]{1,0:T(8,128)(2,1)S(1)} %get-tuple-element.95), channel_id=1, source_target_pairs={{0,6},{1,7},{2,4},{3,5},{4,2},{5,3},{6,0},{7,1},{8,10},{9,11},{10,... | collective-permute-start | bytes 2752520 | tf_op jit(solution)/shard_map/ppermute | solution.py:45
  111.2 29.1 %collective-permute-start.21 = (bf16[256,2048]{1,0:T(8,128)(2,1)S(1)}, bf16[256,2048]{1,0:T(8,128)(2,1)S(1)}, u32[]{:S(2)}, u32[]{:S(2)}) collective-permute-start(bf16[256,2048]{1,0:T(8,128)(2,1)S(1)} %context_term.3), channel_id=1, source_target_pairs={{0,2},{1,3},{2,0},{3,1},{4,6},{5,7},{6,4},{7,5},{8,14},{9,15},{10,... | collective-permute-start | bytes 3145736 | tf_op jit(solution)/shard_map/ppermute | solution.py:45
  133.6 34.4 %collective-permute-start.22 = (bf16[256,2048]{1,0:T(8,128)(2,1)}, bf16[256,2048]{1,0:T(8,128)(2,1)}, u32[]{:S(2)}, u32[]{:S(2)}) collective-permute-start(bf16[256,2048]{1,0:T(8,128)(2,1)} %context_term.4), channel_id=1, source_target_pairs={{0,2},{1,3},{2,0},{3,1},{4,6},{5,7},{6,4},{7,5},{8,14},{9,15},{10,... | collective-permute-start | bytes 3145736 | tf_op jit(solution)/shard_map/ppermute | solution.py:45
  135.8 21.5 %collective-permute-start.20 = (bf16[256,1792]{1,0:T(8,128)(2,1)}, bf16[256,1792]{1,0:T(8,128)(2,1)}, u32[]{:S(2)}, u32[]{:S(2)}) collective-permute-start(bf16[256,1792]{1,0:T(8,128)(2,1)} %get-tuple-element.106), channel_id=1, source_target_pairs={{0,1},{1,0},{2,3},{3,2},{4,5},{5,4},{6,7},{7,6},{8,9},{9,8},{10,11... | collective-permute-start | bytes 2752520 | tf_op jit(solution)/shard_map/ppermute | solution.py:45
  137.9 12.0 %collective-permute-start.17 = (bf16[128,1792]{1,0:T(8,128)(2,1)S(1)}, bf16[128,1792]{1,0:T(8,128)(2,1)S(1)}, u32[]{:S(2)}, u32[]{:S(2)}) collective-permute-start(bf16[128,1792]{1,0:T(8,128)(2,1)S(1)} %get-tuple-element.98), channel_id=1, source_target_pairs={{0,6},{1,7},{2,4},{3,5},{4,2},{5,3},{6,0},{7,1},{8,10},{9,11},{10,... | collective-permute-start | bytes 1376264 | tf_op jit(solution)/shard_map/ppermute | solution.py:45
  137.9 6.8 %collective-permute-start.18 = (bf16[2,256,256]{2,1,0:T(8,128)(2,1)S(1)}, bf16[2,256,256]{2,1,0:T(8,128)(2,1)S(1)}, u32[]{:S(2)}, u32[]{:S(2)}) collective-permute-start(bf16[2,256,256]{2,1,0:T(8,128)(2,1)S(1)} %get-tuple-element.86), channel_id=1, source_target_pairs={{0,48},{1,49},{2,50},{3,51},{4,52},{5,53},{6,54},{7,55},{8,56},{9,... | collective-permute-start | bytes 786440 | tf_op jit(solution)/shard_map/ppermute | solution.py:45
  140.3 20.5 %collective-permute-start.19 = (bf16[144,1792]{1,0:T(8,128)(2,1)}, bf16[144,1792]{1,0:T(8,128)(2,1)}, u32[]{:S(2)}, u32[]{:S(2)}) collective-permute-start(bf16[144,1792]{1,0:T(8,128)(2,1)} %get-tuple-element.97.refs_0_), channel_id=1, source_target_pairs={{0,6},{1,7},{2,4},{3,5},{4,2},{5,3},{6,0},{7,1},{8,10},{9,11},{10,... | collective-permute-start | bytes 1548296 | tf_op jit(solution)/shard_map/ppermute | solution.py:45
  141.8 26.9 %copy-start.8 = (bf16[256,1792]{1,0:T(8,128)(2,1)S(1)}, bf16[256,1792]{1,0:T(8,128)(2,1)}, u32[]{:S(2)}) copy-start(bf16[256,1792]{1,0:T(8,128)(2,1)} %copy-done.6) | copy-start | bytes 2752516
  141.8 26.9 %copy-start.11 = (bf16[256,1792]{1,0:T(8,128)(2,1)S(1)}, bf16[256,1792]{1,0:T(8,128)(2,1)}, u32[]{:S(2)}) copy-start(bf16[256,1792]{1,0:T(8,128)(2,1)} %copy-done.9) | copy-start | bytes 2752516
  144.7 36.9 %collective-permute-start.27 = (bf16[256,1792]{1,0:T(8,128)(2,1)}, bf16[256,1792]{1,0:T(8,128)(2,1)}, u32[]{:S(2)}, u32[]{:S(2)}) collective-permute-start(bf16[256,1792]{1,0:T(8,128)(2,1)} %add.137), channel_id=1, source_target_pairs={{0,1},{1,0},{2,3},{3,2},{4,5},{5,4},{6,7},{7,6},{8,9},{9,8},{10,11... | collective-permute-start | bytes 2752520 | tf_op jit(solution)/shard_map/ppermute | solution.py:45
  150.6 31.0 %collective-permute-start.26 = (bf16[256,1792]{1,0:T(8,128)(2,1)}, bf16[256,1792]{1,0:T(8,128)(2,1)}, u32[]{:S(2)}, u32[]{:S(2)}) collective-permute-start(bf16[256,1792]{1,0:T(8,128)(2,1)} %get-tuple-element.114), channel_id=1, source_target_pairs={{0,6},{1,7},{2,4},{3,5},{4,2},{5,3},{6,0},{7,1},{8,10},{9,11},{10,... | collective-permute-start | bytes 2752520 | tf_op jit(solution)/shard_map/ppermute | solution.py:45
  165.2 16.4 %collective-permute-start.25 = (bf16[144,1792]{1,0:T(8,128)(2,1)S(1)}, bf16[144,1792]{1,0:T(8,128)(2,1)S(1)}, u32[]{:S(2)}, u32[]{:S(2)}) collective-permute-start(bf16[144,1792]{1,0:T(8,128)(2,1)S(1)} %get-tuple-element.112.sent_ref), channel_id=1, source_target_pairs={{0,2},{1,3},{2,0},{3,1},{4,6},{5,7},{6,4},{7,5},{8,14},{9,15},{10,... | collective-permute-start | bytes 1548296 | tf_op jit(solution)/shard_map/ppermute | solution.py:45
  165.3 16.3 %collective-permute-start.23 = (bf16[128,1792]{1,0:T(8,128)(2,1)S(1)}, bf16[128,1792]{1,0:T(8,128)(2,1)S(1)}, u32[]{:S(2)}, u32[]{:S(2)}) collective-permute-start(bf16[128,1792]{1,0:T(8,128)(2,1)S(1)} %get-tuple-element.107), channel_id=1, source_target_pairs={{0,2},{1,3},{2,0},{3,1},{4,6},{5,7},{6,4},{7,5},{8,14},{9,15},{10,... | collective-permute-start | bytes 1376264 | tf_op jit(solution)/shard_map/ppermute | solution.py:45
  168.0 12.8 %collective-permute-start.24 = (bf16[1,256,256]{2,1,0:T(8,128)(2,1)S(1)}, bf16[1,256,256]{2,1,0:T(8,128)(2,1)S(1)}, u32[]{:S(2)}, u32[]{:S(2)}) collective-permute-start(bf16[1,256,256]{2,1,0:T(8,128)(2,1)S(1)} %get-tuple-element.104), channel_id=1, source_target_pairs={{0,64},{1,65},{2,66},{3,67},{4,68},{5,69},{6,70},{7,71},{8,72},{9,... | collective-permute-start | bytes 393224 | tf_op jit(solution)/shard_map/ppermute | solution.py:45
  (31 other events, 236.5 us)
